TPU v7x, 256 devices: a whole 4x4x8 slice. The times are simulated.
256 devices in a mesh: expert: 32 (over y, z_hi, core), dp: 8 (over z_lo, x).
Axes of the slice: x: 4, y: 4, z: 8 (z_hi: 4, z_lo: 2; z = z_hi * 2 + z_lo), core: 2. Of those that a mesh axis runs over, the one named last changes fastest.
Arguments:
- tokens: bfloat16 [4096, 3584], P('expert', 'dp'), may hold values from -6 to 6
- expert_ids: int32 [4096, 8], P('expert'), may hold values from 0 to 31, all different within a row; in each aligned block of 128 rows (0 to 127, 128 to 255, ...) at most 40 rows name the same one
- gate_weights: float32 [4096, 8], P('expert'), may hold values from 0.05 to 0.5
- cotangent: bfloat16 [4096, 3584], P('expert', 'dp'), may hold values from -6 to 6
- holder: int32 [32], replicated, may hold values from 0 to 31, as said below
- migrations: int32 [16, 3], replicated, may hold values from 0 to 31, as said below
- inner_weight: bfloat16 [32, 3584, 2048], P('expert', 'dp'), may hold values from -0.09375 to 0.09375
- outer_weight: bfloat16 [32, 3584, 1024], P('expert', 'dp'), may hold values from -0.1875 to 0.1875
- first_moment: float32 [32, 3584, 2048], P('expert', 'dp'), may hold values from -6 to 6
- second_moment: float32 [32, 3584, 2048], P('expert', 'dp'), may hold values from 0.02 to 0.2
Outputs:
- combined: bfloat16 [4096, 3584], P('expert', 'dp')
- update_step: bfloat16 [32, 3584, 2048], P('expert', 'dp')
Inputs may be any that keep to these rules, and one draw needn't show every extreme that they name: `expert_ids`: within the rows of one index of expert, no expert is named by more than 40 rows, a bound that some block reaches; each row names 8 different experts. `holder`: A permutation of the slots. `migrations`: column 0 is holder of column 1. The rows form 16 // 2 swaps: for each row (e, a, b) there is a row (holder[b], b, a); every slot is a source at most once and a == b never.
All inputs are finite; a program needn't handle non-finite values.
Results may differ from a plain program's by a relative error of at most 0.029.
Values may be sent and summed in bfloat16 or wider, within the bound.
No kernel may reach another device: no remote copies, remote signals or barrier semaphores. Data moves between devices by JAX's collectives and lax.ppermute only.
A program may use at most 128 MiB of HBM per device.

v0:
```python
import jax
import jax.numpy as jnp
from jax import lax
from jax.sharding import PartitionSpec as P

beta_one = 0.9
beta_two = 0.999
epsilon = 1e-08
bias_one = 1.0 - 0.9**10
bias_two = 1.0 - 0.999**10


def on_device(
    tokens,
    expert_ids,
    gate_weights,
    cotangent,
    holder,
    migrations,
    inner_weight,
    outer_weight,
    first_moment,
    second_moment,
):
    experts = holder.shape[0]
    tok_count = tokens.shape[0]
    top_count = expert_ids.shape[1]
    capacity = 5 * tok_count * top_count // (4 * experts)
    slots = jnp.arange(experts, dtype=jnp.int32)
    home = jnp.sum(jnp.where(holder[None, :] == slots[:, None], slots[None, :], 0), axis=1)
    anchor = slots + jnp.sum(
        jnp.where(
            migrations[None, :, 2] == slots[:, None], migrations[None, :, 1] - slots[:, None], 0
        ),
        axis=1,
    )
    inner = inner_weight[0]
    outer = outer_weight[0]
    first = first_moment[0]
    second = second_moment[0]
    hidden_units = inner.shape[1] // 2
    flat_ids = expert_ids.reshape(-1)
    entry_count = flat_ids.shape[0]
    id_hits = flat_ids[:, None] == slots[None, :]
    destination = jnp.sum(jnp.where(id_hits, home[None, :], 0), axis=1)
    dest_hits = (destination[:, None] == slots[None, :]).astype(jnp.int32)
    ranks = jnp.sum((jnp.cumsum(dest_hits, axis=0) - 1) * dest_hits, axis=1)
    places = destination * capacity + ranks
    entries = (
        jnp.full((experts * capacity,), -1, jnp.int32)
        .at[places]
        .set(jnp.arange(entry_count, dtype=jnp.int32))
    )
    valid = entries >= 0
    safe = jnp.where(valid, entries, 0)
    token_rows = safe // top_count
    send_tokens = jnp.where(valid[:, None], tokens[token_rows], jnp.zeros((), jnp.bfloat16))
    gate_pick = jnp.where(valid, gate_weights.reshape(-1)[safe], 0.0)
    send_grads = (gate_pick[:, None] * cotangent[token_rows].astype(jnp.float32)).astype(
        jnp.bfloat16
    )
    arrived_tokens, arrived_grads = (
        lax.all_to_all(send_tokens, "expert", split_axis=0, concat_axis=0, tiled=True),
        lax.all_to_all(send_grads, "expert", split_axis=0, concat_axis=0, tiled=True),
    )
    partial_pre = jnp.dot(arrived_tokens, inner, preferred_element_type=jnp.float32)
    pre = lax.psum(partial_pre.astype(jnp.bfloat16), "dp").astype(jnp.float32)
    gate_part = pre[:, :hidden_units]
    up_part = pre[:, hidden_units:]
    sigma = jax.nn.sigmoid(gate_part)
    silu_value = gate_part * sigma
    hidden = (silu_value * up_part).astype(jnp.bfloat16)
    outputs = lax.dot_general(
        hidden, outer, (((1,), (1,)), ((), ())), preferred_element_type=jnp.float32
    ).astype(jnp.bfloat16)
    returned = lax.all_to_all(outputs, "expert", split_axis=0, concat_axis=0, tiled=True)
    row_index = places.reshape(tok_count, top_count)
    summed = jnp.zeros((tok_count, returned.shape[1]), jnp.float32)
    for pick in range(top_count):
        summed = summed + gate_weights[:, pick : pick + 1] * returned[row_index[:, pick]].astype(
            jnp.float32
        )
    combined = summed.astype(jnp.bfloat16)
    partial_grad = jnp.dot(arrived_grads, outer, preferred_element_type=jnp.float32)
    hidden_grad = lax.psum(partial_grad.astype(jnp.bfloat16), "dp").astype(jnp.float32)
    slope = sigma * (1.0 + gate_part * (1.0 - sigma))
    pre_grad = jnp.concatenate(
        [hidden_grad * up_part * slope, hidden_grad * silu_value], axis=1
    ).astype(jnp.bfloat16)
    weight_grad = lax.dot_general(
        arrived_tokens, pre_grad, (((0,), (0,)), ((), ())), preferred_element_type=jnp.float32
    )
    new_first = beta_one * first + (1.0 - beta_one) * weight_grad
    new_second = beta_two * second + (1.0 - beta_two) * weight_grad * weight_grad
    step = (new_first / bias_one / (jnp.sqrt(new_second / bias_two) + epsilon)).astype(
        jnp.bfloat16
    )[None]
    spread_steps = lax.all_to_all(step, "expert", split_axis=1, concat_axis=0, tiled=True)
    step = lax.all_to_all(
        jnp.take(spread_steps, anchor, axis=0), "expert", split_axis=0, concat_axis=1, tiled=True
    )
    return (combined, step)


def solution(mesh):
    placed = (
        P("expert", "dp"),
        P("expert", None),
        P("expert", None),
        P("expert", "dp"),
        P(),
        P(),
        P("expert", "dp", None),
        P("expert", "dp", None),
        P("expert", "dp", None),
        P("expert", "dp", None),
    )
    return jax.shard_map(
        on_device,
        mesh=mesh,
        in_specs=placed,
        out_specs=(P("expert", "dp"), P("expert", "dp", None)),
        check_vma=False,
    )
```

profile of v0, /device:TPU:1, one launch (start us, length us, event | category | flops | bytes accessed | tf_op | source)
XLA Modules:
  0.0 496.8 jit_solution(2616286780384699532)
XLA Ops:
  9.1 9.0 %reduce-window.6 = s32[32,8,128]{2,1,0:T(8,128)S(1)} reduce-window(s32[32,8,128]{2,1,0:T(8,128)S(1)} %fusion.25, s32[]{:T(128)} %constant.20.clone.1), window={size=1x1x128 pad=0_0x0_0x127_0}, to_apply=%region_2.3 | reduce-window | flops 4161536 | bytes 262148 | tf_op jit(solution)/shard_map/reduce-window
  18.6 4.3 scatter_custom_fusion
  24.9 5.0 gather_fusion.9
  30.0 4.1 gather_fusion.10
  35.5 12.8 %all-to-all-start.2 = ((bf16[32,40,448]{2,1,0:T(8,128)(2,1)}), bf16[32,40,448]{2,1,0:T(8,128)(2,1)}, u32[]{:S(2)}, u32[]{:S(2)}) async-start(bf16[32,40,448]{2,1,0:T(8,128)(2,1)} %fusion.15), calls=%async_computation.2 | async-start | bytes 2621440 | tf_op jit(solution)/shard_map/all_to_all | solution.py:64
  48.6 4.1 gather_fusion
  54.0 28.2 %all-to-all-done.2 = bf16[32,40,448]{2,1,0:T(8,128)(2,1)} async-done(((bf16[32,40,448]{2,1,0:T(8,128)(2,1)}), bf16[32,40,448]{2,1,0:T(8,128)(2,1)}, u32[]{:S(2)}, u32[]{:S(2)}) %all-to-all-start.2) | async-done | bytes 1146912 | tf_op jit(solution)/shard_map/all_to_all | solution.py:64
  82.2 6.1 %all-to-all-start = ((bf16[32,40,448]{2,1,0:T(8,128)(2,1)}), bf16[32,40,448]{2,1,0:T(8,128)(2,1)S(1)}, u32[]{:S(2)}, u32[]{:S(2)}) async-start(bf16[32,40,448]{2,1,0:T(8,128)(2,1)} %broadcast_select_fusion.1), calls=%async_computation | async-start | bytes 2621440 | tf_op jit(solution)/shard_map/all_to_all | solution.py:63
  88.3 4.6 convolution_convert_fusion.1
  92.9 29.4 %all-to-all-done = bf16[32,40,448]{2,1,0:T(8,128)(2,1)S(1)} async-done(((bf16[32,40,448]{2,1,0:T(8,128)(2,1)}), bf16[32,40,448]{2,1,0:T(8,128)(2,1)S(1)}, u32[]{:S(2)}, u32[]{:S(2)}) %all-to-all-start) | async-done | bytes 1146912 | tf_op jit(solution)/shard_map/all_to_all | solution.py:63
  122.3 4.6 convolution_convert_fusion
  126.9 177.3 %all-reduce.3.cloned.1.call-done = (bf16[1280,2048]{1,0:T(8,128)(2,1)}, bf16[1280,1024]{1,0:T(8,128)(2,1)}) async-done(((bf16[1280,2048]{1,0:T(8,128)(2,1)}, bf16[1280,1024]{1,0:T(8,128)(2,1)}), (bf16[1280,2048]{1,0:T(8,128)(2,1)}, bf16[1280,1024]{1,0:T(8,128)(2,1)})) %all-reduce.3.cloned.1.call-update) | async-done | bytes 7864336 | tf_op jit(solution)/shard_map/psum | solution.py:67
  304.2 4.0 convert_element_type.67
  308.3 3.2 fusion.1
  311.5 1.6 copy-done.2
  313.1 6.4 %fusion.17 = bf16[1,448,2048]{2,1,0:T(8,128)(2,1)S(1)} fusion(f32[1,448,2048]{2,1,0:T(8,128)S(1)} %copy-done.8, f32[1,448,2048]{2,1,0:T(8,128)} %param.18, bf16[1280,448]{1,0:T(8,128)(2,1)S(1)} %bitcast.96, bf16[1280,1024]{1,0:T(8,128)(2,1)S(1)} %get-tuple-element.25, bf16[1280,1024]{1,0:T(8,128)(2,1)S(1)} %get-tuple-element.24), kind=kOutput, calls=%fused_computation.41 | convolution fusion | flops 2370306048 | bytes 15564800 | tf_op jit(solution)/shard_map/dot_general | solution.py:90
  319.6 4.7 copy.54
  324.8 11.7 %reduce.18 = bf16[448,2048]{1,0:T(8,128)(2,1)S(1)} reduce(bf16[448,1,2048]{2,1,0:T(2,128)(2,1)} %bitcast.92, bf16[]{:T(256)} %broadcast.211), dimensions={1}, to_apply=%bitcast.83.reduce_sub_computation | reduce | bytes 3670018
  336.5 2.9 reshape.241
  339.5 9.4 %all-to-all-start.3 = ((bf16[32,2,14336]{2,1,0:T(2,128)(2,1)}), bf16[32,2,14336]{2,1,0:T(2,128)(2,1)S(1)}, u32[]{:S(2)}, u32[]{:S(2)}) async-start(bf16[32,2,14336]{2,1,0:T(2,128)(2,1)} %reshape.241), calls=%async_computation.3 | async-start | bytes 3670016 | tf_op jit(solution)/shard_map/all_to_all | solution.py:98
  348.9 6.1 %convolution_convert_fusion.2 = bf16[1280,448]{0,1:T(8,128)(2,1)S(1)} fusion(f32[1280,2048]{1,0:T(8,128)} %copy-done.2, bf16[1,448,1024]{2,1,0:T(8,128)(2,1)} %param.17), kind=kOutput, calls=%fused_computation.36 | convolution fusion | flops 1182842880 | bytes 12550144 | tf_op jit(solution)/shard_map/dot_general | solution.py:73
  355.0 1.5 copy.45
  356.5 29.5 %all-to-all-done.3 = bf16[32,2,14336]{2,1,0:T(2,128)(2,1)S(1)} async-done(((bf16[32,2,14336]{2,1,0:T(2,128)(2,1)}), bf16[32,2,14336]{2,1,0:T(2,128)(2,1)S(1)}, u32[]{:S(2)}, u32[]{:S(2)}) %all-to-all-start.3) | async-done | bytes 1835040 | tf_op jit(solution)/shard_map/all_to_all | solution.py:98
  387.2 11.4 %all-to-all-start.1 = ((bf16[32,40,448]{2,1,0:T(8,128)(2,1)}), bf16[32,40,448]{2,1,0:T(8,128)(2,1)S(1)}, u32[]{:S(2)}, u32[]{:S(2)}) async-start(bf16[32,40,448]{2,1,0:T(8,128)(2,1)} %bitcast.10), calls=%async_computation.1 | async-start | bytes 2621440 | tf_op jit(solution)/shard_map/all_to_all | solution.py:76
  398.8 10.2 %reshape.242 = bf16[448,1,2048]{2,1,0:T(2,128)(2,1)} reshape(bf16[32,2,14336]{2,1,0:T(2,128)(2,1)} %copy-done.3) | data formatting | bytes 3670016
  409.0 12.6 %bitcast_reduce_fusion = bf16[448,2048]{1,0:T(8,128)(2,1)} fusion(bf16[448,1,2048]{2,1,0:T(2,128)(2,1)} %reshape.242), kind=kLoop, calls=%fused_computation.118 | loop fusion | bytes 3670016 | tf_op jit(solution)/shard_map/all_to_all | solution.py:98
  421.6 3.6 all_to_all.46
  425.2 3.6 gather_fusion.11
  428.8 3.1 broadcast_select_fusion
  431.9 10.0 %all-to-all-start.4 = ((bf16[32,14,2048]{2,1,0:T(8,128)(2,1)}), bf16[32,14,2048]{2,1,0:T(8,128)(2,1)}, u32[]{:S(2)}, u32[]{:S(2)}) async-start(bf16[32,14,2048]{2,1,0:T(8,128)(2,1)} %broadcast_select_fusion), calls=%async_computation.4 | async-start | bytes 4194304 | tf_op jit(solution)/shard_map/all_to_all | solution.py:99
  450.3 36.0 %all-to-all-done.4 = bf16[32,14,2048]{2,1,0:T(8,128)(2,1)} async-done(((bf16[32,14,2048]{2,1,0:T(8,128)(2,1)}), bf16[32,14,2048]{2,1,0:T(8,128)(2,1)}, u32[]{:S(2)}, u32[]{:S(2)}) %all-to-all-start.4) | async-done | bytes 1835040 | tf_op jit(solution)/shard_map/all_to_all | solution.py:99
  486.3 3.7 all_to_all.48
  (71 shorter events, 17.6 us)
Async XLA Ops:
  7.2 115.1 %copy-start = (bf16[1,448,2048]{2,1,0:T(8,128)(2,1)S(1)}, bf16[1,448,2048]{2,1,0:T(8,128)(2,1)}, u32[]{:S(2)}) copy-start(bf16[1,448,2048]{2,1,0:T(8,128)(2,1)} %param.16) | copy-start | bytes 5505028
  34.1 14.4 %copy-start.5 = (bf16[128,448]{0,1:T(8,128)(2,1)S(1)}, bf16[128,448]{0,1:T(8,128)(2,1)}, u32[]{:S(2)}) copy-start(bf16[128,448]{0,1:T(8,128)(2,1)} %param.10) | copy-start | bytes 344068
  35.5 46.6 %all-to-all-start.2 = ((bf16[32,40,448]{2,1,0:T(8,128)(2,1)}), bf16[32,40,448]{2,1,0:T(8,128)(2,1)}, u32[]{:S(2)}, u32[]{:S(2)}) async-start(bf16[32,40,448]{2,1,0:T(8,128)(2,1)} %fusion.15), calls=%async_computation.2 | async-start | bytes 2621440 | tf_op jit(solution)/shard_map/all_to_all | solution.py:64
  82.2 40.1 %all-to-all-start = ((bf16[32,40,448]{2,1,0:T(8,128)(2,1)}), bf16[32,40,448]{2,1,0:T(8,128)(2,1)S(1)}, u32[]{:S(2)}, u32[]{:S(2)}) async-start(bf16[32,40,448]{2,1,0:T(8,128)(2,1)} %broadcast_select_fusion.1), calls=%async_computation | async-start | bytes 2621440 | tf_op jit(solution)/shard_map/all_to_all | solution.py:63
  88.3 216.0 %all-reduce.3.cloned.1.call-start = ((), (), s32[]{:S(2)}) async-start(), calls=%async_computation.5 | async-start | bytes 15728640 | tf_op jit(solution)/shard_map/psum | solution.py:67
  304.2 4.1 copy-start.4
  308.3 4.8 copy-start.2
  308.3 4.8 copy-start.8
  339.5 46.5 %all-to-all-start.3 = ((bf16[32,2,14336]{2,1,0:T(2,128)(2,1)}), bf16[32,2,14336]{2,1,0:T(2,128)(2,1)S(1)}, u32[]{:S(2)}, u32[]{:S(2)}) async-start(bf16[32,2,14336]{2,1,0:T(2,128)(2,1)} %reshape.241), calls=%async_computation.3 | async-start | bytes 3670016 | tf_op jit(solution)/shard_map/all_to_all | solution.py:98
  355.0 43.7 %copy-start.7 = (s32[16,3]{0,1:T(4,128)S(1)}, s32[16,3]{0,1:T(4,128)}, u32[]{:S(2)}) copy-start(s32[16,3]{0,1:T(4,128)} %param.15) | copy-start | bytes 580
  386.0 1.2 copy-start.3
  387.2 44.7 %all-to-all-start.1 = ((bf16[32,40,448]{2,1,0:T(8,128)(2,1)}), bf16[32,40,448]{2,1,0:T(8,128)(2,1)S(1)}, u32[]{:S(2)}, u32[]{:S(2)}) async-start(bf16[32,40,448]{2,1,0:T(8,128)(2,1)} %bitcast.10), calls=%async_computation.1 | async-start | bytes 2621440 | tf_op jit(solution)/shard_map/all_to_all | solution.py:76
  431.9 10.5 %copy-start.6 = (f32[128,8]{0,1:T(8,128)S(1)}, f32[128,8]{0,1:T(8,128)}, u32[]{:S(2)}) copy-start(f32[128,8]{0,1:T(8,128)} %param.12) | copy-start | bytes 12292
  431.9 54.4 %all-to-all-start.4 = ((bf16[32,14,2048]{2,1,0:T(8,128)(2,1)}), bf16[32,14,2048]{2,1,0:T(8,128)(2,1)}, u32[]{:S(2)}, u32[]{:S(2)}) async-start(bf16[32,14,2048]{2,1,0:T(8,128)(2,1)} %broadcast_select_fusion), calls=%async_computation.4 | async-start | bytes 4194304 | tf_op jit(solution)/shard_map/all_to_all | solution.py:99
  449.2 40.7 %copy-start.1 = (bf16[1,448,2048]{2,1,0:T(8,128)(2,1)S(1)}, bf16[1,448,2048]{2,1,0:T(8,128)(2,1)}, u32[]{:S(2)}) copy-start(bf16[1,448,2048]{2,1,0:T(8,128)(2,1)} %param.16) | copy-start | bytes 5505028
Sparse Core Ops, SparseCore 0:
  127.1 177.1 all-reduce.2
where the time goes:
time: 506 us; the launch traced here: 497 us
  waiting for transfers between devices  300 us (59%)
  local copies, waits for them, and re-layouts  74.9 us (15%)
  starting transfers between devices  49.7 us (10%)
  other arithmetic  35.7 us (7%)
  matrix products  21.7 us (4%)
  between operations  14.4 us (3%)
    psum x1, waiting for transfers between devices, on_device(): pre = lax.psum(partial_pre.astype(jnp.bfloat16), 'dp').astype(jnp.float32)  177 us
    all_to_all x1, waiting for transfers between devices, on_device(): lax.all_to_all(jnp.take(spread_steps, anchor, axis=0), 'expert', split_ax...  36 us
    all_to_all x1, waiting for transfers between devices, on_device(): lax.all_to_all(step, 'expert', split_axis=1, concat_axis=0, tiled=True)  29.5 us
    all_to_all x1, waiting for transfers between devices, on_device(): lax.all_to_all(send_tokens, 'expert', split_axis=0, concat_axis=0, tiled=...  29.4 us
    all_to_all x1, waiting for transfers between devices, on_device(): lax.all_to_all(send_grads, 'expert', split_axis=0, concat_axis=0, tiled=T...  28.2 us
    unnamed x26, local copies, waits for them, and re-layouts  20.2 us
    all_to_all x2, local copies, waits for them, and re-layouts, on_device(): lax.all_to_all(step, 'expert', split_axis=1, concat_axis=0, tiled=True)  16.2 us
    all_to_all x1, starting transfers between devices, on_device(): lax.all_to_all(send_grads, 'expert', split_axis=0, concat_axis=0, tiled=T...  12.8 us
  transfers between devices with their start and end apart: 6, of which 5 were waited for; matrix products, arithmetic and copies ran while one was open for 11% of the time, Pallas kernels for 0%

commit v1 on v0

v1 whole, which is shorter than its diff:
```python
import functools

import jax
import jax.numpy as jnp
from jax import lax
from jax.experimental import pallas as pl
from jax.experimental.pallas import tpu as pltpu
from jax.sharding import Mesh, PartitionSpec as P

beta_one = 0.9
beta_two = 0.999
epsilon = 1e-08
bias_one = 1.0 - 0.9**10
bias_two = 1.0 - 0.999**10

bf16 = jnp.bfloat16
f32 = jnp.float32

experts = 32
capacity = 40
tok_count = 128
width = 448
hidden_units = 1024
rows = experts * capacity
block_rows = 160
order = (4, 3, 5, 6, 2, 7, 0, 1)
chunks = ((0, 512), (512, 512))

expert_axes = ("y", "zh", "c")
vmem_bytes = 32 * 1024 * 1024


def dot(a, b, contract_a=1, contract_b=0):
    return lax.dot_general(
        a, b, (((contract_a,), (contract_b,)), ((), ())), preferred_element_type=f32
    )


def array(*shape, dtype=bf16):
    return jax.ShapeDtypeStruct(shape, dtype)


def whole(value):
    return pl.BlockSpec(value.shape, lambda *_: (0,) * len(value.shape))


class Kernels:
    def __init__(self):
        self.last = None

    def __call__(
        self,
        kernel,
        name,
        out_shape,
        inputs,
        in_specs=None,
        out_specs=None,
        grid=(1,),
        prefetch=None,
        cost=(0, 1_000_000, 0),
        aliases=None,
        order=True,
        waits=(),
        scratch=(),
    ):
        count = len(inputs) + (prefetch is not None)
        in_specs = [whole(v) for v in inputs] if in_specs is None else list(in_specs)
        if out_specs is None:
            many = isinstance(out_shape, list)
            out_specs = [whole(s) for s in out_shape] if many else whole(out_shape)
        waits = list(waits) + ([self.last] if order and self.last is not None else [])
        in_specs += [pl.BlockSpec(memory_space=pl.ANY)] * len(waits)

        def body(*refs):
            kernel(*refs[:count], *refs[count + len(waits) :])

        args = ([] if prefetch is None else [prefetch]) + list(inputs) + waits
        result = pl.pallas_call(
            body,
            out_shape=out_shape,
            grid_spec=pltpu.PrefetchScalarGridSpec(
                num_scalar_prefetch=0 if prefetch is None else 1,
                grid=grid,
                in_specs=in_specs,
                out_specs=out_specs,
                scratch_shapes=list(scratch),
            ),
            input_output_aliases=aliases or {},
            cost_estimate=pl.CostEstimate(
                flops=cost[0], bytes_accessed=cost[1], transcendentals=cost[2]
            ),
            compiler_params=pltpu.CompilerParams(vmem_limit_bytes=vmem_bytes),
            name=name,
        )(*args)
        self.last = result[-1] if isinstance(result, (list, tuple)) else result
        return result


def shift(value, axis, by):
    n = lax.axis_size(axis)
    return lax.ppermute(value, axis, [(i, (i + by) % n) for i in range(n)])


def exchange(value):
    return lax.all_to_all(value, expert_axes, split_axis=0, concat_axis=0, tiled=True)


def places_of(gates):
    hit = gates > 0.0
    before = lax.broadcasted_iota(jnp.int32, (128, 128), 0) < lax.broadcasted_iota(
        jnp.int32, (128, 128), 1
    )
    rank = dot(
        jnp.where(hit, 1.0, 0.0).astype(bf16), jnp.where(before, 1.0, 0.0).astype(bf16)
    )
    return jnp.where(hit, rank, -1.0).astype(jnp.int32)


def row_numbers():
    return lax.broadcasted_iota(jnp.int32, (capacity, tok_count), 0)


def one_hot(at):
    return jnp.where(at, 1.0, 0.0).astype(bf16)


def weights_of(at, gate):
    return jnp.sum(jnp.where(at, gate, 0.0), axis=1, keepdims=True)


def pick_kernel(gates, values, out):
    wanted = places_of(gates[...])
    at = [row_numbers() == wanted[s : s + 1] for s in range(experts)]
    place = jnp.concatenate([jnp.where(a, 1.0, 0.0) for a in at], axis=0).astype(bf16)
    out[...] = dot(place, values[...]).astype(bf16)


def gates_of_slot(slot, table, sources):
    lane = lax.broadcasted_iota(jnp.int32, (8, 128), 1)
    row = lax.broadcasted_iota(jnp.int32, (8, 128), 0)
    pick = ((row == 0) & (lane == 64 + slot)) | ((row == 1) & (lane == 96 + slot))
    both = dot(one_hot(pick), table, 1, 1)
    gate = both[0:1] + both[1:2]
    parts = [gate[:, s * 128 : (s + 1) * 128] for s in range(sources)]
    return jnp.concatenate(parts + [jnp.zeros_like(parts[0])] * (8 - sources), axis=0)


def arrive_kernel(info, table, out, gates_out, wanted_out):
    gates = gates_of_slot(info[8], table[:, 384:], 8)
    wanted = places_of(gates)
    gates_out[...] = gates
    wanted_out[...] = wanted
    picked = []
    for s in range(8):
        at = row_numbers() == wanted[s : s + 1]
        rows_of = dot(one_hot(at), table[s * 128 : (s + 1) * 128, :])[:, :width]
        picked.append(rows_of * weights_of(at, gates[s : s + 1]))
    out[...] = jnp.concatenate(picked, axis=0).astype(bf16)


def project_kernel(info, left, right, to_right, to_left, next_low, prev_high, own):
    ordered = jnp.concatenate([left[info[g]] for g in range(8)], axis=0)
    result = dot(ordered, right[...]).astype(bf16)
    to_right[...] = result[0:320]
    to_left[...] = result[320:640]
    next_low[...] = result[640:800]
    prev_high[...] = result[800:960]
    own[...] = result[960:1280]


def project(run, info, left, right, blocks, column):
    columns = 256 * blocks
    sizes = (320, 320, 160, 160, 320)
    return run(
        project_kernel,
        "project",
        [array(n, columns) for n in sizes],
        [left, right],
        in_specs=[
            pl.BlockSpec((8, block_rows, width), lambda j, info: (0, 0, 0)),
            pl.BlockSpec((width, 256), lambda j, info: (0, column(j))),
        ],
        out_specs=[pl.BlockSpec((n, 256), lambda j, info: (0, j)) for n in sizes],
        grid=(blocks,),
        prefetch=info,
        cost=(2 * rows * width * columns, 2 * rows * (width + columns), 0),
    )


def add(*values):
    total = values[0].astype(f32)
    for value in values[1:]:
        total = total + value.astype(f32)
    return total


def second_kernel(next_low, got_left, prev_high, got_right, right, left):
    right[...] = add(next_low[...], got_left[...]).astype(bf16)
    left[...] = add(prev_high[...], got_right[...]).astype(bf16)


def third_kernel(own, low, got_right, high, got_left, total):
    half = low.shape[0]
    total[:half] = add(own[:half], low[...], got_right[...]).astype(bf16)
    total[half:] = add(own[half:], high[...], got_left[...]).astype(bf16)


class RingSum:
    def __init__(self, run, pieces, axis="x"):
        self.run = run
        self.axis = axis
        to_right, to_left, self.next_low, self.prev_high, self.own = pieces
        self.columns = self.own.shape[1]
        self.block = 256 if self.columns % 256 == 0 else self.columns
        self.height = self.next_low.shape[0]
        self.got_left = shift(to_right, axis, 1)
        self.got_right = shift(to_left, axis, -1)

    def half(self, which):
        return pl.BlockSpec((self.height, self.block), lambda j: (which, j))

    def second(self):
        right, left = self.run(
            second_kernel,
            "second",
            [array(self.height, self.columns)] * 2,
            [self.next_low, self.got_left, self.prev_high, self.got_right],
            in_specs=[self.half(0)] * 4,
            out_specs=[self.half(0)] * 2,
            grid=(self.columns // self.block,),
        )
        self.low = shift(right, self.axis, 1)
        self.high = shift(left, self.axis, -1)

    def third(self, waits=()):
        both = pl.BlockSpec((2 * self.height, self.block), lambda j: (0, j))
        self.total = self.run(
            third_kernel,
            "third",
            array(2 * self.height, self.columns),
            [self.own, self.low, self.got_right, self.high, self.got_left],
            in_specs=[both, self.half(0), self.half(1), self.half(0), self.half(1)],
            out_specs=both,
            grid=(self.columns // self.block,),
            waits=waits,
        )
        return self.total

    def cross(self, waits=()):
        self.other = shift(self.third(waits), "zl", 1)

    def result(self):
        return [self.total, self.other]


def forward_kernel(from_left, from_right, low, high):
    low[...] = from_left[...]
    high[...] = from_right[...]


class RowGather:
    def __init__(self, run, value, axis="x"):
        self.run = run
        self.axis = axis
        self.own = value
        self.from_left = shift(self.own, axis, 1)
        self.from_right = shift(self.own, axis, -1)

    def second(self):
        height, columns = self.own.shape
        block = 256 if columns % 256 == 0 else columns
        first = pl.BlockSpec((height // 2, block), lambda j: (0, j))
        last = pl.BlockSpec((height // 2, block), lambda j: (1, j))
        low, high = self.run(
            forward_kernel,
            "forward",
            [array(height // 2, columns)] * 2,
            [self.from_left, self.from_right],
            in_specs=[first, last],
            out_specs=[first, first],
            grid=(columns // block,),
        )
        self.far_low = shift(low, self.axis, 1)
        self.far_high = shift(high, self.axis, -1)

    def result(self):
        return [self.own, self.from_right, self.far_low, self.far_high, self.from_left]


def hidden_kernel(*refs):
    out = refs[-1]
    at = 0
    for i in range(0, len(refs) - 1, 2):
        pre = add(refs[i][...], refs[i + 1][...])
        units = pre.shape[1] // 2
        gate, up = pre[:, :units], pre[:, units:]
        out[:, at : at + units] = (gate * jax.nn.sigmoid(gate) * up).astype(bf16)
        at += units


def hidden_of(run, sums):
    inputs = [v for s in sums for v in s.result()]
    return run(
        hidden_kernel,
        "hidden",
        array(320, hidden_units),
        inputs,
        in_specs=[pl.BlockSpec((80, v.shape[1]), lambda i: (i, 0)) for v in inputs],
        out_specs=pl.BlockSpec((80, hidden_units), lambda i: (i, 0)),
        grid=(4,),
        cost=(0, 3_000_000, 320 * hidden_units),
    )


def slope_kernel(pre, pre_other, back, back_other, out):
    p = add(pre[...], pre_other[...])
    units = p.shape[1] // 2
    gate, up = p[:, :units], p[:, units:]
    hidden_grad = add(back[...], back_other[...])
    sigma = jax.nn.sigmoid(gate)
    slope = sigma * (1.0 + gate * (1.0 - sigma))
    out[:, :units] = (hidden_grad * up * slope).astype(bf16)
    out[:, units:] = (hidden_grad * (gate * sigma)).astype(bf16)


def pre_grad_of(run, pre, back):
    inputs = pre.result() + back.result()
    columns = pre.columns
    return run(
        slope_kernel,
        "slope",
        array(320, columns),
        inputs,
        in_specs=[pl.BlockSpec((80, v.shape[1]), lambda i: (i, 0)) for v in inputs],
        out_specs=pl.BlockSpec((80, columns), lambda i: (i, 0)),
        grid=(4,),
        cost=(0, 3_000_000, 160 * columns),
    )


def ordered_rows(pieces):
    own, following, far_low, far_high, previous = [p[...] for p in pieces]
    return jnp.concatenate(
        [
            far_low,
            following[160:],
            far_high,
            previous[:160],
            following[:160],
            previous[160:],
            own,
        ],
        axis=0,
    )


def adam_kernel(info, tokens, *refs):
    pieces, (first, second, step) = refs[:5], refs[5:]
    ordered = jnp.concatenate([tokens[info[g]] for g in range(8)], axis=0)
    weight_grad = dot(ordered, ordered_rows(pieces), 0, 0)
    new_first = beta_one * first[...] + (1.0 - beta_one) * weight_grad
    new_second = beta_two * second[...] + (1.0 - beta_two) * weight_grad * weight_grad
    result = new_first / bias_one / (jnp.sqrt(new_second / bias_two) + epsilon)
    step[0] = result[:, :128].astype(bf16)
    step[1] = result[:, 128:].astype(bf16)


def adam(run, info, tokens, pieces, first, second, blocks, column):
    moments = pl.BlockSpec((width, 256), lambda j, info: (0, column(j)))
    return run(
        adam_kernel,
        "adam",
        array(2 * blocks, width, 128),
        [tokens, *pieces, first, second],
        in_specs=[pl.BlockSpec((8, block_rows, width), lambda j, info: (0, 0, 0))]
        + [pl.BlockSpec((p.shape[0], 256), lambda j, info: (0, j)) for p in pieces]
        + [moments, moments],
        out_specs=pl.BlockSpec((2, width, 128), lambda j, info: (j, 0, 0)),
        grid=(blocks,),
        prefetch=info,
        cost=(2 * rows * width * 256 * blocks, 2_000_000 * blocks, width * 512 * blocks),
    )


def reorder_kernel(anchor, source, out):
    def one(d, carry):
        out[d] = source[anchor[d]]
        return carry

    lax.fori_loop(0, experts, one, 0)


def place_kernel(moved, *refs, out):
    for i in range(moved.shape[0]):
        refs[out][:, i * 128 : (i + 1) * 128] = moved[i]


def place(run, moved, base, chunk, through=None):
    start, units = chunk
    tiles = units // 128
    anywhere = pl.BlockSpec(memory_space=pl.ANY)
    in_specs = [pl.BlockSpec((tiles, width, 128), lambda j: (j, 0, 0))]
    out_specs = [
        pl.BlockSpec(
            (width, units), lambda j: (0, start // units + j * (hidden_units // units))
        )
    ]
    inputs, shapes, aliases = [moved], [array(width, 2 * hidden_units)], {}
    for value, at in ((base, 0), (through, 1)):
        if value is None:
            continue
        aliases[len(inputs)] = at
        inputs.append(value)
        in_specs.append(anywhere)
        if at:
            shapes.append(array(*value.shape))
            out_specs.append(anywhere)
    return run(
        functools.partial(place_kernel, out=len(inputs) - 1),
        "place",
        shapes,
        inputs,
        in_specs=in_specs,
        out_specs=out_specs,
        grid=(2,),
        aliases=aliases,
    )


def outputs_kernel(info, *refs):
    pieces, (outer, gates, wanted, out_here, out_there, held) = refs[:5], refs[5:]
    g = pl.program_id(0)

    @pl.when(g == 0)
    def _():
        result = dot(ordered_rows(pieces), outer[...], 1, 1).astype(bf16).astype(f32)
        result = jnp.concatenate([result, jnp.zeros((rows, 512 - width), f32)], axis=1)
        for i in range(8):
            for s in range(4):
                at = i * block_rows + s * capacity
                held[4 * info[i] + s] = result[at : at + capacity]

    def work(first, out):
        for s in range(4):
            source = info[first + s]
            at = row_numbers() == wanted[pl.ds(source, 1), :]
            weights = weights_of(at, gates[pl.ds(source, 1), :])
            part = (held[source] * weights).astype(bf16)
            out[s * 128 : (s + 1) * 128, :] = dot(one_hot(at), part, 0, 0).astype(bf16)

    @pl.when(g < 4)
    def _():
        work(9 + 16 + 4 * g, out_there)

    @pl.when(g >= 4)
    def _():
        work(9 + 4 * (g - 4), out_here)


def split_kernel(here, other, to_right, to_left, next_low, prev_high, own):
    total = add(here[...], other[...]).astype(bf16)
    own[...] = total[0:512]
    next_low[...] = total[512:768]
    to_right[256:] = total[768:1024]
    to_right[:256] = total[1024:1280]
    to_left[:256] = total[1280:1536]
    to_left[256:] = total[1536:1792]
    prev_high[...] = total[1792:2048]


def cut_kernel(value, *outs):
    for i, out in enumerate(outs):
        out[...] = value[i * tok_count : (i + 1) * tok_count]


def sum_kernel(*refs):
    refs[-1][...] = add(*[r[...] for r in refs[:-1]])[:, :width].astype(bf16)


def on_device(
    tokens,
    expert_ids,
    gate_weights,
    cotangent,
    holder,
    migrations,
    inner_weight,
    outer_weight,
    first_moment,
    second_moment,
):
    slots = jnp.arange(experts, dtype=jnp.int32)
    anchor = slots + jnp.sum(
        jnp.where(
            migrations[None, :, 2] == slots[:, None], migrations[None, :, 1] - slots[:, None], 0
        ),
        axis=1,
    )
    slot = lax.axis_index(expert_axes)
    blocks = (2 * lax.axis_index("x") + jnp.array(order, jnp.int32)) % 8
    core, y, z = slots // 16, slots // 4 % 4, slots % 4
    relative = (
        (lax.axis_index("y") + y) % 4 * 8
        + (lax.axis_index("zh") + z) % 4 * 2
        + (lax.axis_index("c") + core) % 2
    )
    info = jnp.concatenate([blocks, slot[None], relative]).astype(jnp.int32)

    inner = inner_weight[0]
    outer = outer_weight[0]
    first = first_moment[0]
    second = second_moment[0]

    ids = expert_ids.T
    weights = gate_weights.T
    gates = jnp.zeros((experts, tok_count), f32)
    for k in range(ids.shape[0]):
        gates = gates + jnp.where(ids[k : k + 1] == holder[:, None], weights[k : k + 1], 0.0)

    high = lax.reduce_precision(gates, 8, 7)
    table = jnp.concatenate(
        [cotangent, high.T.astype(bf16), (gates - high).T.astype(bf16)], axis=1
    )
    table = lax.all_gather(table, expert_axes, axis=0, tiled=True)

    run = Kernels()
    cost = (2 * rows * 128 * 512, 2_000_000, 0)
    picked = run(pick_kernel, "pick", array(rows, width), [gates, tokens], cost=cost)
    routed_tokens = exchange(picked.reshape(experts, capacity, width))
    routed_tokens = routed_tokens.reshape(8, block_rows, width)

    def column(chunk):
        start, units = chunk
        n = units // 256
        return lambda j: start // 256 + j % n + 4 * (j // n)

    def pre_sum(chunk):
        blocks = 2 * chunk[1] // 256
        return RingSum(
            run, project(run, info, routed_tokens, inner, blocks, column(chunk))
        )

    def back_sum(chunk):
        start, units = chunk
        return RingSum(
            run,
            project(
                run, info, routed_grads, outer, units // 256, lambda j: start // 256 + j
            ),
        )

    def steps(chunk, gather):
        return adam(
            run,
            info,
            routed_tokens,
            gather.result(),
            first,
            second,
            2 * chunk[1] // 256,
            column(chunk),
        )

    def spread(step):
        return exchange(step.reshape(experts, -1, 128))

    def deliver(pieces):
        picked = run(
            reorder_kernel, "reorder", array(*pieces.shape), [pieces], prefetch=anchor
        )
        return exchange(picked).reshape(-1, width, 128)

    one, two = chunks
    pre_one = pre_sum(one)
    pre_two = pre_sum(two)
    pre_one.second()
    routed_grads, gates, wanted = run(
        arrive_kernel,
        "arrive",
        [
            array(rows, width),
            array(experts, tok_count, dtype=f32),
            array(experts, tok_count, dtype=jnp.int32),
        ],
        [table],
        in_specs=[pl.BlockSpec((1024, 512), lambda g, info: (g, 0))],
        out_specs=[
            pl.BlockSpec((2 * block_rows, width), lambda g, info: (g, 0)),
            pl.BlockSpec((8, tok_count), lambda g, info: (g, 0)),
            pl.BlockSpec((8, tok_count), lambda g, info: (g, 0)),
        ],
        grid=(4,),
        prefetch=info,
        waits=[pre_two.got_left, pre_two.got_right],
    )
    routed_grads = routed_grads.reshape(8, block_rows, width)
    back_one = back_sum(one)
    pre_one.cross()
    pre_two.second()
    back_one.second()
    back_one.cross()
    pre_two.cross()
    back_two = back_sum(two)
    grad_one = RowGather(run, pre_grad_of(run, pre_one, back_one))
    back_two.second()
    grad_one.second()
    back_two.cross()
    grad_two = RowGather(run, pre_grad_of(run, pre_two, back_two))
    hidden = RowGather(run, hidden_of(run, (pre_one, pre_two)))
    step_one = steps(one, grad_one)
    spread_one = spread(step_one)
    grad_two.second()
    hidden.second()
    moved_one = deliver(spread_one)
    step_two = steps(two, grad_two)
    update, step_two = place(run, moved_one, None, one, step_two)
    spread_two = spread(step_two)
    gathered = hidden.result()
    early = lambda g, info: (jnp.minimum(g, 3), 0)
    late = lambda g, info: (jnp.maximum(g - 4, 0), 0)
    out_here, out_there = run(
        outputs_kernel,
        "outputs",
        [array(2048, 512)] * 2,
        [*gathered, outer, gates, wanted],
        out_specs=[pl.BlockSpec((512, 512), late), pl.BlockSpec((512, 512), early)],
        grid=(8,),
        prefetch=info,
        cost=(2 * rows * hidden_units * width, 5_000_000, 0),
        scratch=[pltpu.VMEM((experts, capacity, 512), f32)],
    )
    other = shift(out_there, "c", 1)
    pieces = run(
        split_kernel,
        "split",
        [array(n, 512) for n in (512, 512, 256, 256, 512)],
        [out_here, other],
    )
    along_y = RingSum(run, pieces, "y")
    along_y.second()
    moved_two = deliver(spread_two)
    parts = run(cut_kernel, "cut", [array(tok_count, 512)] * 4, [along_y.third()])
    parts = [parts[0]] + [shift(parts[by], "zh", by) for by in (1, 2, 3)]
    combined = run(sum_kernel, "sum", array(tok_count, width), parts)
    (update,) = place(run, moved_two, update, two)
    return combined, update[None]


def solution(mesh):
    whole = Mesh(mesh.devices.reshape(4, 4, 2, 2, 4), ("y", "zh", "c", "zl", "x"))
    dp = ("zl", "x")
    placed = (
        P(expert_axes, dp),
        P(expert_axes, None),
        P(expert_axes, None),
        P(expert_axes, dp),
        P(),
        P(),
        P(expert_axes, dp, None),
        P(expert_axes, dp, None),
        P(expert_axes, dp, None),
        P(expert_axes, dp, None),
    )
    return jax.shard_map(
        on_device,
        mesh=whole,
        in_specs=placed,
        out_specs=(P(expert_axes, dp), P(expert_axes, dp, None)),
        check_vma=False,
    )
```

time: 506 us -> 390 us (0.77)
  waiting for transfers between devices: 300 us -> 144 us
  starting transfers between devices: 49.7 us -> 139 us
  Pallas kernels: 0 us -> 53.9 us
  local copies, waits for them, and re-layouts: 74.9 us -> 29.4 us
  other arithmetic: 35.7 us -> 3.36 us
  matrix products: 21.7 us -> 0 us
    psum x1 -> x0, waiting for transfers between devices: 177 us -> none  [on_device(): pre = lax.psum(partial_pre.astype(jnp.bfloat16), 'dp').astype(jnp.float32)]
    ppermute x0 -> x40, waiting for transfers between devices: none -> 108 us  [shift(): return lax.ppermute(value, axis, [(i, (i + by) % n) for i in range(n)])]
    all_to_all x5, waiting for transfers between devices: 123 us -> 36 us  [exchange(): lax.all_to_all(value, expert_axes, split_axis=0, concat_axis=0, tiled=True)]
    ppermute x0 -> x40, starting transfers between devices: none -> 79.2 us  [shift(): return lax.ppermute(value, axis, [(i, (i + by) % n) for i in range(n)])]
    pallas_call x0 -> x32, Pallas kernels: none -> 53.9 us  [__call__(): pl.pallas_call(body, out_shape=out_shape, grid_spec=pltpu.PrefetchScalarG...]
    gather x12 -> x0, local copies, waits for them, and re-layouts: 23.5 us -> none  [the longest x8 6.79 us: on_device(): returned[row_index[:, pick]].astype(jnp.float32)]
    dot_general x4 -> x0, matrix products: 21.7 us -> none  [the longest x1 6.44 us: on_device(): lax.dot_general(arrived_tokens, pre_grad, (((0,), (0,)), ((), ())), prefe...]
    all_to_all x3 -> x0, local copies, waits for them, and re-layouts: 19.9 us -> none  [the longest x2 16.2 us: on_device(): lax.all_to_all(step, 'expert', split_axis=1, concat_axis=0, tiled=True)]
  transfers between devices with their start and end apart: 6 -> 46, of which waited for: 5 -> 19; matrix products, arithmetic and copies ran while one was open for 11% -> 1% of each run, Pallas kernels for 0% -> 9%
where the time goes in v1:
time: 390 us; the launch traced here: 384 us
  waiting for transfers between devices  144 us (37%)
  starting transfers between devices  139 us (36%)
  Pallas kernels  53.9 us (14%)
  local copies, waits for them, and re-layouts  29.4 us (8%)
  between operations  14.8 us (4%)
    ppermute x40, waiting for transfers between devices, shift(): return lax.ppermute(value, axis, [(i, (i + by) % n) for i in range(n)])  108 us
    ppermute x40, starting transfers between devices, shift(): return lax.ppermute(value, axis, [(i, (i + by) % n) for i in range(n)])  79.2 us
    all_to_all x5, starting transfers between devices, exchange(): lax.all_to_all(value, expert_axes, split_axis=0, concat_axis=0, tiled=True)  59.3 us
    pallas_call x32, Pallas kernels, __call__(): pl.pallas_call(body, out_shape=out_shape, grid_spec=pltpu.PrefetchScalarG...  53.9 us
    all_to_all x5, waiting for transfers between devices, exchange(): lax.all_to_all(value, expert_axes, split_axis=0, concat_axis=0, tiled=True)  36 us
    unnamed x94, local copies, waits for them, and re-layouts  26.6 us
  transfers between devices with their start and end apart: 46, of which 19 were waited for; matrix products, arithmetic and copies ran while one was open for 1% of the time, Pallas kernels for 9%

profile of v1, /device:TPU:1, one launch (start us, length us, event | category | flops | bytes accessed | tf_op | source)
XLA Modules:
  0.0 383.8 jit_solution(10171815449954451033)
XLA Ops:
  15.5 12.8 %all-to-all-start = ((bf16[32,40,448]{2,1,0:T(8,128)(2,1)}), bf16[32,40,448]{2,1,0:T(8,128)(2,1)S(1)}, u32[]{:S(2)}, u32[]{:S(2)}) async-start(bf16[32,40,448]{2,1,0:T(8,128)(2,1)} %bitcast.19), calls=%async_computation | async-start | bytes 2621440 | tf_op jit(solution)/shard_map/all_to_all | solution.py:106
  28.5 36.0 %all-to-all-done = bf16[32,40,448]{2,1,0:T(8,128)(2,1)S(1)} async-done(((bf16[32,40,448]{2,1,0:T(8,128)(2,1)}), bf16[32,40,448]{2,1,0:T(8,128)(2,1)S(1)}, u32[]{:S(2)}, u32[]{:S(2)}) %all-to-all-start) | async-done | bytes 1146912 | tf_op jit(solution)/shard_map/all_to_all | solution.py:106
  64.5 3.1 project.4
  70.4 3.1 project.5
  76.3 5.3 %collective-permute-done.refs_1_.refs_4_ = bf16[320,1024]{1,0:T(8,128)(2,1)S(1)} collective-permute-done((bf16[320,1024]{1,0:T(8,128)(2,1)S(1)}, bf16[320,1024]{1,0:T(8,128)(2,1)S(1)}, u32[]{:S(2)}, u32[]{:S(2)}) %collective-permute-start) | collective-permute-done | bytes 655392 | tf_op jit(solution)/shard_map/ppermute | solution.py:102
  86.2 9.4 %collective-permute-done.4.refs_2_.refs_1_.refs_4_ = bf16[320,1024]{1,0:T(8,128)(2,1)S(1)} collective-permute-done((bf16[320,1024]{1,0:T(8,128)(2,1)S(1)}, bf16[320,1024]{1,0:T(8,128)(2,1)S(1)}, u32[]{:S(2)}, u32[]{:S(2)}) %collective-permute-start.4) | collective-permute-done | bytes 655392 | tf_op jit(solution)/shard_map/ppermute | solution.py:102
  100.3 2.9 arrive.1
  111.2 8.2 %collective-permute-start.6 = (bf16[320,1024]{1,0:T(8,128)(2,1)S(1)}, bf16[320,1024]{1,0:T(8,128)(2,1)S(1)}, u32[]{:S(2)}, u32[]{:S(2)}) collective-permute-start(bf16[320,1024]{1,0:T(8,128)(2,1)S(1)} %third.5.refs_4_.refs_0_), channel_id=1, source_target_pairs={{0,4},{4,0},{1,5},{5,1},{2,6},{6,2},{3,7},{7,3},{8,12},{12,8},{9,1... | collective-permute-start | bytes 1966088 | tf_op jit(solution)/shard_map/ppermute | solution.py:102
  120.2 3.0 collective-permute-start.12
  127.2 7.1 %collective-permute-start.16 = (bf16[320,512]{1,0:T(8,128)(2,1)S(1)}, bf16[320,512]{1,0:T(8,128)(2,1)S(1)}, u32[]{:S(2)}, u32[]{:S(2)}) collective-permute-start(bf16[320,512]{1,0:T(8,128)(2,1)S(1)} %third.6.refs_5_.refs_2_), channel_id=1, source_target_pairs={{0,4},{4,0},{1,5},{5,1},{2,6},{6,2},{3,7},{7,3},{8,12},{12,8},{9,1... | collective-permute-start | bytes 983048 | tf_op jit(solution)/shard_map/ppermute | solution.py:102
  136.7 3.3 collective-permute-done.16.refs_3_
  143.3 2.7 collective-permute-start.15
  146.0 3.6 collective-permute-start.13
  149.6 12.6 %collective-permute-done.14.refs_1_.refs_4_ = bf16[320,512]{1,0:T(8,128)(2,1)S(1)} collective-permute-done((bf16[320,512]{1,0:T(8,128)(2,1)S(1)}, bf16[320,512]{1,0:T(8,128)(2,1)S(1)}, u32[]{:S(2)}, u32[]{:S(2)}) %collective-permute-start.14) | collective-permute-done | bytes 327712 | tf_op jit(solution)/shard_map/ppermute | solution.py:102
  168.1 5.0 %collective-permute-start.21 = (bf16[320,512]{1,0:T(8,128)(2,1)S(1)}, bf16[320,512]{1,0:T(8,128)(2,1)S(1)}, u32[]{:S(2)}, u32[]{:S(2)}) collective-permute-start(bf16[320,512]{1,0:T(8,128)(2,1)S(1)} %third.8.refs_2_.refs_4_), channel_id=1, source_target_pairs={{0,4},{4,0},{1,5},{5,1},{2,6},{6,2},{3,7},{7,3},{8,12},{12,8},{9,1... | collective-permute-start | bytes 983048 | tf_op jit(solution)/shard_map/ppermute | solution.py:102
  180.7 5.1 %adam.2.refs_2_ = bf16[8,448,128]{2,1,0:T(8,128)(2,1)} custom-call(s32[41]{0:T(128)S(1)} %copy-done.39, bf16[8,160,448]{2,1,0:T(8,128)(2,1)S(1)} %bitcast.53, bf16[320,1024]{1,0:T(8,128)(2,1)S(1)} %slope.2.refs_4_.refs_2_, bf16[320,1024]{1,0:T(8,128)(2,1)S(1)} %collective-permute-done.20.refs_1_.refs_3_, ...), custom_call_target="tpu_custom_call" | custom-call | flops 1174405120 | bytes 8000000 | tf_op jit(solution)/shard_map/adam/pallas_call | solution.py:79
  185.7 18.2 %all-to-all-start.1 = ((bf16[32,112,128]{2,1,0:T(8,128)(2,1)}), bf16[32,112,128]{2,1,0:T(8,128)(2,1)}, u32[]{:S(2)}, u32[]{:S(2)}) async-start(bf16[32,112,128]{2,1,0:T(8,128)(2,1)} %bitcast.28), calls=%async_computation.1 | async-start | bytes 1835008 | tf_op jit(solution)/shard_map/all_to_all | solution.py:106
  209.6 11.7 %collective-permute-done.24.refs_0_.refs_6_ = bf16[320,1024]{1,0:T(8,128)(2,1)S(1)} collective-permute-done((bf16[320,1024]{1,0:T(8,128)(2,1)S(1)}, bf16[320,1024]{1,0:T(8,128)(2,1)S(1)}, u32[]{:S(2)}, u32[]{:S(2)}) %collective-permute-start.24) | collective-permute-done | bytes 655392 | tf_op jit(solution)/shard_map/ppermute | solution.py:102
  223.0 12.0 %collective-permute-done.22.refs_1_.refs_2_ = bf16[320,1024]{1,0:T(8,128)(2,1)S(1)} collective-permute-done((bf16[320,1024]{1,0:T(8,128)(2,1)S(1)}, bf16[320,1024]{1,0:T(8,128)(2,1)S(1)}, u32[]{:S(2)}, u32[]{:S(2)}) %collective-permute-start.22) | collective-permute-done | bytes 655392 | tf_op jit(solution)/shard_map/ppermute | solution.py:102
  238.5 2.9 reorder.2.refs_9_
  241.3 10.9 %all-to-all-start.2 = ((bf16[32,112,128]{2,1,0:T(8,128)(2,1)}), bf16[32,112,128]{2,1,0:T(8,128)(2,1)}, u32[]{:S(2)}, u32[]{:S(2)}) async-start(bf16[32,112,128]{2,1,0:T(8,128)(2,1)} %reorder.2.refs_9_), calls=%async_computation.2 | async-start | bytes 1835008 | tf_op jit(solution)/shard_map/all_to_all | solution.py:106
  257.7 5.2 %collective-permute-done.30.refs_4_ = bf16[160,1024]{1,0:T(8,128)(2,1)S(1)} collective-permute-done((bf16[160,1024]{1,0:T(8,128)(2,1)}, bf16[160,1024]{1,0:T(8,128)(2,1)S(1)}, u32[]{:S(2)}, u32[]{:S(2)}) %collective-permute-start.30) | collective-permute-done | bytes 327712 | tf_op jit(solution)/shard_map/ppermute | solution.py:102
  270.2 4.4 %adam.3.refs_2_ = bf16[8,448,128]{2,1,0:T(8,128)(2,1)S(1)} custom-call(s32[41]{0:T(128)S(1)} %copy-done.40, bf16[8,160,448]{2,1,0:T(8,128)(2,1)S(1)} %bitcast.54, bf16[320,1024]{1,0:T(8,128)(2,1)S(1)} %copy-done.10, bf16[320,1024]{1,0:T(8,128)(2,1)S(1)} %copy-done.15, bf16[160,1024]{1,0:T(8,128)(2,1)S(1)} %collective-permute-done.30.refs_4_, ...), custom_call_target="tpu_custom_call" | custom-call | flops 1174405120 | bytes 8000000 | tf_op jit(solution)/shard_map/adam/pallas_call | solution.py:79
  280.9 7.7 %outputs.1 = (bf16[2048,512]{1,0:T(8,128)(2,1)S(1)}, bf16[2048,512]{1,0:T(8,128)(2,1)}) custom-call(s32[41]{0:T(128)S(1)} %copy-done.40, bf16[320,1024]{1,0:T(8,128)(2,1)S(1)} %copy-done.8, bf16[320,1024]{1,0:T(8,128)(2,1)S(1)} %copy-done.17, bf16[160,1024]{1,0:T(8,128)(2,1)S(1)} %collective-permute-done.28.refs_3_, ...), custom_call_target="tpu_custom_call" | custom-call | flops 1174405120 | bytes 5000000 | tf_op jit(solution)/shard_map/outputs/pallas_call | solution.py:79
  291.9 9.6 %all-to-all-start.3 = ((bf16[32,112,128]{2,1,0:T(8,128)(2,1)}), bf16[32,112,128]{2,1,0:T(8,128)(2,1)S(1)}, u32[]{:S(2)}, u32[]{:S(2)}) async-start(bf16[32,112,128]{2,1,0:T(8,128)(2,1)} %bitcast.30), calls=%async_computation.3 | async-start | bytes 1835008 | tf_op jit(solution)/shard_map/all_to_all | solution.py:106
  308.2 18.6 %collective-permute-done.33.refs_1_.refs_4_ = bf16[512,512]{1,0:T(8,128)(2,1)S(1)} collective-permute-done((bf16[512,512]{1,0:T(8,128)(2,1)S(1)}, bf16[512,512]{1,0:T(8,128)(2,1)S(1)}, u32[]{:S(2)}, u32[]{:S(2)}) %collective-permute-start.33) | collective-permute-done | bytes 524320 | tf_op jit(solution)/shard_map/ppermute | solution.py:102
  329.8 7.8 %all-to-all-start.4 = ((bf16[32,112,128]{2,1,0:T(8,128)(2,1)}), bf16[32,112,128]{2,1,0:T(8,128)(2,1)S(1)}, u32[]{:S(2)}, u32[]{:S(2)}) async-start(bf16[32,112,128]{2,1,0:T(8,128)(2,1)} %reorder.3.refs_5_), calls=%async_computation.4 | async-start | bytes 1835008 | tf_op jit(solution)/shard_map/all_to_all | solution.py:106
  340.4 14.6 %collective-permute-done.35.refs_1_ = bf16[256,512]{1,0:T(8,128)(2,1)S(1)} collective-permute-done((bf16[256,512]{1,0:T(8,128)(2,1)}, bf16[256,512]{1,0:T(8,128)(2,1)S(1)}, u32[]{:S(2)}, u32[]{:S(2)}) %collective-permute-start.35) | collective-permute-done | bytes 262176 | tf_op jit(solution)/shard_map/ppermute | solution.py:102
  356.5 3.1 collective-permute-start.37
  359.6 4.1 %collective-permute-start.38 = (bf16[128,512]{1,0:T(8,128)(2,1)S(1)}, bf16[128,512]{1,0:T(8,128)(2,1)S(1)}, u32[]{:S(2)}, u32[]{:S(2)}) collective-permute-start(bf16[128,512]{1,0:T(8,128)(2,1)S(1)} %get-tuple-element.103), channel_id=1, source_target_pairs={{0,32},{16,48},{32,0},{48,16},{1,33},{17,49},{33,1},{49,17},{2,34}... | collective-permute-start | bytes 393224 | tf_op jit(solution)/shard_map/ppermute | solution.py:102
  363.7 3.5 collective-permute-start.39
  369.3 4.9 %collective-permute-done.38.refs_2_ = bf16[128,512]{1,0:T(8,128)(2,1)S(1)} collective-permute-done((bf16[128,512]{1,0:T(8,128)(2,1)S(1)}, bf16[128,512]{1,0:T(8,128)(2,1)S(1)}, u32[]{:S(2)}, u32[]{:S(2)}) %collective-permute-start.38) | collective-permute-done | bytes 131104 | tf_op jit(solution)/shard_map/ppermute | solution.py:102
  (198 shorter events, 106.7 us)
Async XLA Ops:
  7.2 89.2 %all-gather.2.cloned.1.call-start = ((), (), s32[]{:S(2)}) async-start(), calls=%async_computation.5 | async-start | bytes 4325376 | tf_op jit(solution)/shard_map/all_gather | solution.py:525
  15.5 48.9 %all-to-all-start = ((bf16[32,40,448]{2,1,0:T(8,128)(2,1)}), bf16[32,40,448]{2,1,0:T(8,128)(2,1)S(1)}, u32[]{:S(2)}, u32[]{:S(2)}) async-start(bf16[32,40,448]{2,1,0:T(8,128)(2,1)} %bitcast.19), calls=%async_computation | async-start | bytes 2621440 | tf_op jit(solution)/shard_map/all_to_all | solution.py:106
  67.6 14.0 %collective-permute-start = (bf16[320,1024]{1,0:T(8,128)(2,1)S(1)}, bf16[320,1024]{1,0:T(8,128)(2,1)S(1)}, u32[]{:S(2)}, u32[]{:S(2)}) collective-permute-start(bf16[320,1024]{1,0:T(8,128)(2,1)S(1)} %get-tuple-element.56), channel_id=1, source_target_pairs={{0,1},{1,2},{2,3},{3,0},{4,5},{5,6},{6,7},{7,4},{8,9},{9,10},{10,1... | collective-permute-start | bytes 1966088 | tf_op jit(solution)/shard_map/ppermute | solution.py:102
  68.6 13.0 %collective-permute-start.1 = (bf16[320,1024]{1,0:T(8,128)(2,1)S(1)}, bf16[320,1024]{1,0:T(8,128)(2,1)S(1)}, u32[]{:S(2)}, u32[]{:S(2)}) collective-permute-start(bf16[320,1024]{1,0:T(8,128)(2,1)S(1)} %get-tuple-element.58), channel_id=1, source_target_pairs={{0,3},{1,0},{2,1},{3,2},{4,7},{5,4},{6,5},{7,6},{8,11},{9,8},{10,9... | collective-permute-start | bytes 1966088 | tf_op jit(solution)/shard_map/ppermute | solution.py:102
  73.5 22.0 %collective-permute-start.4 = (bf16[320,1024]{1,0:T(8,128)(2,1)S(1)}, bf16[320,1024]{1,0:T(8,128)(2,1)S(1)}, u32[]{:S(2)}, u32[]{:S(2)}) collective-permute-start(bf16[320,1024]{1,0:T(8,128)(2,1)S(1)} %get-tuple-element.62), channel_id=1, source_target_pairs={{0,1},{1,2},{2,3},{3,0},{4,5},{5,6},{6,7},{7,4},{8,9},{9,10},{10,1... | collective-permute-start | bytes 1966088 | tf_op jit(solution)/shard_map/ppermute | solution.py:102
  73.6 22.0 %collective-permute-start.5 = (bf16[320,1024]{1,0:T(8,128)(2,1)S(1)}, bf16[320,1024]{1,0:T(8,128)(2,1)S(1)}, u32[]{:S(2)}, u32[]{:S(2)}) collective-permute-start(bf16[320,1024]{1,0:T(8,128)(2,1)S(1)} %get-tuple-element.63), channel_id=1, source_target_pairs={{0,3},{1,0},{2,1},{3,2},{4,7},{5,4},{6,5},{7,6},{8,11},{9,8},{10,9... | collective-permute-start | bytes 1966088 | tf_op jit(solution)/shard_map/ppermute | solution.py:102
  83.5 25.4 %collective-permute-start.2 = (bf16[160,1024]{1,0:T(8,128)(2,1)}, bf16[160,1024]{1,0:T(8,128)(2,1)}, u32[]{:S(2)}, u32[]{:S(2)}) collective-permute-start(bf16[160,1024]{1,0:T(8,128)(2,1)} %get-tuple-element.60), channel_id=1, source_target_pairs={{0,1},{1,2},{2,3},{3,0},{4,5},{5,6},{6,7},{7,4},{8,9},{9,10},{10,1... | collective-permute-start | bytes 983048 | tf_op jit(solution)/shard_map/ppermute | solution.py:102
  84.2 24.7 %collective-permute-start.3 = (bf16[160,1024]{1,0:T(8,128)(2,1)}, bf16[160,1024]{1,0:T(8,128)(2,1)}, u32[]{:S(2)}, u32[]{:S(2)}) collective-permute-start(bf16[160,1024]{1,0:T(8,128)(2,1)} %get-tuple-element.61.refs_4_), channel_id=1, source_target_pairs={{0,3},{1,0},{2,1},{3,2},{4,7},{5,4},{6,5},{7,6},{8,11},{9,8},{10,9... | collective-permute-start | bytes 983048 | tf_op jit(solution)/shard_map/ppermute | solution.py:102
  106.5 13.4 %collective-permute-start.10 = (bf16[320,512]{1,0:T(8,128)(2,1)S(1)}, bf16[320,512]{1,0:T(8,128)(2,1)S(1)}, u32[]{:S(2)}, u32[]{:S(2)}) collective-permute-start(bf16[320,512]{1,0:T(8,128)(2,1)S(1)} %get-tuple-element.74), channel_id=1, source_target_pairs={{0,3},{1,0},{2,1},{3,2},{4,7},{5,4},{6,5},{7,6},{8,11},{9,8},{10,9... | collective-permute-start | bytes 983048 | tf_op jit(solution)/shard_map/ppermute | solution.py:102
  111.2 25.5 %collective-permute-start.6 = (bf16[320,1024]{1,0:T(8,128)(2,1)S(1)}, bf16[320,1024]{1,0:T(8,128)(2,1)S(1)}, u32[]{:S(2)}, u32[]{:S(2)}) collective-permute-start(bf16[320,1024]{1,0:T(8,128)(2,1)S(1)} %third.5.refs_4_.refs_0_), channel_id=1, source_target_pairs={{0,4},{4,0},{1,5},{5,1},{2,6},{6,2},{3,7},{7,3},{8,12},{12,8},{9,1... | collective-permute-start | bytes 1966088 | tf_op jit(solution)/shard_map/ppermute | solution.py:102
  127.2 12.9 %collective-permute-start.16 = (bf16[320,512]{1,0:T(8,128)(2,1)S(1)}, bf16[320,512]{1,0:T(8,128)(2,1)S(1)}, u32[]{:S(2)}, u32[]{:S(2)}) collective-permute-start(bf16[320,512]{1,0:T(8,128)(2,1)S(1)} %third.6.refs_5_.refs_2_), channel_id=1, source_target_pairs={{0,4},{4,0},{1,5},{5,1},{2,6},{6,2},{3,7},{7,3},{8,12},{12,8},{9,1... | collective-permute-start | bytes 983048 | tf_op jit(solution)/shard_map/ppermute | solution.py:102
  140.5 24.6 %collective-permute-start.19 = (bf16[320,1024]{1,0:T(8,128)(2,1)S(1)}, bf16[320,1024]{1,0:T(8,128)(2,1)S(1)}, u32[]{:S(2)}, u32[]{:S(2)}) collective-permute-start(bf16[320,1024]{1,0:T(8,128)(2,1)S(1)} %slope.2.refs_4_.refs_2_), channel_id=1, source_target_pairs={{0,1},{1,2},{2,3},{3,0},{4,5},{5,6},{6,7},{7,4},{8,9},{9,10},{10,1... | collective-permute-start | bytes 1966088 | tf_op jit(solution)/shard_map/ppermute | solution.py:102
  140.6 24.5 %collective-permute-start.20 = (bf16[320,1024]{1,0:T(8,128)(2,1)S(1)}, bf16[320,1024]{1,0:T(8,128)(2,1)S(1)}, u32[]{:S(2)}, u32[]{:S(2)}) collective-permute-start(bf16[320,1024]{1,0:T(8,128)(2,1)S(1)} %slope.2.refs_4_.refs_2_), channel_id=1, source_target_pairs={{0,3},{1,0},{2,1},{3,2},{4,7},{5,4},{6,5},{7,6},{8,11},{9,8},{10,9... | collective-permute-start | bytes 1966088 | tf_op jit(solution)/shard_map/ppermute | solution.py:102
  143.3 18.9 %collective-permute-start.14 = (bf16[320,512]{1,0:T(8,128)(2,1)S(1)}, bf16[320,512]{1,0:T(8,128)(2,1)S(1)}, u32[]{:S(2)}, u32[]{:S(2)}) collective-permute-start(bf16[320,512]{1,0:T(8,128)(2,1)S(1)} %get-tuple-element.79), channel_id=1, source_target_pairs={{0,1},{1,2},{2,3},{3,0},{4,5},{5,6},{6,7},{7,4},{8,9},{9,10},{10,1... | collective-permute-start | bytes 983048 | tf_op jit(solution)/shard_map/ppermute | solution.py:102
  143.3 18.9 %collective-permute-start.15 = (bf16[320,512]{1,0:T(8,128)(2,1)S(1)}, bf16[320,512]{1,0:T(8,128)(2,1)S(1)}, u32[]{:S(2)}, u32[]{:S(2)}) collective-permute-start(bf16[320,512]{1,0:T(8,128)(2,1)S(1)} %get-tuple-element.81), channel_id=1, source_target_pairs={{0,3},{1,0},{2,1},{3,2},{4,7},{5,4},{6,5},{7,6},{8,11},{9,8},{10,9... | collective-permute-start | bytes 983048 | tf_op jit(solution)/shard_map/ppermute | solution.py:102
  146.0 29.9 %collective-permute-start.13 = (bf16[320,1024]{1,0:T(8,128)(2,1)S(1)}, bf16[320,1024]{1,0:T(8,128)(2,1)S(1)}, u32[]{:S(2)}, u32[]{:S(2)}) collective-permute-start(bf16[320,1024]{1,0:T(8,128)(2,1)S(1)} %third.7.refs_3_.refs_0_.refs_2_), channel_id=1, source_target_pairs={{0,4},{4,0},{1,5},{5,1},{2,6},{6,2},{3,7},{7,3},{8,12},{12,8},{9,1... | collective-permute-start | bytes 1966088 | tf_op jit(solution)/shard_map/ppermute | solution.py:102
  185.7 52.8 %all-to-all-start.1 = ((bf16[32,112,128]{2,1,0:T(8,128)(2,1)}), bf16[32,112,128]{2,1,0:T(8,128)(2,1)}, u32[]{:S(2)}, u32[]{:S(2)}) async-start(bf16[32,112,128]{2,1,0:T(8,128)(2,1)} %bitcast.28), calls=%async_computation.1 | async-start | bytes 1835008 | tf_op jit(solution)/shard_map/all_to_all | solution.py:106
  204.0 17.3 %collective-permute-start.24 = (bf16[320,1024]{1,0:T(8,128)(2,1)S(1)}, bf16[320,1024]{1,0:T(8,128)(2,1)S(1)}, u32[]{:S(2)}, u32[]{:S(2)}) collective-permute-start(bf16[320,1024]{1,0:T(8,128)(2,1)S(1)} %slope.3.refs_4_.refs_2_), channel_id=1, source_target_pairs={{0,1},{1,2},{2,3},{3,0},{4,5},{5,6},{6,7},{7,4},{8,9},{9,10},{10,1... | collective-permute-start | bytes 1966088 | tf_op jit(solution)/shard_map/ppermute | solution.py:102
  205.3 15.9 %collective-permute-start.25 = (bf16[320,1024]{1,0:T(8,128)(2,1)S(1)}, bf16[320,1024]{1,0:T(8,128)(2,1)S(1)}, u32[]{:S(2)}, u32[]{:S(2)}) collective-permute-start(bf16[320,1024]{1,0:T(8,128)(2,1)S(1)} %slope.3.refs_4_.refs_2_), channel_id=1, source_target_pairs={{0,3},{1,0},{2,1},{3,2},{4,7},{5,4},{6,5},{7,6},{8,11},{9,8},{10,9... | collective-permute-start | bytes 1966088 | tf_op jit(solution)/shard_map/ppermute | solution.py:102
  206.7 28.2 %collective-permute-start.22 = (bf16[320,1024]{1,0:T(8,128)(2,1)S(1)}, bf16[320,1024]{1,0:T(8,128)(2,1)S(1)}, u32[]{:S(2)}, u32[]{:S(2)}) collective-permute-start(bf16[320,1024]{1,0:T(8,128)(2,1)S(1)} %hidden.1.refs_9_.refs_1_), channel_id=1, source_target_pairs={{0,3},{1,0},{2,1},{3,2},{4,7},{5,4},{6,5},{7,6},{8,11},{9,8},{10,9... | collective-permute-start | bytes 1966088 | tf_op jit(solution)/shard_map/ppermute | solution.py:102
  208.0 27.2 %collective-permute-start.23 = (bf16[320,1024]{1,0:T(8,128)(2,1)S(1)}, bf16[320,1024]{1,0:T(8,128)(2,1)S(1)}, u32[]{:S(2)}, u32[]{:S(2)}) collective-permute-start(bf16[320,1024]{1,0:T(8,128)(2,1)S(1)} %hidden.1.refs_9_.refs_1_), channel_id=1, source_target_pairs={{0,1},{1,2},{2,3},{3,0},{4,5},{5,6},{6,7},{7,4},{8,9},{9,10},{10,1... | collective-permute-start | bytes 1966088 | tf_op jit(solution)/shard_map/ppermute | solution.py:102
  241.3 34.3 %all-to-all-start.2 = ((bf16[32,112,128]{2,1,0:T(8,128)(2,1)}), bf16[32,112,128]{2,1,0:T(8,128)(2,1)}, u32[]{:S(2)}, u32[]{:S(2)}) async-start(bf16[32,112,128]{2,1,0:T(8,128)(2,1)} %reorder.2.refs_9_), calls=%async_computation.2 | async-start | bytes 1835008 | tf_op jit(solution)/shard_map/all_to_all | solution.py:106
  255.0 22.6 %collective-permute-start.28 = (bf16[160,1024]{1,0:T(8,128)(2,1)}, bf16[160,1024]{1,0:T(8,128)(2,1)S(1)}, u32[]{:S(2)}, u32[]{:S(2)}) collective-permute-start(bf16[160,1024]{1,0:T(8,128)(2,1)} %get-tuple-element.87), channel_id=1, source_target_pairs={{0,1},{1,2},{2,3},{3,0},{4,5},{5,6},{6,7},{7,4},{8,9},{9,10},{10,1... | collective-permute-start | bytes 983048 | tf_op jit(solution)/shard_map/ppermute | solution.py:102
  255.0 22.6 %collective-permute-start.29 = (bf16[160,1024]{1,0:T(8,128)(2,1)}, bf16[160,1024]{1,0:T(8,128)(2,1)}, u32[]{:S(2)}, u32[]{:S(2)}) collective-permute-start(bf16[160,1024]{1,0:T(8,128)(2,1)} %get-tuple-element.88.refs_2_), channel_id=1, source_target_pairs={{0,3},{1,0},{2,1},{3,2},{4,7},{5,4},{6,5},{7,6},{8,11},{9,8},{10,9... | collective-permute-start | bytes 983048 | tf_op jit(solution)/shard_map/ppermute | solution.py:102
  291.9 36.1 %all-to-all-start.3 = ((bf16[32,112,128]{2,1,0:T(8,128)(2,1)}), bf16[32,112,128]{2,1,0:T(8,128)(2,1)S(1)}, u32[]{:S(2)}, u32[]{:S(2)}) async-start(bf16[32,112,128]{2,1,0:T(8,128)(2,1)} %bitcast.30), calls=%async_computation.3 | async-start | bytes 1835008 | tf_op jit(solution)/shard_map/all_to_all | solution.py:106
  305.2 21.6 %collective-permute-start.33 = (bf16[512,512]{1,0:T(8,128)(2,1)S(1)}, bf16[512,512]{1,0:T(8,128)(2,1)S(1)}, u32[]{:S(2)}, u32[]{:S(2)}) collective-permute-start(bf16[512,512]{1,0:T(8,128)(2,1)S(1)} %get-tuple-element.96), channel_id=1, source_target_pairs={{0,64},{64,128},{128,192},{192,0},{1,65},{65,129},{129,193},{193,1... | collective-permute-start | bytes 1572872 | tf_op jit(solution)/shard_map/ppermute | solution.py:102
  306.9 20.3 %collective-permute-start.34 = (bf16[512,512]{1,0:T(8,128)(2,1)S(1)}, bf16[512,512]{1,0:T(8,128)(2,1)S(1)}, u32[]{:S(2)}, u32[]{:S(2)}) collective-permute-start(bf16[512,512]{1,0:T(8,128)(2,1)S(1)} %get-tuple-element.98), channel_id=1, source_target_pairs={{0,192},{64,0},{128,64},{192,128},{1,193},{65,1},{129,65},{193,129... | collective-permute-start | bytes 1572872 | tf_op jit(solution)/shard_map/ppermute | solution.py:102
  329.8 46.0 %all-to-all-start.4 = ((bf16[32,112,128]{2,1,0:T(8,128)(2,1)}), bf16[32,112,128]{2,1,0:T(8,128)(2,1)S(1)}, u32[]{:S(2)}, u32[]{:S(2)}) async-start(bf16[32,112,128]{2,1,0:T(8,128)(2,1)} %reorder.3.refs_5_), calls=%async_computation.4 | async-start | bytes 1835008 | tf_op jit(solution)/shard_map/all_to_all | solution.py:106
  337.6 17.5 %collective-permute-start.35 = (bf16[256,512]{1,0:T(8,128)(2,1)}, bf16[256,512]{1,0:T(8,128)(2,1)S(1)}, u32[]{:S(2)}, u32[]{:S(2)}) collective-permute-start(bf16[256,512]{1,0:T(8,128)(2,1)} %get-tuple-element.99), channel_id=1, source_target_pairs={{0,64},{64,128},{128,192},{192,0},{1,65},{65,129},{129,193},{193,1... | collective-permute-start | bytes 786440 | tf_op jit(solution)/shard_map/ppermute | solution.py:102
  339.0 16.0 %collective-permute-start.36 = (bf16[256,512]{1,0:T(8,128)(2,1)S(1)}, bf16[256,512]{1,0:T(8,128)(2,1)S(1)}, u32[]{:S(2)}, u32[]{:S(2)}) collective-permute-start(bf16[256,512]{1,0:T(8,128)(2,1)S(1)} %get-tuple-element.100.refs_2_), channel_id=1, source_target_pairs={{0,192},{64,0},{128,64},{192,128},{1,193},{65,1},{129,65},{193,129... | collective-permute-start | bytes 786440 | tf_op jit(solution)/shard_map/ppermute | solution.py:102
  356.5 12.8 %collective-permute-start.37 = (bf16[128,512]{1,0:T(8,128)(2,1)S(1)}, bf16[128,512]{1,0:T(8,128)(2,1)S(1)}, u32[]{:S(2)}, u32[]{:S(2)}) collective-permute-start(bf16[128,512]{1,0:T(8,128)(2,1)S(1)} %get-tuple-element.102), channel_id=1, source_target_pairs={{0,16},{16,32},{32,48},{48,0},{1,17},{17,33},{33,49},{49,1},{2,18}... | collective-permute-start | bytes 393224 | tf_op jit(solution)/shard_map/ppermute | solution.py:102
  359.6 14.6 %collective-permute-start.38 = (bf16[128,512]{1,0:T(8,128)(2,1)S(1)}, bf16[128,512]{1,0:T(8,128)(2,1)S(1)}, u32[]{:S(2)}, u32[]{:S(2)}) collective-permute-start(bf16[128,512]{1,0:T(8,128)(2,1)S(1)} %get-tuple-element.103), channel_id=1, source_target_pairs={{0,32},{16,48},{32,0},{48,16},{1,33},{17,49},{33,1},{49,17},{2,34}... | collective-permute-start | bytes 393224 | tf_op jit(solution)/shard_map/ppermute | solution.py:102
  (59 other events, 548.1 us)
Sparse Core Ops, SparseCore 0:
  12.1 76.5 all-gather.1

commit v2 on v1

--- a/solution.py
+++ b/solution.py
@@ -25,6 +25,7 @@
 block_rows = 160
 order = (4, 3, 5, 6, 2, 7, 0, 1)
 chunks = ((0, 512), (512, 512))
+span = 512
 
 expert_axes = ("y", "zh", "c")
 vmem_bytes = 32 * 1024 * 1024
@@ -169,7 +170,7 @@
     own[...] = result[960:1280]
 
 
-def project(run, info, left, right, blocks, column):
+def project(run, info, left, right, blocks, column, waits=()):
     columns = 256 * blocks
     sizes = (320, 320, 160, 160, 320)
     return run(
@@ -185,6 +186,7 @@
         grid=(blocks,),
         prefetch=info,
         cost=(2 * rows * width * columns, 2 * rows * (width + columns), 0),
+        waits=waits,
     )
 
 
@@ -220,7 +222,7 @@
     def half(self, which):
         return pl.BlockSpec((self.height, self.block), lambda j: (which, j))
 
-    def second(self):
+    def second(self, waits=()):
         right, left = self.run(
             second_kernel,
             "second",
@@ -229,6 +231,7 @@
             in_specs=[self.half(0)] * 4,
             out_specs=[self.half(0)] * 2,
             grid=(self.columns // self.block,),
+            waits=waits,
         )
         self.low = shift(right, self.axis, 1)
         self.high = shift(left, self.axis, -1)
@@ -288,31 +291,6 @@
         return [self.own, self.from_right, self.far_low, self.far_high, self.from_left]
 
 
-def hidden_kernel(*refs):
-    out = refs[-1]
-    at = 0
-    for i in range(0, len(refs) - 1, 2):
-        pre = add(refs[i][...], refs[i + 1][...])
-        units = pre.shape[1] // 2
-        gate, up = pre[:, :units], pre[:, units:]
-        out[:, at : at + units] = (gate * jax.nn.sigmoid(gate) * up).astype(bf16)
-        at += units
-
-
-def hidden_of(run, sums):
-    inputs = [v for s in sums for v in s.result()]
-    return run(
-        hidden_kernel,
-        "hidden",
-        array(320, hidden_units),
-        inputs,
-        in_specs=[pl.BlockSpec((80, v.shape[1]), lambda i: (i, 0)) for v in inputs],
-        out_specs=pl.BlockSpec((80, hidden_units), lambda i: (i, 0)),
-        grid=(4,),
-        cost=(0, 3_000_000, 320 * hidden_units),
-    )
-
-
 def slope_kernel(pre, pre_other, back, back_other, out):
     p = add(pre[...], pre_other[...])
     units = p.shape[1] // 2
@@ -321,21 +299,30 @@
     sigma = jax.nn.sigmoid(gate)
     slope = sigma * (1.0 + gate * (1.0 - sigma))
     out[:, :units] = (hidden_grad * up * slope).astype(bf16)
-    out[:, units:] = (hidden_grad * (gate * sigma)).astype(bf16)
-
-
-def pre_grad_of(run, pre, back):
-    inputs = pre.result() + back.result()
-    columns = pre.columns
+    out[:, units : 2 * units] = (hidden_grad * (gate * sigma)).astype(bf16)
+
+
+def both_kernel(pre_one, other_one, pre_two, other_two, back, back_other, out):
+    slope_kernel(pre_two, other_two, back, back_other, out)
+    at = pre_two.shape[1]
+    for value, other in ((pre_one, other_one), (pre_two, other_two)):
+        pre = add(value[...], other[...])
+        units = pre.shape[1] // 2
+        gate, up = pre[:, :units], pre[:, units:]
+        out[:, at : at + units] = (gate * jax.nn.sigmoid(gate) * up).astype(bf16)
+        at += units
+
+
+def activation(run, kernel, name, sums, columns):
+    inputs = [v for s in sums for v in s.result()]
     return run(
-        slope_kernel,
-        "slope",
+        kernel,
+        name,
         array(320, columns),
         inputs,
         in_specs=[pl.BlockSpec((80, v.shape[1]), lambda i: (i, 0)) for v in inputs],
         out_specs=pl.BlockSpec((80, columns), lambda i: (i, 0)),
         grid=(4,),
-        cost=(0, 3_000_000, 160 * columns),
     )
 
 
@@ -383,48 +370,49 @@
     )
 
 
-def reorder_kernel(anchor, source, out):
+def merge_kernel(anchor, spread, step, out):
+    height = step.shape[1]
+
     def one(d, carry):
-        out[d] = source[anchor[d]]
+        out[d, :height] = spread[anchor[d]]
+        out[d, height:] = step[d]
         return carry
 
     lax.fori_loop(0, experts, one, 0)
 
 
-def place_kernel(moved, *refs, out):
-    for i in range(moved.shape[0]):
-        refs[out][:, i * 128 : (i + 1) * 128] = moved[i]
-
-
-def place(run, moved, base, chunk, through=None):
-    start, units = chunk
-    tiles = units // 128
-    anywhere = pl.BlockSpec(memory_space=pl.ANY)
-    in_specs = [pl.BlockSpec((tiles, width, 128), lambda j: (j, 0, 0))]
-    out_specs = [
-        pl.BlockSpec(
-            (width, units), lambda j: (0, start // units + j * (hidden_units // units))
-        )
-    ]
-    inputs, shapes, aliases = [moved], [array(width, 2 * hidden_units)], {}
-    for value, at in ((base, 0), (through, 1)):
-        if value is None:
-            continue
-        aliases[len(inputs)] = at
-        inputs.append(value)
-        in_specs.append(anywhere)
-        if at:
-            shapes.append(array(*value.shape))
-            out_specs.append(anywhere)
+def reorder_kernel(anchor, merged, out):
+    height = out.shape[1]
+
+    def one(d, carry):
+        out[d] = merged[anchor[d], height:]
+        return carry
+
+    lax.fori_loop(0, experts, one, 0)
+
+
+def place_kernel(first, second, out):
+    for chunk, moved in enumerate((first, second)):
+
+        @pl.when(pl.program_id(0) % 2 == chunk)
+        def _():
+            for piece in range(moved.shape[0]):
+                at, tile = piece % 4 * 112, piece // 4 * 128
+                out[at : at + 112, tile : tile + 128] = moved[piece, :112]
+
+
+def place(run, first, second):
+    half = experts // 2
     return run(
-        functools.partial(place_kernel, out=len(inputs) - 1),
+        place_kernel,
         "place",
-        shapes,
-        inputs,
-        in_specs=in_specs,
-        out_specs=out_specs,
-        grid=(2,),
-        aliases=aliases,
+        array(width, 2 * hidden_units),
+        [first, second],
+        in_specs=[
+            pl.BlockSpec((half, *v.shape[1:]), lambda j: (j // 2, 0, 0)) for v in (first, second)
+        ],
+        out_specs=pl.BlockSpec((width, span), lambda j: (0, j)),
+        grid=(4,),
     )
 
 
@@ -541,12 +529,18 @@
             run, project(run, info, routed_tokens, inner, blocks, column(chunk))
         )
 
-    def back_sum(chunk):
+    def back_sum(chunk, waits=()):
         start, units = chunk
         return RingSum(
             run,
             project(
-                run, info, routed_grads, outer, units // 256, lambda j: start // 256 + j
+                run,
+                info,
+                routed_grads,
+                outer,
+                units // 256,
+                lambda j: start // 256 + j,
+                waits,
             ),
         )
 
@@ -564,12 +558,6 @@
 
     def spread(step):
         return exchange(step.reshape(experts, -1, 128))
-
-    def deliver(pieces):
-        picked = run(
-            reorder_kernel, "reorder", array(*pieces.shape), [pieces], prefetch=anchor
-        )
-        return exchange(picked).reshape(-1, width, 128)
 
     one, two = chunks
     pre_one = pre_sum(one)
@@ -592,31 +580,29 @@
         ],
         grid=(4,),
         prefetch=info,
-        waits=[pre_two.got_left, pre_two.got_right],
     )
     routed_grads = routed_grads.reshape(8, block_rows, width)
-    back_one = back_sum(one)
+    back_one = back_sum(one, waits=[pre_two.got_left, pre_two.got_right])
     pre_one.cross()
+    back_one.second()
+    back_two = back_sum(two)
+    back_one.cross()
+    back_two.second(waits=[pre_one.other])
     pre_two.second()
-    back_one.second()
-    back_one.cross()
+    back_two.cross()
     pre_two.cross()
-    back_two = back_sum(two)
-    grad_one = RowGather(run, pre_grad_of(run, pre_one, back_one))
-    back_two.second()
+    grad_one = RowGather(
+        run, activation(run, slope_kernel, "slope", [pre_one, back_one], pre_one.columns)
+    )
     grad_one.second()
-    back_two.cross()
-    grad_two = RowGather(run, pre_grad_of(run, pre_two, back_two))
-    hidden = RowGather(run, hidden_of(run, (pre_one, pre_two)))
-    step_one = steps(one, grad_one)
-    spread_one = spread(step_one)
-    grad_two.second()
-    hidden.second()
-    moved_one = deliver(spread_one)
-    step_two = steps(two, grad_two)
-    update, step_two = place(run, moved_one, None, one, step_two)
-    spread_two = spread(step_two)
-    gathered = hidden.result()
+    sums = [pre_one, pre_two, back_two]
+    both = RowGather(
+        run,
+        activation(run, both_kernel, "both", sums, pre_two.columns + hidden_units),
+    )
+    first_spread = spread(steps(one, grad_one))
+    both.second()
+    gathered = both.result()
     early = lambda g, info: (jnp.minimum(g, 3), 0)
     late = lambda g, info: (jnp.maximum(g - 4, 0), 0)
     out_here, out_there = run(
@@ -624,6 +610,10 @@
         "outputs",
         [array(2048, 512)] * 2,
         [*gathered, outer, gates, wanted],
+        in_specs=[
+            pl.BlockSpec((p.shape[0], hidden_units), lambda g, info: (0, 1)) for p in gathered
+        ]
+        + [whole(outer), whole(gates), whole(wanted)],
         out_specs=[pl.BlockSpec((512, 512), late), pl.BlockSpec((512, 512), early)],
         grid=(8,),
         prefetch=info,
@@ -631,6 +621,16 @@
         scratch=[pltpu.VMEM((experts, capacity, 512), f32)],
     )
     other = shift(out_there, "c", 1)
+    step_two = steps(two, both).reshape(experts, -1, 128)
+    height = step_two.shape[1]
+    merged = run(
+        merge_kernel,
+        "merge",
+        array(experts, 2 * height, 128),
+        [first_spread, step_two],
+        prefetch=anchor,
+    )
+    merged = exchange(merged)
     pieces = run(
         split_kernel,
         "split",
@@ -639,11 +639,14 @@
     )
     along_y = RingSum(run, pieces, "y")
     along_y.second()
-    moved_two = deliver(spread_two)
     parts = run(cut_kernel, "cut", [array(tok_count, 512)] * 4, [along_y.third()])
     parts = [parts[0]] + [shift(parts[by], "zh", by) for by in (1, 2, 3)]
     combined = run(sum_kernel, "sum", array(tok_count, width), parts)
-    (update,) = place(run, moved_two, update, two)
+    second_spread = run(
+        reorder_kernel, "reorder", array(experts, height, 128), [merged], prefetch=anchor
+    )
+    second_moved = exchange(second_spread)
+    update = place(run, merged, second_moved)
     return combined, update[None]
 
 

time: 390 us -> 370 us (0.949)
  the two profiles are of different devices: /device:TPU:1 before, /device:TPU:39 now
where the time goes in v2:
time: 370 us; the launch traced here: 364 us
  waiting for transfers between devices  181 us (49%)
  starting transfers between devices  100 us (27%)
  Pallas kernels  51.8 us (14%)
  between operations  14.7 us (4%)
  local copies, waits for them, and re-layouts  13 us (4%)
    ppermute x36, waiting for transfers between devices, shift(): return lax.ppermute(value, axis, [(i, (i + by) % n) for i in range(n)])  117 us
    all_to_all x4, waiting for transfers between devices, exchange(): lax.all_to_all(value, expert_axes, split_axis=0, concat_axis=0, tiled=True)  64.9 us
    ppermute x36, starting transfers between devices, shift(): return lax.ppermute(value, axis, [(i, (i + by) % n) for i in range(n)])  55.9 us
    pallas_call x29, Pallas kernels, __call__(): pl.pallas_call(body, out_shape=out_shape, grid_spec=pltpu.PrefetchScalarG...  51.8 us
    all_to_all x4, starting transfers between devices, exchange(): lax.all_to_all(value, expert_axes, split_axis=0, concat_axis=0, tiled=True)  44.2 us
    unnamed x67, local copies, waits for them, and re-layouts  11.1 us
  transfers between devices with their start and end apart: 41, of which 28 were waited for; matrix products, arithmetic and copies ran while one was open for 1% of the time, Pallas kernels for 12%

profile of v2, /device:TPU:39, one launch (start us, length us, event | category | flops | bytes accessed | tf_op | source)
XLA Modules:
  0.0 364.4 jit_solution(12500533655420457221)
XLA Ops:
  15.4 11.0 %all-to-all-start = ((bf16[32,40,448]{2,1,0:T(8,128)(2,1)}), bf16[32,40,448]{2,1,0:T(8,128)(2,1)S(1)}, u32[]{:S(2)}, u32[]{:S(2)}) async-start(bf16[32,40,448]{2,1,0:T(8,128)(2,1)} %bitcast.19), calls=%async_computation | async-start | bytes 2621440 | tf_op jit(solution)/shard_map/all_to_all | solution.py:107
  26.6 38.8 %all-to-all-done = bf16[32,40,448]{2,1,0:T(8,128)(2,1)S(1)} async-done(((bf16[32,40,448]{2,1,0:T(8,128)(2,1)}), bf16[32,40,448]{2,1,0:T(8,128)(2,1)S(1)}, u32[]{:S(2)}, u32[]{:S(2)}) %all-to-all-start) | async-done | bytes 1146912 | tf_op jit(solution)/shard_map/all_to_all | solution.py:107
  65.4 3.1 project.4
  70.1 3.5 project.5
  75.3 10.1 %collective-permute-done.refs_1_.refs_4_ = bf16[320,1024]{1,0:T(8,128)(2,1)S(1)} collective-permute-done((bf16[320,1024]{1,0:T(8,128)(2,1)S(1)}, bf16[320,1024]{1,0:T(8,128)(2,1)S(1)}, u32[]{:S(2)}, u32[]{:S(2)}) %collective-permute-start) | collective-permute-done | bytes 655392 | tf_op jit(solution)/shard_map/ppermute | solution.py:103
  93.1 2.9 arrive.1
  121.4 8.4 %collective-permute-done.11.refs_1_ = bf16[160,512]{1,0:T(8,128)(2,1)S(1)} collective-permute-done((bf16[160,512]{1,0:T(8,128)(2,1)S(1)}, bf16[160,512]{1,0:T(8,128)(2,1)S(1)}, u32[]{:S(2)}, u32[]{:S(2)}) %collective-permute-start.11) | collective-permute-done | bytes 163872 | tf_op jit(solution)/shard_map/ppermute | solution.py:103
  137.5 6.4 %collective-permute-done.15.refs_1_ = bf16[160,512]{1,0:T(8,128)(2,1)S(1)} collective-permute-done((bf16[160,512]{1,0:T(8,128)(2,1)S(1)}, bf16[160,512]{1,0:T(8,128)(2,1)S(1)}, u32[]{:S(2)}, u32[]{:S(2)}) %collective-permute-start.15) | collective-permute-done | bytes 163872 | tf_op jit(solution)/shard_map/ppermute | solution.py:103
  144.0 3.0 collective-permute-done.16.refs_3_
  151.5 10.5 %collective-permute-done.20.refs_0_.refs_6_ = bf16[320,1024]{1,0:T(8,128)(2,1)S(1)} collective-permute-done((bf16[320,1024]{1,0:T(8,128)(2,1)S(1)}, bf16[320,1024]{1,0:T(8,128)(2,1)S(1)}, u32[]{:S(2)}, u32[]{:S(2)}) %collective-permute-start.20) | collective-permute-done | bytes 655392 | tf_op jit(solution)/shard_map/ppermute | solution.py:103
  165.4 4.6 %collective-permute-done.18.refs_5_ = bf16[320,512]{1,0:T(8,128)(2,1)S(1)} collective-permute-done((bf16[320,512]{1,0:T(8,128)(2,1)S(1)}, bf16[320,512]{1,0:T(8,128)(2,1)S(1)}, u32[]{:S(2)}, u32[]{:S(2)}) %collective-permute-start.18) | collective-permute-done | bytes 327712 | tf_op jit(solution)/shard_map/ppermute | solution.py:103
  171.3 12.1 %collective-permute-start.23 = (bf16[320,2048]{1,0:T(8,128)(2,1)S(1)}, bf16[320,2048]{1,0:T(8,128)(2,1)}, u32[]{:S(2)}, u32[]{:S(2)}) collective-permute-start(bf16[320,2048]{1,0:T(8,128)(2,1)S(1)} %both.1.refs_9_.refs_1_.refs_2_), channel_id=1, source_target_pairs={{0,1},{1,2},{2,3},{3,0},{4,5},{5,6},{6,7},{7,4},{8,9},{9,10},{10,1... | collective-permute-start | bytes 3932168 | tf_op jit(solution)/shard_map/ppermute | solution.py:103
  183.4 5.1 %adam.2.refs_2_ = bf16[8,448,128]{2,1,0:T(8,128)(2,1)} custom-call(s32[41]{0:T(128)S(1)} %copy-done.25, bf16[8,160,448]{2,1,0:T(8,128)(2,1)S(1)} %bitcast.51, bf16[320,1024]{1,0:T(8,128)(2,1)S(1)} %slope.1.refs_2_, bf16[320,1024]{1,0:T(8,128)(2,1)S(1)} %collective-permute-done.21.refs_1_.refs_3_, bf16[160,1024]{1,0:T(8,128)(2,1)S(1)} %collective-permute-done.24.refs_4_, ...), custom_call_target="tpu_custom_call" | custom-call | flops 1174405120 | bytes 8000000 | tf_op jit(solution)/shard_map/adam/pallas_call | solution.py:80
  188.5 9.0 %all-to-all-start.1 = ((bf16[32,112,128]{2,1,0:T(8,128)(2,1)}), bf16[32,112,128]{2,1,0:T(8,128)(2,1)}, u32[]{:S(2)}, u32[]{:S(2)}) async-start(bf16[32,112,128]{2,1,0:T(8,128)(2,1)} %bitcast.28), calls=%async_computation.1 | async-start | bytes 1835008 | tf_op jit(solution)/shard_map/all_to_all | solution.py:107
  200.0 7.2 %collective-permute-done.23.refs_0_.refs_5_.refs_6_ = bf16[320,2048]{1,0:T(8,128)(2,1)} collective-permute-done((bf16[320,2048]{1,0:T(8,128)(2,1)S(1)}, bf16[320,2048]{1,0:T(8,128)(2,1)}, u32[]{:S(2)}, u32[]{:S(2)}) %collective-permute-start.23) | collective-permute-done | bytes 1310752 | tf_op jit(solution)/shard_map/ppermute | solution.py:103
  207.2 4.3 %forward.3 = (bf16[160,2048]{1,0:T(8,128)(2,1)S(1)}, bf16[160,2048]{1,0:T(8,128)(2,1)S(1)}) custom-call(bf16[320,2048]{1,0:T(8,128)(2,1)} %collective-permute-done.23.refs_0_.refs_5_.refs_6_, bf16[320,2048]{1,0:T(8,128)(2,1)} %collective-permute-done.22.refs_1_.refs_2_.refs_3_, bf16[8,448,128]{2,1,0:T(8,128)(2,1)} %adam.2.refs_2_), custom_call_target="tpu_custom_call" | custom-call | bytes 1000000 | tf_op jit(solution)/shard_map/forward/pallas_call | solution.py:80
  211.5 3.3 collective-permute-start.26
  215.4 8.0 %collective-permute-done.26.refs_3_.refs_4_ = bf16[160,2048]{1,0:T(8,128)(2,1)S(1)} collective-permute-done((bf16[160,2048]{1,0:T(8,128)(2,1)S(1)}, bf16[160,2048]{1,0:T(8,128)(2,1)S(1)}, u32[]{:S(2)}, u32[]{:S(2)}) %collective-permute-start.26) | collective-permute-done | bytes 655392 | tf_op jit(solution)/shard_map/ppermute | solution.py:103
  223.4 3.1 collective-permute-done.27.refs_4_.refs_5_
  226.6 6.8 %outputs.1 = (bf16[2048,512]{1,0:T(8,128)(2,1)S(1)}, bf16[2048,512]{1,0:T(8,128)(2,1)S(1)}) custom-call(s32[41]{0:T(128)S(1)} %copy-done.26, bf16[320,2048]{1,0:T(8,128)(2,1)S(1)} %both.1.refs_9_.refs_1_.refs_2_, bf16[320,2048]{1,0:T(8,128)(2,1)} %collective-permute-done.22.refs_1_.refs_2_.refs_3_, ...), custom_call_target="tpu_custom_call" | custom-call | flops 1174405120 | bytes 5000000 | tf_op jit(solution)/shard_map/outputs/pallas_call | solution.py:80
  234.7 5.1 %adam.3.refs_3_ = bf16[8,448,128]{2,1,0:T(8,128)(2,1)S(1)} custom-call(s32[41]{0:T(128)S(1)} %copy-done.26, bf16[8,160,448]{2,1,0:T(8,128)(2,1)S(1)} %bitcast.52, bf16[320,2048]{1,0:T(8,128)(2,1)S(1)} %both.1.refs_9_.refs_1_.refs_2_, bf16[320,2048]{1,0:T(8,128)(2,1)} %collective-permute-done.22.refs_1_.refs_2_.refs_3_, ...), custom_call_target="tpu_custom_call" | custom-call | flops 1174405120 | bytes 8000000 | tf_op jit(solution)/shard_map/adam/pallas_call | solution.py:80
  241.2 3.2 merge.1.refs_2_
  244.4 11.3 %all-to-all-start.2 = ((bf16[32,224,128]{2,1,0:T(8,128)(2,1)}), bf16[32,224,128]{2,1,0:T(8,128)(2,1)S(1)}, u32[]{:S(2)}, u32[]{:S(2)}) async-start(bf16[32,224,128]{2,1,0:T(8,128)(2,1)} %merge.1.refs_2_), calls=%async_computation.2 | async-start | bytes 3670016 | tf_op jit(solution)/shard_map/all_to_all | solution.py:107
  256.0 4.1 %collective-permute-done.28.refs_1_ = bf16[2048,512]{1,0:T(8,128)(2,1)S(1)} collective-permute-done((bf16[2048,512]{1,0:T(8,128)(2,1)}, bf16[2048,512]{1,0:T(8,128)(2,1)S(1)}, u32[]{:S(2)}, u32[]{:S(2)}) %collective-permute-start.28) | collective-permute-done | bytes 2097184 | tf_op jit(solution)/shard_map/ppermute | solution.py:103
  265.0 18.0 %collective-permute-done.29.refs_1_.refs_4_ = bf16[512,512]{1,0:T(8,128)(2,1)S(1)} collective-permute-done((bf16[512,512]{1,0:T(8,128)(2,1)S(1)}, bf16[512,512]{1,0:T(8,128)(2,1)S(1)}, u32[]{:S(2)}, u32[]{:S(2)}) %collective-permute-start.29) | collective-permute-done | bytes 524320 | tf_op jit(solution)/shard_map/ppermute | solution.py:103
  286.4 7.2 %collective-permute-done.31.refs_1_ = bf16[256,512]{1,0:T(8,128)(2,1)S(1)} collective-permute-done((bf16[256,512]{1,0:T(8,128)(2,1)S(1)}, bf16[256,512]{1,0:T(8,128)(2,1)S(1)}, u32[]{:S(2)}, u32[]{:S(2)}) %collective-permute-start.31) | collective-permute-done | bytes 262176 | tf_op jit(solution)/shard_map/ppermute | solution.py:103
  294.4 7.3 %collective-permute-start.33 = (bf16[128,512]{1,0:T(8,128)(2,1)S(1)}, bf16[128,512]{1,0:T(8,128)(2,1)S(1)}, u32[]{:S(2)}, u32[]{:S(2)}) collective-permute-start(bf16[128,512]{1,0:T(8,128)(2,1)S(1)} %get-tuple-element.95), channel_id=1, source_target_pairs={{0,16},{16,32},{32,48},{48,0},{1,17},{17,33},{33,49},{49,1},{2,18}... | collective-permute-start | bytes 393224 | tf_op jit(solution)/shard_map/ppermute | solution.py:103
  301.8 2.9 collective-permute-start.34
  304.6 3.5 collective-permute-start.35
  308.1 3.6 %collective-permute-done.33.refs_1_ = bf16[128,512]{1,0:T(8,128)(2,1)S(1)} collective-permute-done((bf16[128,512]{1,0:T(8,128)(2,1)S(1)}, bf16[128,512]{1,0:T(8,128)(2,1)S(1)}, u32[]{:S(2)}, u32[]{:S(2)}) %collective-permute-start.33) | collective-permute-done | bytes 131104 | tf_op jit(solution)/shard_map/ppermute | solution.py:103
  315.8 12.9 %all-to-all-start.3 = ((bf16[32,112,128]{2,1,0:T(8,128)(2,1)}), bf16[32,112,128]{2,1,0:T(8,128)(2,1)S(1)}, u32[]{:S(2)}, u32[]{:S(2)}) async-start(bf16[32,112,128]{2,1,0:T(8,128)(2,1)} %reorder.1.refs_2_), calls=%async_computation.3 | async-start | bytes 1835008 | tf_op jit(solution)/shard_map/all_to_all | solution.py:107
  329.5 26.1 %all-to-all-done.3.refs_1_ = bf16[32,112,128]{2,1,0:T(8,128)(2,1)S(1)} async-done(((bf16[32,112,128]{2,1,0:T(8,128)(2,1)}), bf16[32,112,128]{2,1,0:T(8,128)(2,1)S(1)}, u32[]{:S(2)}, u32[]{:S(2)}) %all-to-all-start.3) | async-done | bytes 917536 | tf_op jit(solution)/shard_map/all_to_all | solution.py:107
  (158 shorter events, 83.1 us)
Async XLA Ops:
  7.2 83.1 %all-gather.2.cloned.1.call-start = ((), (), s32[]{:S(2)}) async-start(), calls=%async_computation.4 | async-start | bytes 4325376 | tf_op jit(solution)/shard_map/all_gather | solution.py:513
  15.4 50.0 %all-to-all-start = ((bf16[32,40,448]{2,1,0:T(8,128)(2,1)}), bf16[32,40,448]{2,1,0:T(8,128)(2,1)S(1)}, u32[]{:S(2)}, u32[]{:S(2)}) async-start(bf16[32,40,448]{2,1,0:T(8,128)(2,1)} %bitcast.19), calls=%async_computation | async-start | bytes 2621440 | tf_op jit(solution)/shard_map/all_to_all | solution.py:107
  68.5 16.8 %collective-permute-start = (bf16[320,1024]{1,0:T(8,128)(2,1)S(1)}, bf16[320,1024]{1,0:T(8,128)(2,1)S(1)}, u32[]{:S(2)}, u32[]{:S(2)}) collective-permute-start(bf16[320,1024]{1,0:T(8,128)(2,1)S(1)} %get-tuple-element.52), channel_id=1, source_target_pairs={{0,1},{1,2},{2,3},{3,0},{4,5},{5,6},{6,7},{7,4},{8,9},{9,10},{10,1... | collective-permute-start | bytes 1966088 | tf_op jit(solution)/shard_map/ppermute | solution.py:103
  69.0 18.0 %collective-permute-start.1 = (bf16[320,1024]{1,0:T(8,128)(2,1)S(1)}, bf16[320,1024]{1,0:T(8,128)(2,1)S(1)}, u32[]{:S(2)}, u32[]{:S(2)}) collective-permute-start(bf16[320,1024]{1,0:T(8,128)(2,1)S(1)} %get-tuple-element.54), channel_id=1, source_target_pairs={{0,3},{1,0},{2,1},{3,2},{4,7},{5,4},{6,5},{7,6},{8,11},{9,8},{10,9... | collective-permute-start | bytes 1966088 | tf_op jit(solution)/shard_map/ppermute | solution.py:103
  73.6 25.8 %collective-permute-start.4 = (bf16[320,1024]{1,0:T(8,128)(2,1)}, bf16[320,1024]{1,0:T(8,128)(2,1)S(1)}, u32[]{:S(2)}, u32[]{:S(2)}) collective-permute-start(bf16[320,1024]{1,0:T(8,128)(2,1)} %get-tuple-element.59), channel_id=1, source_target_pairs={{0,1},{1,2},{2,3},{3,0},{4,5},{5,6},{6,7},{7,4},{8,9},{9,10},{10,1... | collective-permute-start | bytes 1966088 | tf_op jit(solution)/shard_map/ppermute | solution.py:103
  75.3 25.8 %collective-permute-start.5 = (bf16[320,1024]{1,0:T(8,128)(2,1)}, bf16[320,1024]{1,0:T(8,128)(2,1)S(1)}, u32[]{:S(2)}, u32[]{:S(2)}) collective-permute-start(bf16[320,1024]{1,0:T(8,128)(2,1)} %get-tuple-element.60), channel_id=1, source_target_pairs={{0,3},{1,0},{2,1},{3,2},{4,7},{5,4},{6,5},{7,6},{8,11},{9,8},{10,9... | collective-permute-start | bytes 1966088 | tf_op jit(solution)/shard_map/ppermute | solution.py:103
  88.7 17.4 %collective-permute-start.2 = (bf16[160,1024]{1,0:T(8,128)(2,1)}, bf16[160,1024]{1,0:T(8,128)(2,1)}, u32[]{:S(2)}, u32[]{:S(2)}) collective-permute-start(bf16[160,1024]{1,0:T(8,128)(2,1)} %get-tuple-element.56), channel_id=1, source_target_pairs={{0,1},{1,2},{2,3},{3,0},{4,5},{5,6},{6,7},{7,4},{8,9},{9,10},{10,1... | collective-permute-start | bytes 983048 | tf_op jit(solution)/shard_map/ppermute | solution.py:103
  88.9 19.1 %collective-permute-start.3 = (bf16[160,1024]{1,0:T(8,128)(2,1)}, bf16[160,1024]{1,0:T(8,128)(2,1)}, u32[]{:S(2)}, u32[]{:S(2)}) collective-permute-start(bf16[160,1024]{1,0:T(8,128)(2,1)} %get-tuple-element.57.refs_2_), channel_id=1, source_target_pairs={{0,3},{1,0},{2,1},{3,2},{4,7},{5,4},{6,5},{7,6},{8,11},{9,8},{10,9... | collective-permute-start | bytes 983048 | tf_op jit(solution)/shard_map/ppermute | solution.py:103
  102.9 12.0 %collective-permute-start.8 = (bf16[320,512]{1,0:T(8,128)(2,1)S(1)}, bf16[320,512]{1,0:T(8,128)(2,1)S(1)}, u32[]{:S(2)}, u32[]{:S(2)}) collective-permute-start(bf16[320,512]{1,0:T(8,128)(2,1)S(1)} %get-tuple-element.68), channel_id=1, source_target_pairs={{0,3},{1,0},{2,1},{3,2},{4,7},{5,4},{6,5},{7,6},{8,11},{9,8},{10,9... | collective-permute-start | bytes 983048 | tf_op jit(solution)/shard_map/ppermute | solution.py:103
  110.3 20.9 %collective-permute-start.6 = (bf16[320,1024]{1,0:T(8,128)(2,1)S(1)}, bf16[320,1024]{1,0:T(8,128)(2,1)S(1)}, u32[]{:S(2)}, u32[]{:S(2)}) collective-permute-start(bf16[320,1024]{1,0:T(8,128)(2,1)S(1)} %third.5.refs_4_.refs_0_), channel_id=1, source_target_pairs={{0,4},{4,0},{1,5},{5,1},{2,6},{6,2},{3,7},{7,3},{8,12},{12,8},{9,1... | collective-permute-start | bytes 1966088 | tf_op jit(solution)/shard_map/ppermute | solution.py:103
  116.9 14.2 %collective-permute-start.10 = (bf16[320,512]{1,0:T(8,128)(2,1)S(1)}, bf16[320,512]{1,0:T(8,128)(2,1)S(1)}, u32[]{:S(2)}, u32[]{:S(2)}) collective-permute-start(bf16[320,512]{1,0:T(8,128)(2,1)S(1)} %get-tuple-element.73), channel_id=1, source_target_pairs={{0,3},{1,0},{2,1},{3,2},{4,7},{5,4},{6,5},{7,6},{8,11},{9,8},{10,9... | collective-permute-start | bytes 983048 | tf_op jit(solution)/shard_map/ppermute | solution.py:103
  117.3 13.9 %collective-permute-start.9 = (bf16[320,512]{1,0:T(8,128)(2,1)S(1)}, bf16[320,512]{1,0:T(8,128)(2,1)S(1)}, u32[]{:S(2)}, u32[]{:S(2)}) collective-permute-start(bf16[320,512]{1,0:T(8,128)(2,1)S(1)} %get-tuple-element.71), channel_id=1, source_target_pairs={{0,1},{1,2},{2,3},{3,0},{4,5},{5,6},{6,7},{7,4},{8,9},{9,10},{10,1... | collective-permute-start | bytes 983048 | tf_op jit(solution)/shard_map/ppermute | solution.py:103
  120.0 10.9 %collective-permute-start.12 = (bf16[160,512]{1,0:T(8,128)(2,1)S(1)}, bf16[160,512]{1,0:T(8,128)(2,1)S(1)}, u32[]{:S(2)}, u32[]{:S(2)}) collective-permute-start(bf16[160,512]{1,0:T(8,128)(2,1)S(1)} %get-tuple-element.69.refs_3_), channel_id=1, source_target_pairs={{0,3},{1,0},{2,1},{3,2},{4,7},{5,4},{6,5},{7,6},{8,11},{9,8},{10,9... | collective-permute-start | bytes 491528 | tf_op jit(solution)/shard_map/ppermute | solution.py:103
  132.4 14.8 %collective-permute-start.13 = (bf16[160,1024]{1,0:T(8,128)(2,1)S(1)}, bf16[160,1024]{1,0:T(8,128)(2,1)S(1)}, u32[]{:S(2)}, u32[]{:S(2)}) collective-permute-start(bf16[160,1024]{1,0:T(8,128)(2,1)S(1)} %get-tuple-element.77), channel_id=1, source_target_pairs={{0,1},{1,2},{2,3},{3,0},{4,5},{5,6},{6,7},{7,4},{8,9},{9,10},{10,1... | collective-permute-start | bytes 983048 | tf_op jit(solution)/shard_map/ppermute | solution.py:103
  134.9 12.4 %collective-permute-start.14 = (bf16[160,1024]{1,0:T(8,128)(2,1)S(1)}, bf16[160,1024]{1,0:T(8,128)(2,1)S(1)}, u32[]{:S(2)}, u32[]{:S(2)}) collective-permute-start(bf16[160,1024]{1,0:T(8,128)(2,1)S(1)} %get-tuple-element.78.refs_5_), channel_id=1, source_target_pairs={{0,3},{1,0},{2,1},{3,2},{4,7},{5,4},{6,5},{7,6},{8,11},{9,8},{10,9... | collective-permute-start | bytes 983048 | tf_op jit(solution)/shard_map/ppermute | solution.py:103
  134.9 13.1 %collective-permute-start.19 = (bf16[320,512]{1,0:T(8,128)(2,1)S(1)}, bf16[320,512]{1,0:T(8,128)(2,1)S(1)}, u32[]{:S(2)}, u32[]{:S(2)}) collective-permute-start(bf16[320,512]{1,0:T(8,128)(2,1)S(1)} %third.6.refs_5_.refs_2_), channel_id=1, source_target_pairs={{0,4},{4,0},{1,5},{5,1},{2,6},{6,2},{3,7},{7,3},{8,12},{12,8},{9,1... | collective-permute-start | bytes 983048 | tf_op jit(solution)/shard_map/ppermute | solution.py:103
  148.5 13.5 %collective-permute-start.20 = (bf16[320,1024]{1,0:T(8,128)(2,1)S(1)}, bf16[320,1024]{1,0:T(8,128)(2,1)S(1)}, u32[]{:S(2)}, u32[]{:S(2)}) collective-permute-start(bf16[320,1024]{1,0:T(8,128)(2,1)S(1)} %slope.1.refs_2_), channel_id=1, source_target_pairs={{0,1},{1,2},{2,3},{3,0},{4,5},{5,6},{6,7},{7,4},{8,9},{9,10},{10,1... | collective-permute-start | bytes 1966088 | tf_op jit(solution)/shard_map/ppermute | solution.py:103
  148.9 14.7 %collective-permute-start.21 = (bf16[320,1024]{1,0:T(8,128)(2,1)S(1)}, bf16[320,1024]{1,0:T(8,128)(2,1)S(1)}, u32[]{:S(2)}, u32[]{:S(2)}) collective-permute-start(bf16[320,1024]{1,0:T(8,128)(2,1)S(1)} %slope.1.refs_2_), channel_id=1, source_target_pairs={{0,3},{1,0},{2,1},{3,2},{4,7},{5,4},{6,5},{7,6},{8,11},{9,8},{10,9... | collective-permute-start | bytes 1966088 | tf_op jit(solution)/shard_map/ppermute | solution.py:103
  150.0 19.9 %collective-permute-start.17 = (bf16[320,1024]{1,0:T(8,128)(2,1)S(1)}, bf16[320,1024]{1,0:T(8,128)(2,1)S(1)}, u32[]{:S(2)}, u32[]{:S(2)}) collective-permute-start(bf16[320,1024]{1,0:T(8,128)(2,1)S(1)} %third.8.refs_4_.refs_2_), channel_id=1, source_target_pairs={{0,4},{4,0},{1,5},{5,1},{2,6},{6,2},{3,7},{7,3},{8,12},{12,8},{9,1... | collective-permute-start | bytes 1966088 | tf_op jit(solution)/shard_map/ppermute | solution.py:103
  150.0 19.9 %collective-permute-start.18 = (bf16[320,512]{1,0:T(8,128)(2,1)S(1)}, bf16[320,512]{1,0:T(8,128)(2,1)S(1)}, u32[]{:S(2)}, u32[]{:S(2)}) collective-permute-start(bf16[320,512]{1,0:T(8,128)(2,1)S(1)} %third.7.refs_5_.refs_4_), channel_id=1, source_target_pairs={{0,4},{4,0},{1,5},{5,1},{2,6},{6,2},{3,7},{7,3},{8,12},{12,8},{9,1... | collective-permute-start | bytes 983048 | tf_op jit(solution)/shard_map/ppermute | solution.py:103
  163.8 19.6 %collective-permute-start.24 = (bf16[160,1024]{1,0:T(8,128)(2,1)S(1)}, bf16[160,1024]{1,0:T(8,128)(2,1)S(1)}, u32[]{:S(2)}, u32[]{:S(2)}) collective-permute-start(bf16[160,1024]{1,0:T(8,128)(2,1)S(1)} %get-tuple-element.81), channel_id=1, source_target_pairs={{0,1},{1,2},{2,3},{3,0},{4,5},{5,6},{6,7},{7,4},{8,9},{9,10},{10,1... | collective-permute-start | bytes 983048 | tf_op jit(solution)/shard_map/ppermute | solution.py:103
  164.2 19.2 %collective-permute-start.25 = (bf16[160,1024]{1,0:T(8,128)(2,1)S(1)}, bf16[160,1024]{1,0:T(8,128)(2,1)S(1)}, u32[]{:S(2)}, u32[]{:S(2)}) collective-permute-start(bf16[160,1024]{1,0:T(8,128)(2,1)S(1)} %get-tuple-element.80.refs_6_), channel_id=1, source_target_pairs={{0,3},{1,0},{2,1},{3,2},{4,7},{5,4},{6,5},{7,6},{8,11},{9,8},{10,9... | collective-permute-start | bytes 983048 | tf_op jit(solution)/shard_map/ppermute | solution.py:103
  171.0 29.0 %collective-permute-start.22 = (bf16[320,2048]{1,0:T(8,128)(2,1)S(1)}, bf16[320,2048]{1,0:T(8,128)(2,1)}, u32[]{:S(2)}, u32[]{:S(2)}) collective-permute-start(bf16[320,2048]{1,0:T(8,128)(2,1)S(1)} %both.1.refs_9_.refs_1_.refs_2_), channel_id=1, source_target_pairs={{0,3},{1,0},{2,1},{3,2},{4,7},{5,4},{6,5},{7,6},{8,11},{9,8},{10,9... | collective-permute-start | bytes 3932168 | tf_op jit(solution)/shard_map/ppermute | solution.py:103
  171.3 35.9 %collective-permute-start.23 = (bf16[320,2048]{1,0:T(8,128)(2,1)S(1)}, bf16[320,2048]{1,0:T(8,128)(2,1)}, u32[]{:S(2)}, u32[]{:S(2)}) collective-permute-start(bf16[320,2048]{1,0:T(8,128)(2,1)S(1)} %both.1.refs_9_.refs_1_.refs_2_), channel_id=1, source_target_pairs={{0,1},{1,2},{2,3},{3,0},{4,5},{5,6},{6,7},{7,4},{8,9},{9,10},{10,1... | collective-permute-start | bytes 3932168 | tf_op jit(solution)/shard_map/ppermute | solution.py:103
  188.5 52.7 %all-to-all-start.1 = ((bf16[32,112,128]{2,1,0:T(8,128)(2,1)}), bf16[32,112,128]{2,1,0:T(8,128)(2,1)}, u32[]{:S(2)}, u32[]{:S(2)}) async-start(bf16[32,112,128]{2,1,0:T(8,128)(2,1)} %bitcast.28), calls=%async_computation.1 | async-start | bytes 1835008 | tf_op jit(solution)/shard_map/all_to_all | solution.py:107
  211.5 11.9 %collective-permute-start.26 = (bf16[160,2048]{1,0:T(8,128)(2,1)S(1)}, bf16[160,2048]{1,0:T(8,128)(2,1)S(1)}, u32[]{:S(2)}, u32[]{:S(2)}) collective-permute-start(bf16[160,2048]{1,0:T(8,128)(2,1)S(1)} %get-tuple-element.82), channel_id=1, source_target_pairs={{0,1},{1,2},{2,3},{3,0},{4,5},{5,6},{6,7},{7,4},{8,9},{9,10},{10,1... | collective-permute-start | bytes 1966088 | tf_op jit(solution)/shard_map/ppermute | solution.py:103
  214.9 11.7 %collective-permute-start.27 = (bf16[160,2048]{1,0:T(8,128)(2,1)S(1)}, bf16[160,2048]{1,0:T(8,128)(2,1)S(1)}, u32[]{:S(2)}, u32[]{:S(2)}) collective-permute-start(bf16[160,2048]{1,0:T(8,128)(2,1)S(1)} %get-tuple-element.83.refs_9_), channel_id=1, source_target_pairs={{0,3},{1,0},{2,1},{3,2},{4,7},{5,4},{6,5},{7,6},{8,11},{9,8},{10,9... | collective-permute-start | bytes 1966088 | tf_op jit(solution)/shard_map/ppermute | solution.py:103
  244.4 69.7 %all-to-all-start.2 = ((bf16[32,224,128]{2,1,0:T(8,128)(2,1)}), bf16[32,224,128]{2,1,0:T(8,128)(2,1)S(1)}, u32[]{:S(2)}, u32[]{:S(2)}) async-start(bf16[32,224,128]{2,1,0:T(8,128)(2,1)} %merge.1.refs_2_), calls=%async_computation.2 | async-start | bytes 3670016 | tf_op jit(solution)/shard_map/all_to_all | solution.py:107
  262.2 20.8 %collective-permute-start.29 = (bf16[512,512]{1,0:T(8,128)(2,1)S(1)}, bf16[512,512]{1,0:T(8,128)(2,1)S(1)}, u32[]{:S(2)}, u32[]{:S(2)}) collective-permute-start(bf16[512,512]{1,0:T(8,128)(2,1)S(1)} %get-tuple-element.89), channel_id=1, source_target_pairs={{0,64},{64,128},{128,192},{192,0},{1,65},{65,129},{129,193},{193,1... | collective-permute-start | bytes 1572872 | tf_op jit(solution)/shard_map/ppermute | solution.py:103
  263.7 19.6 %collective-permute-start.30 = (bf16[512,512]{1,0:T(8,128)(2,1)S(1)}, bf16[512,512]{1,0:T(8,128)(2,1)S(1)}, u32[]{:S(2)}, u32[]{:S(2)}) collective-permute-start(bf16[512,512]{1,0:T(8,128)(2,1)S(1)} %get-tuple-element.91), channel_id=1, source_target_pairs={{0,192},{64,0},{128,64},{192,128},{1,193},{65,1},{129,65},{193,129... | collective-permute-start | bytes 1572872 | tf_op jit(solution)/shard_map/ppermute | solution.py:103
  294.4 17.3 %collective-permute-start.33 = (bf16[128,512]{1,0:T(8,128)(2,1)S(1)}, bf16[128,512]{1,0:T(8,128)(2,1)S(1)}, u32[]{:S(2)}, u32[]{:S(2)}) collective-permute-start(bf16[128,512]{1,0:T(8,128)(2,1)S(1)} %get-tuple-element.95), channel_id=1, source_target_pairs={{0,16},{16,32},{32,48},{48,0},{1,17},{17,33},{33,49},{49,1},{2,18}... | collective-permute-start | bytes 393224 | tf_op jit(solution)/shard_map/ppermute | solution.py:103
  315.8 39.7 %all-to-all-start.3 = ((bf16[32,112,128]{2,1,0:T(8,128)(2,1)}), bf16[32,112,128]{2,1,0:T(8,128)(2,1)S(1)}, u32[]{:S(2)}, u32[]{:S(2)}) async-start(bf16[32,112,128]{2,1,0:T(8,128)(2,1)} %reorder.1.refs_2_), calls=%async_computation.3 | async-start | bytes 1835008 | tf_op jit(solution)/shard_map/all_to_all | solution.py:107
  (41 other events, 501.8 us)
Sparse Core Ops, SparseCore 0:
  12.1 75.3 all-gather.1

commit v3 on v2

--- a/solution.py
+++ b/solution.py
@@ -272,7 +272,7 @@
 
     def second(self):
         height, columns = self.own.shape
-        block = 256 if columns % 256 == 0 else columns
+        block = 1024 if columns % 1024 == 0 else columns
         first = pl.BlockSpec((height // 2, block), lambda j: (0, j))
         last = pl.BlockSpec((height // 2, block), lambda j: (1, j))
         low, high = self.run(
@@ -584,16 +584,16 @@
     routed_grads = routed_grads.reshape(8, block_rows, width)
     back_one = back_sum(one, waits=[pre_two.got_left, pre_two.got_right])
     pre_one.cross()
+    pre_two.second()
     back_one.second()
-    back_two = back_sum(two)
-    back_one.cross()
-    back_two.second(waits=[pre_one.other])
-    pre_two.second()
-    back_two.cross()
+    back_two = back_sum(two, waits=[pre_two.low, pre_two.high])
+    back_one.cross(waits=[pre_one.other])
     pre_two.cross()
+    back_two.second()
     grad_one = RowGather(
         run, activation(run, slope_kernel, "slope", [pre_one, back_one], pre_one.columns)
     )
+    back_two.cross(waits=[pre_two.other])
     grad_one.second()
     sums = [pre_one, pre_two, back_two]
     both = RowGather(

time: 370 us -> 362 us (0.978)
  the two profiles are of different devices: /device:TPU:39 before, /device:TPU:1 now
where the time goes in v3:
time: 362 us; the launch traced here: 356 us
  waiting for transfers between devices  146 us (40%)
  starting transfers between devices  130 us (36%)
  Pallas kernels  49.1 us (14%)
  between operations  14.8 us (4%)
  local copies, waits for them, and re-layouts  12.5 us (3%)
    ppermute x36, waiting for transfers between devices, shift(): return lax.ppermute(value, axis, [(i, (i + by) % n) for i in range(n)])  80.9 us
    ppermute x36, starting transfers between devices, shift(): return lax.ppermute(value, axis, [(i, (i + by) % n) for i in range(n)])  73 us
    all_to_all x4, waiting for transfers between devices, exchange(): lax.all_to_all(value, expert_axes, split_axis=0, concat_axis=0, tiled=True)  61 us
    all_to_all x4, starting transfers between devices, exchange(): lax.all_to_all(value, expert_axes, split_axis=0, concat_axis=0, tiled=True)  57.3 us
    pallas_call x29, Pallas kernels, __call__(): pl.pallas_call(body, out_shape=out_shape, grid_spec=pltpu.PrefetchScalarG...  49.1 us
    unnamed x65, local copies, waits for them, and re-layouts  10.5 us
  transfers between devices with their start and end apart: 41, of which 20 were waited for; matrix products, arithmetic and copies ran while one was open for 1% of the time, Pallas kernels for 11%

profile of v3, /device:TPU:1, one launch (start us, length us, event | category | flops | bytes accessed | tf_op | source)
XLA Modules:
  0.0 355.7 jit_solution(11050044510589333970)
XLA Ops:
  15.4 12.8 %all-to-all-start = ((bf16[32,40,448]{2,1,0:T(8,128)(2,1)}), bf16[32,40,448]{2,1,0:T(8,128)(2,1)S(1)}, u32[]{:S(2)}, u32[]{:S(2)}) async-start(bf16[32,40,448]{2,1,0:T(8,128)(2,1)} %bitcast.19), calls=%async_computation | async-start | bytes 2621440 | tf_op jit(solution)/shard_map/all_to_all | solution.py:107
  28.3 35.7 %all-to-all-done = bf16[32,40,448]{2,1,0:T(8,128)(2,1)S(1)} async-done(((bf16[32,40,448]{2,1,0:T(8,128)(2,1)}), bf16[32,40,448]{2,1,0:T(8,128)(2,1)S(1)}, u32[]{:S(2)}, u32[]{:S(2)}) %all-to-all-start) | async-done | bytes 1146912 | tf_op jit(solution)/shard_map/all_to_all | solution.py:107
  64.0 3.1 project.4
  70.1 3.5 project.5
  76.4 4.9 %collective-permute-done.refs_1_.refs_4_ = bf16[320,1024]{1,0:T(8,128)(2,1)S(1)} collective-permute-done((bf16[320,1024]{1,0:T(8,128)(2,1)S(1)}, bf16[320,1024]{1,0:T(8,128)(2,1)S(1)}, u32[]{:S(2)}, u32[]{:S(2)}) %collective-permute-start) | collective-permute-done | bytes 655392 | tf_op jit(solution)/shard_map/ppermute | solution.py:103
  86.0 3.8 %all-gather.2.cloned.1.call-done.refs_1_ = bf16[4096,512]{1,0:T(8,128)(2,1)} async-done(((bf16[128,512]{1,0:T(8,128)(2,1)}), bf16[4096,512]{1,0:T(8,128)(2,1)}) %all-gather.2.cloned.1.call-update) | async-done | bytes 4194320 | tf_op jit(solution)/shard_map/all_gather | solution.py:513
  98.0 4.3 %collective-permute-done.2.refs_1_ = bf16[160,1024]{1,0:T(8,128)(2,1)} collective-permute-done((bf16[160,1024]{1,0:T(8,128)(2,1)}, bf16[160,1024]{1,0:T(8,128)(2,1)}, u32[]{:S(2)}, u32[]{:S(2)}) %collective-permute-start.2) | collective-permute-done | bytes 327712 | tf_op jit(solution)/shard_map/ppermute | solution.py:103
  104.5 8.0 %collective-permute-start.6 = (bf16[320,1024]{1,0:T(8,128)(2,1)S(1)}, bf16[320,1024]{1,0:T(8,128)(2,1)S(1)}, u32[]{:S(2)}, u32[]{:S(2)}) collective-permute-start(bf16[320,1024]{1,0:T(8,128)(2,1)S(1)} %third.5.refs_4_.refs_0_), channel_id=1, source_target_pairs={{0,4},{4,0},{1,5},{5,1},{2,6},{6,2},{3,7},{7,3},{8,12},{12,8},{9,1... | collective-permute-start | bytes 1966088 | tf_op jit(solution)/shard_map/ppermute | solution.py:103
  115.9 3.0 collective-permute-start.8
  121.7 3.1 collective-permute-done.9.refs_1_.refs_4_
  127.7 4.1 %collective-permute-done.7.refs_3_.refs_1_ = bf16[160,1024]{1,0:T(8,128)(2,1)S(1)} collective-permute-done((bf16[160,1024]{1,0:T(8,128)(2,1)S(1)}, bf16[160,1024]{1,0:T(8,128)(2,1)S(1)}, u32[]{:S(2)}, u32[]{:S(2)}) %collective-permute-start.7) | collective-permute-done | bytes 327712 | tf_op jit(solution)/shard_map/ppermute | solution.py:103
  148.9 7.0 %collective-permute-done.16.refs_1_ = bf16[160,512]{1,0:T(8,128)(2,1)S(1)} collective-permute-done((bf16[160,512]{1,0:T(8,128)(2,1)S(1)}, bf16[160,512]{1,0:T(8,128)(2,1)S(1)}, u32[]{:S(2)}, u32[]{:S(2)}) %collective-permute-start.16) | collective-permute-done | bytes 163872 | tf_op jit(solution)/shard_map/ppermute | solution.py:103
  160.4 3.6 %collective-permute-done.19.refs_5_ = bf16[320,512]{1,0:T(8,128)(2,1)S(1)} collective-permute-done((bf16[320,512]{1,0:T(8,128)(2,1)S(1)}, bf16[320,512]{1,0:T(8,128)(2,1)S(1)}, u32[]{:S(2)}, u32[]{:S(2)}) %collective-permute-start.19) | collective-permute-done | bytes 327712 | tf_op jit(solution)/shard_map/ppermute | solution.py:103
  166.3 9.8 %collective-permute-start.23 = (bf16[320,2048]{1,0:T(8,128)(2,1)S(1)}, bf16[320,2048]{1,0:T(8,128)(2,1)}, u32[]{:S(2)}, u32[]{:S(2)}) collective-permute-start(bf16[320,2048]{1,0:T(8,128)(2,1)S(1)} %both.1.refs_9_.refs_1_.refs_2_), channel_id=1, source_target_pairs={{0,1},{1,2},{2,3},{3,0},{4,5},{5,6},{6,7},{7,4},{8,9},{9,10},{10,1... | collective-permute-start | bytes 3932168 | tf_op jit(solution)/shard_map/ppermute | solution.py:103
  176.1 5.1 %adam.2.refs_2_ = bf16[8,448,128]{2,1,0:T(8,128)(2,1)} custom-call(s32[41]{0:T(128)S(1)} %copy-done.24, bf16[8,160,448]{2,1,0:T(8,128)(2,1)S(1)} %bitcast.51, bf16[320,1024]{1,0:T(8,128)(2,1)S(1)} %slope.1.refs_6_.refs_2_, bf16[320,1024]{1,0:T(8,128)(2,1)S(1)} %collective-permute-done.21.refs_1_.refs_3_, ...), custom_call_target="tpu_custom_call" | custom-call | flops 1174405120 | bytes 8000000 | tf_op jit(solution)/shard_map/adam/pallas_call | solution.py:80
  181.1 20.3 %all-to-all-start.1 = ((bf16[32,112,128]{2,1,0:T(8,128)(2,1)}), bf16[32,112,128]{2,1,0:T(8,128)(2,1)}, u32[]{:S(2)}, u32[]{:S(2)}) async-start(bf16[32,112,128]{2,1,0:T(8,128)(2,1)} %bitcast.28), calls=%async_computation.1 | async-start | bytes 1835008 | tf_op jit(solution)/shard_map/all_to_all | solution.py:107
  203.2 3.0 collective-permute-start.27
  206.8 8.9 %collective-permute-done.26.refs_3_.refs_4_ = bf16[160,2048]{1,0:T(8,128)(2,1)S(1)} collective-permute-done((bf16[160,2048]{1,0:T(8,128)(2,1)S(1)}, bf16[160,2048]{1,0:T(8,128)(2,1)S(1)}, u32[]{:S(2)}, u32[]{:S(2)}) %collective-permute-start.26) | collective-permute-done | bytes 655392 | tf_op jit(solution)/shard_map/ppermute | solution.py:103
  215.8 6.8 %outputs.1 = (bf16[2048,512]{1,0:T(8,128)(2,1)S(1)}, bf16[2048,512]{1,0:T(8,128)(2,1)S(1)}) custom-call(s32[41]{0:T(128)S(1)} %copy-done.25, bf16[320,2048]{1,0:T(8,128)(2,1)S(1)} %both.1.refs_9_.refs_1_.refs_2_, bf16[320,2048]{1,0:T(8,128)(2,1)} %collective-permute-done.22.refs_1_.refs_2_.refs_3_, ...), custom_call_target="tpu_custom_call" | custom-call | flops 1174405120 | bytes 5000000 | tf_op jit(solution)/shard_map/outputs/pallas_call | solution.py:80
  223.9 5.1 %adam.3.refs_3_ = bf16[8,448,128]{2,1,0:T(8,128)(2,1)S(1)} custom-call(s32[41]{0:T(128)S(1)} %copy-done.25, bf16[8,160,448]{2,1,0:T(8,128)(2,1)S(1)} %bitcast.52, bf16[320,2048]{1,0:T(8,128)(2,1)S(1)} %both.1.refs_9_.refs_1_.refs_2_, bf16[320,2048]{1,0:T(8,128)(2,1)} %collective-permute-done.22.refs_1_.refs_2_.refs_3_, ...), custom_call_target="tpu_custom_call" | custom-call | flops 1174405120 | bytes 8000000 | tf_op jit(solution)/shard_map/adam/pallas_call | solution.py:80
  230.4 3.2 merge.1.refs_2_
  233.6 15.4 %all-to-all-start.2 = ((bf16[32,224,128]{2,1,0:T(8,128)(2,1)}), bf16[32,224,128]{2,1,0:T(8,128)(2,1)S(1)}, u32[]{:S(2)}, u32[]{:S(2)}) async-start(bf16[32,224,128]{2,1,0:T(8,128)(2,1)} %merge.1.refs_2_), calls=%async_computation.2 | async-start | bytes 3670016 | tf_op jit(solution)/shard_map/all_to_all | solution.py:107
  249.3 4.1 %collective-permute-done.28.refs_1_ = bf16[2048,512]{1,0:T(8,128)(2,1)S(1)} collective-permute-done((bf16[2048,512]{1,0:T(8,128)(2,1)}, bf16[2048,512]{1,0:T(8,128)(2,1)S(1)}, u32[]{:S(2)}, u32[]{:S(2)}) %collective-permute-start.28) | collective-permute-done | bytes 2097184 | tf_op jit(solution)/shard_map/ppermute | solution.py:103
  258.4 14.9 %collective-permute-done.29.refs_1_.refs_4_ = bf16[512,512]{1,0:T(8,128)(2,1)S(1)} collective-permute-done((bf16[512,512]{1,0:T(8,128)(2,1)S(1)}, bf16[512,512]{1,0:T(8,128)(2,1)S(1)}, u32[]{:S(2)}, u32[]{:S(2)}) %collective-permute-start.29) | collective-permute-done | bytes 524320 | tf_op jit(solution)/shard_map/ppermute | solution.py:103
  276.9 7.5 %collective-permute-done.31.refs_1_ = bf16[256,512]{1,0:T(8,128)(2,1)S(1)} collective-permute-done((bf16[256,512]{1,0:T(8,128)(2,1)S(1)}, bf16[256,512]{1,0:T(8,128)(2,1)S(1)}, u32[]{:S(2)}, u32[]{:S(2)}) %collective-permute-start.31) | collective-permute-done | bytes 262176 | tf_op jit(solution)/shard_map/ppermute | solution.py:103
  284.4 3.7 %collective-permute-done.32.refs_3_ = bf16[256,512]{1,0:T(8,128)(2,1)S(1)} collective-permute-done((bf16[256,512]{1,0:T(8,128)(2,1)S(1)}, bf16[256,512]{1,0:T(8,128)(2,1)S(1)}, u32[]{:S(2)}, u32[]{:S(2)}) %collective-permute-start.32) | collective-permute-done | bytes 262176 | tf_op jit(solution)/shard_map/ppermute | solution.py:103
  289.8 8.8 %collective-permute-start.34 = (bf16[128,512]{1,0:T(8,128)(2,1)S(1)}, bf16[128,512]{1,0:T(8,128)(2,1)S(1)}, u32[]{:S(2)}, u32[]{:S(2)}) collective-permute-start(bf16[128,512]{1,0:T(8,128)(2,1)S(1)} %get-tuple-element.96), channel_id=1, source_target_pairs={{0,32},{16,48},{32,0},{48,16},{1,33},{17,49},{33,1},{49,17},{2,34}... | collective-permute-start | bytes 393224 | tf_op jit(solution)/shard_map/ppermute | solution.py:103
  298.6 3.5 collective-permute-start.35
  302.1 4.8 %collective-permute-done.34.refs_2_ = bf16[128,512]{1,0:T(8,128)(2,1)S(1)} collective-permute-done((bf16[128,512]{1,0:T(8,128)(2,1)S(1)}, bf16[128,512]{1,0:T(8,128)(2,1)S(1)}, u32[]{:S(2)}, u32[]{:S(2)}) %collective-permute-start.34) | collective-permute-done | bytes 131104 | tf_op jit(solution)/shard_map/ppermute | solution.py:103
  306.8 3.3 collective-permute-done.35.refs_3_
  311.9 8.8 %all-to-all-start.3 = ((bf16[32,112,128]{2,1,0:T(8,128)(2,1)}), bf16[32,112,128]{2,1,0:T(8,128)(2,1)S(1)}, u32[]{:S(2)}, u32[]{:S(2)}) async-start(bf16[32,112,128]{2,1,0:T(8,128)(2,1)} %reorder.1.refs_2_), calls=%async_computation.3 | async-start | bytes 1835008 | tf_op jit(solution)/shard_map/all_to_all | solution.py:107
  321.6 25.3 %all-to-all-done.3.refs_1_ = bf16[32,112,128]{2,1,0:T(8,128)(2,1)S(1)} async-done(((bf16[32,112,128]{2,1,0:T(8,128)(2,1)}), bf16[32,112,128]{2,1,0:T(8,128)(2,1)S(1)}, u32[]{:S(2)}, u32[]{:S(2)}) %all-to-all-start.3) | async-done | bytes 917536 | tf_op jit(solution)/shard_map/all_to_all | solution.py:107
  (156 shorter events, 81.8 us)
Async XLA Ops:
  7.2 82.7 %all-gather.2.cloned.1.call-start = ((), (), s32[]{:S(2)}) async-start(), calls=%async_computation.4 | async-start | bytes 4325376 | tf_op jit(solution)/shard_map/all_gather | solution.py:513
  15.4 48.6 %all-to-all-start = ((bf16[32,40,448]{2,1,0:T(8,128)(2,1)}), bf16[32,40,448]{2,1,0:T(8,128)(2,1)S(1)}, u32[]{:S(2)}, u32[]{:S(2)}) async-start(bf16[32,40,448]{2,1,0:T(8,128)(2,1)} %bitcast.19), calls=%async_computation | async-start | bytes 2621440 | tf_op jit(solution)/shard_map/all_to_all | solution.py:107
  67.2 14.1 %collective-permute-start = (bf16[320,1024]{1,0:T(8,128)(2,1)S(1)}, bf16[320,1024]{1,0:T(8,128)(2,1)S(1)}, u32[]{:S(2)}, u32[]{:S(2)}) collective-permute-start(bf16[320,1024]{1,0:T(8,128)(2,1)S(1)} %get-tuple-element.52), channel_id=1, source_target_pairs={{0,1},{1,2},{2,3},{3,0},{4,5},{5,6},{6,7},{7,4},{8,9},{9,10},{10,1... | collective-permute-start | bytes 1966088 | tf_op jit(solution)/shard_map/ppermute | solution.py:103
  68.4 12.8 %collective-permute-start.1 = (bf16[320,1024]{1,0:T(8,128)(2,1)S(1)}, bf16[320,1024]{1,0:T(8,128)(2,1)S(1)}, u32[]{:S(2)}, u32[]{:S(2)}) collective-permute-start(bf16[320,1024]{1,0:T(8,128)(2,1)S(1)} %get-tuple-element.54), channel_id=1, source_target_pairs={{0,3},{1,0},{2,1},{3,2},{4,7},{5,4},{6,5},{7,6},{8,11},{9,8},{10,9... | collective-permute-start | bytes 1966088 | tf_op jit(solution)/shard_map/ppermute | solution.py:103
  73.6 22.6 %collective-permute-start.4 = (bf16[320,1024]{1,0:T(8,128)(2,1)}, bf16[320,1024]{1,0:T(8,128)(2,1)S(1)}, u32[]{:S(2)}, u32[]{:S(2)}) collective-permute-start(bf16[320,1024]{1,0:T(8,128)(2,1)} %get-tuple-element.59), channel_id=1, source_target_pairs={{0,1},{1,2},{2,3},{3,0},{4,5},{5,6},{6,7},{7,4},{8,9},{9,10},{10,1... | collective-permute-start | bytes 1966088 | tf_op jit(solution)/shard_map/ppermute | solution.py:103
  73.7 22.5 %collective-permute-start.5 = (bf16[320,1024]{1,0:T(8,128)(2,1)}, bf16[320,1024]{1,0:T(8,128)(2,1)S(1)}, u32[]{:S(2)}, u32[]{:S(2)}) collective-permute-start(bf16[320,1024]{1,0:T(8,128)(2,1)} %get-tuple-element.60), channel_id=1, source_target_pairs={{0,3},{1,0},{2,1},{3,2},{4,7},{5,4},{6,5},{7,6},{8,11},{9,8},{10,9... | collective-permute-start | bytes 1966088 | tf_op jit(solution)/shard_map/ppermute | solution.py:103
  83.2 19.0 %collective-permute-start.2 = (bf16[160,1024]{1,0:T(8,128)(2,1)}, bf16[160,1024]{1,0:T(8,128)(2,1)}, u32[]{:S(2)}, u32[]{:S(2)}) collective-permute-start(bf16[160,1024]{1,0:T(8,128)(2,1)} %get-tuple-element.56), channel_id=1, source_target_pairs={{0,1},{1,2},{2,3},{3,0},{4,5},{5,6},{6,7},{7,4},{8,9},{9,10},{10,1... | collective-permute-start | bytes 983048 | tf_op jit(solution)/shard_map/ppermute | solution.py:103
  84.2 18.1 %collective-permute-start.3 = (bf16[160,1024]{1,0:T(8,128)(2,1)}, bf16[160,1024]{1,0:T(8,128)(2,1)}, u32[]{:S(2)}, u32[]{:S(2)}) collective-permute-start(bf16[160,1024]{1,0:T(8,128)(2,1)} %get-tuple-element.57.refs_2_), channel_id=1, source_target_pairs={{0,3},{1,0},{2,1},{3,2},{4,7},{5,4},{6,5},{7,6},{8,11},{9,8},{10,9... | collective-permute-start | bytes 983048 | tf_op jit(solution)/shard_map/ppermute | solution.py:103
  104.5 31.8 %collective-permute-start.6 = (bf16[320,1024]{1,0:T(8,128)(2,1)S(1)}, bf16[320,1024]{1,0:T(8,128)(2,1)S(1)}, u32[]{:S(2)}, u32[]{:S(2)}) collective-permute-start(bf16[320,1024]{1,0:T(8,128)(2,1)S(1)} %third.5.refs_4_.refs_0_), channel_id=1, source_target_pairs={{0,4},{4,0},{1,5},{5,1},{2,6},{6,2},{3,7},{7,3},{8,12},{12,8},{9,1... | collective-permute-start | bytes 1966088 | tf_op jit(solution)/shard_map/ppermute | solution.py:103
  115.8 16.0 %collective-permute-start.7 = (bf16[160,1024]{1,0:T(8,128)(2,1)S(1)}, bf16[160,1024]{1,0:T(8,128)(2,1)S(1)}, u32[]{:S(2)}, u32[]{:S(2)}) collective-permute-start(bf16[160,1024]{1,0:T(8,128)(2,1)S(1)} %get-tuple-element.65), channel_id=1, source_target_pairs={{0,1},{1,2},{2,3},{3,0},{4,5},{5,6},{6,7},{7,4},{8,9},{9,10},{10,1... | collective-permute-start | bytes 983048 | tf_op jit(solution)/shard_map/ppermute | solution.py:103
  115.9 15.9 %collective-permute-start.8 = (bf16[160,1024]{1,0:T(8,128)(2,1)S(1)}, bf16[160,1024]{1,0:T(8,128)(2,1)S(1)}, u32[]{:S(2)}, u32[]{:S(2)}) collective-permute-start(bf16[160,1024]{1,0:T(8,128)(2,1)S(1)} %get-tuple-element.66.refs_4_), channel_id=1, source_target_pairs={{0,3},{1,0},{2,1},{3,2},{4,7},{5,4},{6,5},{7,6},{8,11},{9,8},{10,9... | collective-permute-start | bytes 983048 | tf_op jit(solution)/shard_map/ppermute | solution.py:103
  125.0 11.3 %collective-permute-start.11 = (bf16[160,512]{1,0:T(8,128)(2,1)S(1)}, bf16[160,512]{1,0:T(8,128)(2,1)S(1)}, u32[]{:S(2)}, u32[]{:S(2)}) collective-permute-start(bf16[160,512]{1,0:T(8,128)(2,1)S(1)} %get-tuple-element.71), channel_id=1, source_target_pairs={{0,1},{1,2},{2,3},{3,0},{4,5},{5,6},{6,7},{7,4},{8,9},{9,10},{10,1... | collective-permute-start | bytes 491528 | tf_op jit(solution)/shard_map/ppermute | solution.py:103
  125.1 11.3 %collective-permute-start.12 = (bf16[160,512]{1,0:T(8,128)(2,1)S(1)}, bf16[160,512]{1,0:T(8,128)(2,1)S(1)}, u32[]{:S(2)}, u32[]{:S(2)}) collective-permute-start(bf16[160,512]{1,0:T(8,128)(2,1)S(1)} %get-tuple-element.72.refs_5_), channel_id=1, source_target_pairs={{0,3},{1,0},{2,1},{3,2},{4,7},{5,4},{6,5},{7,6},{8,11},{9,8},{10,9... | collective-permute-start | bytes 491528 | tf_op jit(solution)/shard_map/ppermute | solution.py:103
  137.8 18.3 %collective-permute-start.13 = (bf16[320,1024]{1,0:T(8,128)(2,1)S(1)}, bf16[320,1024]{1,0:T(8,128)(2,1)S(1)}, u32[]{:S(2)}, u32[]{:S(2)}) collective-permute-start(bf16[320,1024]{1,0:T(8,128)(2,1)S(1)} %third.7.refs_4_.refs_2_), channel_id=1, source_target_pairs={{0,4},{4,0},{1,5},{5,1},{2,6},{6,2},{3,7},{7,3},{8,12},{12,8},{9,1... | collective-permute-start | bytes 1966088 | tf_op jit(solution)/shard_map/ppermute | solution.py:103
  143.5 14.1 %collective-permute-start.20 = (bf16[320,1024]{1,0:T(8,128)(2,1)S(1)}, bf16[320,1024]{1,0:T(8,128)(2,1)S(1)}, u32[]{:S(2)}, u32[]{:S(2)}) collective-permute-start(bf16[320,1024]{1,0:T(8,128)(2,1)S(1)} %slope.1.refs_6_.refs_2_), channel_id=1, source_target_pairs={{0,1},{1,2},{2,3},{3,0},{4,5},{5,6},{6,7},{7,4},{8,9},{9,10},{10,1... | collective-permute-start | bytes 1966088 | tf_op jit(solution)/shard_map/ppermute | solution.py:103
  143.6 14.1 %collective-permute-start.21 = (bf16[320,1024]{1,0:T(8,128)(2,1)S(1)}, bf16[320,1024]{1,0:T(8,128)(2,1)S(1)}, u32[]{:S(2)}, u32[]{:S(2)}) collective-permute-start(bf16[320,1024]{1,0:T(8,128)(2,1)S(1)} %slope.1.refs_6_.refs_2_), channel_id=1, source_target_pairs={{0,3},{1,0},{2,1},{3,2},{4,7},{5,4},{6,5},{7,6},{8,11},{9,8},{10,9... | collective-permute-start | bytes 1966088 | tf_op jit(solution)/shard_map/ppermute | solution.py:103
  157.7 18.4 %collective-permute-start.24 = (bf16[160,1024]{1,0:T(8,128)(2,1)S(1)}, bf16[160,1024]{1,0:T(8,128)(2,1)S(1)}, u32[]{:S(2)}, u32[]{:S(2)}) collective-permute-start(bf16[160,1024]{1,0:T(8,128)(2,1)S(1)} %get-tuple-element.81), channel_id=1, source_target_pairs={{0,1},{1,2},{2,3},{3,0},{4,5},{5,6},{6,7},{7,4},{8,9},{9,10},{10,1... | collective-permute-start | bytes 983048 | tf_op jit(solution)/shard_map/ppermute | solution.py:103
  158.3 17.7 %collective-permute-start.25 = (bf16[160,1024]{1,0:T(8,128)(2,1)S(1)}, bf16[160,1024]{1,0:T(8,128)(2,1)S(1)}, u32[]{:S(2)}, u32[]{:S(2)}) collective-permute-start(bf16[160,1024]{1,0:T(8,128)(2,1)S(1)} %get-tuple-element.80.refs_6_), channel_id=1, source_target_pairs={{0,3},{1,0},{2,1},{3,2},{4,7},{5,4},{6,5},{7,6},{8,11},{9,8},{10,9... | collective-permute-start | bytes 983048 | tf_op jit(solution)/shard_map/ppermute | solution.py:103
  165.0 36.5 %collective-permute-start.22 = (bf16[320,2048]{1,0:T(8,128)(2,1)S(1)}, bf16[320,2048]{1,0:T(8,128)(2,1)}, u32[]{:S(2)}, u32[]{:S(2)}) collective-permute-start(bf16[320,2048]{1,0:T(8,128)(2,1)S(1)} %both.1.refs_9_.refs_1_.refs_2_), channel_id=1, source_target_pairs={{0,3},{1,0},{2,1},{3,2},{4,7},{5,4},{6,5},{7,6},{8,11},{9,8},{10,9... | collective-permute-start | bytes 3932168 | tf_op jit(solution)/shard_map/ppermute | solution.py:103
  166.3 35.2 %collective-permute-start.23 = (bf16[320,2048]{1,0:T(8,128)(2,1)S(1)}, bf16[320,2048]{1,0:T(8,128)(2,1)}, u32[]{:S(2)}, u32[]{:S(2)}) collective-permute-start(bf16[320,2048]{1,0:T(8,128)(2,1)S(1)} %both.1.refs_9_.refs_1_.refs_2_), channel_id=1, source_target_pairs={{0,1},{1,2},{2,3},{3,0},{4,5},{5,6},{6,7},{7,4},{8,9},{9,10},{10,1... | collective-permute-start | bytes 3932168 | tf_op jit(solution)/shard_map/ppermute | solution.py:103
  181.1 49.3 %all-to-all-start.1 = ((bf16[32,112,128]{2,1,0:T(8,128)(2,1)}), bf16[32,112,128]{2,1,0:T(8,128)(2,1)}, u32[]{:S(2)}, u32[]{:S(2)}) async-start(bf16[32,112,128]{2,1,0:T(8,128)(2,1)} %bitcast.28), calls=%async_computation.1 | async-start | bytes 1835008 | tf_op jit(solution)/shard_map/all_to_all | solution.py:107
  203.1 12.7 %collective-permute-start.26 = (bf16[160,2048]{1,0:T(8,128)(2,1)S(1)}, bf16[160,2048]{1,0:T(8,128)(2,1)S(1)}, u32[]{:S(2)}, u32[]{:S(2)}) collective-permute-start(bf16[160,2048]{1,0:T(8,128)(2,1)S(1)} %get-tuple-element.82), channel_id=1, source_target_pairs={{0,1},{1,2},{2,3},{3,0},{4,5},{5,6},{6,7},{7,4},{8,9},{9,10},{10,1... | collective-permute-start | bytes 1966088 | tf_op jit(solution)/shard_map/ppermute | solution.py:103
  203.2 12.6 %collective-permute-start.27 = (bf16[160,2048]{1,0:T(8,128)(2,1)S(1)}, bf16[160,2048]{1,0:T(8,128)(2,1)S(1)}, u32[]{:S(2)}, u32[]{:S(2)}) collective-permute-start(bf16[160,2048]{1,0:T(8,128)(2,1)S(1)} %get-tuple-element.83.refs_9_), channel_id=1, source_target_pairs={{0,3},{1,0},{2,1},{3,2},{4,7},{5,4},{6,5},{7,6},{8,11},{9,8},{10,9... | collective-permute-start | bytes 1966088 | tf_op jit(solution)/shard_map/ppermute | solution.py:103
  233.6 76.6 %all-to-all-start.2 = ((bf16[32,224,128]{2,1,0:T(8,128)(2,1)}), bf16[32,224,128]{2,1,0:T(8,128)(2,1)S(1)}, u32[]{:S(2)}, u32[]{:S(2)}) async-start(bf16[32,224,128]{2,1,0:T(8,128)(2,1)} %merge.1.refs_2_), calls=%async_computation.2 | async-start | bytes 3670016 | tf_op jit(solution)/shard_map/all_to_all | solution.py:107
  255.5 17.7 %collective-permute-start.29 = (bf16[512,512]{1,0:T(8,128)(2,1)S(1)}, bf16[512,512]{1,0:T(8,128)(2,1)S(1)}, u32[]{:S(2)}, u32[]{:S(2)}) collective-permute-start(bf16[512,512]{1,0:T(8,128)(2,1)S(1)} %get-tuple-element.89), channel_id=1, source_target_pairs={{0,64},{64,128},{128,192},{192,0},{1,65},{65,129},{129,193},{193,1... | collective-permute-start | bytes 1572872 | tf_op jit(solution)/shard_map/ppermute | solution.py:103
  257.0 16.3 %collective-permute-start.30 = (bf16[512,512]{1,0:T(8,128)(2,1)S(1)}, bf16[512,512]{1,0:T(8,128)(2,1)S(1)}, u32[]{:S(2)}, u32[]{:S(2)}) collective-permute-start(bf16[512,512]{1,0:T(8,128)(2,1)S(1)} %get-tuple-element.91), channel_id=1, source_target_pairs={{0,192},{64,0},{128,64},{192,128},{1,193},{65,1},{129,65},{193,129... | collective-permute-start | bytes 1572872 | tf_op jit(solution)/shard_map/ppermute | solution.py:103
  273.6 10.8 %collective-permute-start.31 = (bf16[256,512]{1,0:T(8,128)(2,1)S(1)}, bf16[256,512]{1,0:T(8,128)(2,1)S(1)}, u32[]{:S(2)}, u32[]{:S(2)}) collective-permute-start(bf16[256,512]{1,0:T(8,128)(2,1)S(1)} %get-tuple-element.92), channel_id=1, source_target_pairs={{0,64},{64,128},{128,192},{192,0},{1,65},{65,129},{129,193},{193,1... | collective-permute-start | bytes 786440 | tf_op jit(solution)/shard_map/ppermute | solution.py:103
  275.7 12.4 %collective-permute-start.32 = (bf16[256,512]{1,0:T(8,128)(2,1)S(1)}, bf16[256,512]{1,0:T(8,128)(2,1)S(1)}, u32[]{:S(2)}, u32[]{:S(2)}) collective-permute-start(bf16[256,512]{1,0:T(8,128)(2,1)S(1)} %get-tuple-element.93.refs_5_), channel_id=1, source_target_pairs={{0,192},{64,0},{128,64},{192,128},{1,193},{65,1},{129,65},{193,129... | collective-permute-start | bytes 786440 | tf_op jit(solution)/shard_map/ppermute | solution.py:103
  288.5 13.5 %collective-permute-start.33 = (bf16[128,512]{1,0:T(8,128)(2,1)S(1)}, bf16[128,512]{1,0:T(8,128)(2,1)S(1)}, u32[]{:S(2)}, u32[]{:S(2)}) collective-permute-start(bf16[128,512]{1,0:T(8,128)(2,1)S(1)} %get-tuple-element.95), channel_id=1, source_target_pairs={{0,16},{16,32},{32,48},{48,0},{1,17},{17,33},{33,49},{49,1},{2,18}... | collective-permute-start | bytes 393224 | tf_op jit(solution)/shard_map/ppermute | solution.py:103
  289.8 17.1 %collective-permute-start.34 = (bf16[128,512]{1,0:T(8,128)(2,1)S(1)}, bf16[128,512]{1,0:T(8,128)(2,1)S(1)}, u32[]{:S(2)}, u32[]{:S(2)}) collective-permute-start(bf16[128,512]{1,0:T(8,128)(2,1)S(1)} %get-tuple-element.96), channel_id=1, source_target_pairs={{0,32},{16,48},{32,0},{48,16},{1,33},{17,49},{33,1},{49,17},{2,34}... | collective-permute-start | bytes 393224 | tf_op jit(solution)/shard_map/ppermute | solution.py:103
  298.6 11.5 %collective-permute-start.35 = (bf16[128,512]{1,0:T(8,128)(2,1)S(1)}, bf16[128,512]{1,0:T(8,128)(2,1)S(1)}, u32[]{:S(2)}, u32[]{:S(2)}) collective-permute-start(bf16[128,512]{1,0:T(8,128)(2,1)S(1)} %get-tuple-element.97.refs_4_), channel_id=1, source_target_pairs={{0,48},{16,0},{32,16},{48,32},{1,49},{17,1},{33,17},{49,33},{2,50}... | collective-permute-start | bytes 393224 | tf_op jit(solution)/shard_map/ppermute | solution.py:103
  311.9 34.9 %all-to-all-start.3 = ((bf16[32,112,128]{2,1,0:T(8,128)(2,1)}), bf16[32,112,128]{2,1,0:T(8,128)(2,1)S(1)}, u32[]{:S(2)}, u32[]{:S(2)}) async-start(bf16[32,112,128]{2,1,0:T(8,128)(2,1)} %reorder.1.refs_2_), calls=%async_computation.3 | async-start | bytes 1835008 | tf_op jit(solution)/shard_map/all_to_all | solution.py:107
  (40 other events, 409.2 us)
Sparse Core Ops, SparseCore 0:
  12.1 77.7 all-gather.1

commit v4 on v3

--- a/solution.py
+++ b/solution.py
@@ -28,7 +28,7 @@
 span = 512
 
 expert_axes = ("y", "zh", "c")
-vmem_bytes = 32 * 1024 * 1024
+vmem_bytes = 40 * 1024 * 1024
 
 
 def dot(a, b, contract_a=1, contract_b=0):
@@ -602,6 +602,16 @@
     )
     first_spread = spread(steps(one, grad_one))
     both.second()
+    step_two = steps(two, both).reshape(experts, -1, 128)
+    height = step_two.shape[1]
+    merged = run(
+        merge_kernel,
+        "merge",
+        array(experts, 2 * height, 128),
+        [first_spread, step_two],
+        prefetch=anchor,
+    )
+    merged = exchange(merged)
     gathered = both.result()
     early = lambda g, info: (jnp.minimum(g, 3), 0)
     late = lambda g, info: (jnp.maximum(g - 4, 0), 0)
@@ -621,16 +631,6 @@
         scratch=[pltpu.VMEM((experts, capacity, 512), f32)],
     )
     other = shift(out_there, "c", 1)
-    step_two = steps(two, both).reshape(experts, -1, 128)
-    height = step_two.shape[1]
-    merged = run(
-        merge_kernel,
-        "merge",
-        array(experts, 2 * height, 128),
-        [first_spread, step_two],
-        prefetch=anchor,
-    )
-    merged = exchange(merged)
     pieces = run(
         split_kernel,
         "split",
@@ -639,13 +639,14 @@
     )
     along_y = RingSum(run, pieces, "y")
     along_y.second()
-    parts = run(cut_kernel, "cut", [array(tok_count, 512)] * 4, [along_y.third()])
+    by_rows = along_y.third()
+    second_spread = run(
+        reorder_kernel, "reorder", array(experts, height, 128), [merged], prefetch=anchor
+    )
+    second_moved = exchange(second_spread)
+    parts = run(cut_kernel, "cut", [array(tok_count, 512)] * 4, [by_rows])
     parts = [parts[0]] + [shift(parts[by], "zh", by) for by in (1, 2, 3)]
     combined = run(sum_kernel, "sum", array(tok_count, width), parts)
-    second_spread = run(
-        reorder_kernel, "reorder", array(experts, height, 128), [merged], prefetch=anchor
-    )
-    second_moved = exchange(second_spread)
     update = place(run, merged, second_moved)
     return combined, update[None]
 

time: 362 us -> 359 us (level)
  the two profiles are of different devices: /device:TPU:1 before, /device:TPU:6 now
where the time goes in v4:
time: 359 us; the launch traced here: 354 us
  waiting for transfers between devices  167 us (47%)
  starting transfers between devices  99.8 us (28%)
  Pallas kernels  50.9 us (14%)
  local copies, waits for them, and re-layouts  18.9 us (5%)
  between operations  14.8 us (4%)
    ppermute x36, waiting for transfers between devices, shift(): return lax.ppermute(value, axis, [(i, (i + by) % n) for i in range(n)])  127 us
    ppermute x36, starting transfers between devices, shift(): return lax.ppermute(value, axis, [(i, (i + by) % n) for i in range(n)])  67.1 us
    pallas_call x29, Pallas kernels, __call__(): pl.pallas_call(body, out_shape=out_shape, grid_spec=pltpu.PrefetchScalarG...  50.9 us
    all_to_all x4, waiting for transfers between devices, exchange(): lax.all_to_all(value, expert_axes, split_axis=0, concat_axis=0, tiled=True)  39.5 us
    all_to_all x4, starting transfers between devices, exchange(): lax.all_to_all(value, expert_axes, split_axis=0, concat_axis=0, tiled=True)  32.7 us
    unnamed x75, local copies, waits for them, and re-layouts  16.9 us
  transfers between devices with their start and end apart: 41, of which 25 were waited for; matrix products, arithmetic and copies ran while one was open for 1% of the time, Pallas kernels for 11%

profile of v4, /device:TPU:6, one launch (start us, length us, event | category | flops | bytes accessed | tf_op | source)
XLA Modules:
  0.0 354.2 jit_solution(13481806926064042537)
XLA Ops:
  15.4 11.5 %all-to-all-start = ((bf16[32,40,448]{2,1,0:T(8,128)(2,1)}), bf16[32,40,448]{2,1,0:T(8,128)(2,1)S(1)}, u32[]{:S(2)}, u32[]{:S(2)}) async-start(bf16[32,40,448]{2,1,0:T(8,128)(2,1)} %bitcast.19), calls=%async_computation | async-start | bytes 2621440 | tf_op jit(solution)/shard_map/all_to_all | solution.py:107
  27.1 39.5 %all-to-all-done = bf16[32,40,448]{2,1,0:T(8,128)(2,1)S(1)} async-done(((bf16[32,40,448]{2,1,0:T(8,128)(2,1)}), bf16[32,40,448]{2,1,0:T(8,128)(2,1)S(1)}, u32[]{:S(2)}, u32[]{:S(2)}) %all-to-all-start) | async-done | bytes 1146912 | tf_op jit(solution)/shard_map/all_to_all | solution.py:107
  71.8 3.5 project.5
  77.4 10.0 %collective-permute-done.refs_1_.refs_4_ = bf16[320,1024]{1,0:T(8,128)(2,1)S(1)} collective-permute-done((bf16[320,1024]{1,0:T(8,128)(2,1)S(1)}, bf16[320,1024]{1,0:T(8,128)(2,1)S(1)}, u32[]{:S(2)}, u32[]{:S(2)}) %collective-permute-start) | collective-permute-done | bytes 655392 | tf_op jit(solution)/shard_map/ppermute | solution.py:103
  108.0 3.9 %collective-permute-start.6 = (bf16[320,1024]{1,0:T(8,128)(2,1)S(1)}, bf16[320,1024]{1,0:T(8,128)(2,1)S(1)}, u32[]{:S(2)}, u32[]{:S(2)}) collective-permute-start(bf16[320,1024]{1,0:T(8,128)(2,1)S(1)} %third.5.refs_4_.refs_0_), channel_id=1, source_target_pairs={{0,4},{4,0},{1,5},{5,1},{2,6},{6,2},{3,7},{7,3},{8,12},{12,8},{9,1... | collective-permute-start | bytes 1966088 | tf_op jit(solution)/shard_map/ppermute | solution.py:103
  118.0 5.8 %collective-permute-done.10.refs_3_.refs_2_ = bf16[320,512]{1,0:T(8,128)(2,1)S(1)} collective-permute-done((bf16[320,512]{1,0:T(8,128)(2,1)S(1)}, bf16[320,512]{1,0:T(8,128)(2,1)S(1)}, u32[]{:S(2)}, u32[]{:S(2)}) %collective-permute-start.10) | collective-permute-done | bytes 327712 | tf_op jit(solution)/shard_map/ppermute | solution.py:103
  124.0 3.4 collective-permute-start.11
  132.5 3.4 collective-permute-start.14
  140.5 3.7 %collective-permute-done.15.refs_3_.refs_2_ = bf16[320,512]{1,0:T(8,128)(2,1)S(1)} collective-permute-done((bf16[320,512]{1,0:T(8,128)(2,1)S(1)}, bf16[320,512]{1,0:T(8,128)(2,1)S(1)}, u32[]{:S(2)}, u32[]{:S(2)}) %collective-permute-start.15) | collective-permute-done | bytes 327712 | tf_op jit(solution)/shard_map/ppermute | solution.py:103
  147.5 3.3 collective-permute-start.20
  154.0 10.1 %collective-permute-done.16.refs_1_ = bf16[160,512]{1,0:T(8,128)(2,1)S(1)} collective-permute-done((bf16[160,512]{1,0:T(8,128)(2,1)S(1)}, bf16[160,512]{1,0:T(8,128)(2,1)S(1)}, u32[]{:S(2)}, u32[]{:S(2)}) %collective-permute-start.16) | collective-permute-done | bytes 163872 | tf_op jit(solution)/shard_map/ppermute | solution.py:103
  164.1 4.1 %collective-permute-done.17.refs_3_ = bf16[160,512]{1,0:T(8,128)(2,1)S(1)} collective-permute-done((bf16[160,512]{1,0:T(8,128)(2,1)S(1)}, bf16[160,512]{1,0:T(8,128)(2,1)S(1)}, u32[]{:S(2)}, u32[]{:S(2)}) %collective-permute-start.17) | collective-permute-done | bytes 163872 | tf_op jit(solution)/shard_map/ppermute | solution.py:103
  170.8 4.9 %collective-permute-done.19.refs_5_ = bf16[320,512]{1,0:T(8,128)(2,1)S(1)} collective-permute-done((bf16[320,512]{1,0:T(8,128)(2,1)S(1)}, bf16[320,512]{1,0:T(8,128)(2,1)S(1)}, u32[]{:S(2)}, u32[]{:S(2)}) %collective-permute-start.19) | collective-permute-done | bytes 327712 | tf_op jit(solution)/shard_map/ppermute | solution.py:103
  176.7 12.8 %collective-permute-start.23 = (bf16[320,2048]{1,0:T(8,128)(2,1)S(1)}, bf16[320,2048]{1,0:T(8,128)(2,1)}, u32[]{:S(2)}, u32[]{:S(2)}) collective-permute-start(bf16[320,2048]{1,0:T(8,128)(2,1)S(1)} %both.1.refs_9_.refs_2_.refs_1_), channel_id=1, source_target_pairs={{0,1},{1,2},{2,3},{3,0},{4,5},{5,6},{6,7},{7,4},{8,9},{9,10},{10,1... | collective-permute-start | bytes 3932168 | tf_op jit(solution)/shard_map/ppermute | solution.py:103
  189.5 5.1 %adam.2.refs_2_ = bf16[8,448,128]{2,1,0:T(8,128)(2,1)} custom-call(s32[41]{0:T(128)S(1)} %copy-done.27, bf16[8,160,448]{2,1,0:T(8,128)(2,1)S(1)} %bitcast.51, bf16[320,1024]{1,0:T(8,128)(2,1)S(1)} %slope.1.refs_6_.refs_2_, bf16[320,1024]{1,0:T(8,128)(2,1)S(1)} %collective-permute-done.21.refs_1_.refs_3_, ...), custom_call_target="tpu_custom_call" | custom-call | flops 1174405120 | bytes 8000000 | tf_op jit(solution)/shard_map/adam/pallas_call | solution.py:80
  194.6 5.7 %all-to-all-start.1 = ((bf16[32,112,128]{2,1,0:T(8,128)(2,1)}), bf16[32,112,128]{2,1,0:T(8,128)(2,1)}, u32[]{:S(2)}, u32[]{:S(2)}) async-start(bf16[32,112,128]{2,1,0:T(8,128)(2,1)} %bitcast.28), calls=%async_computation.1 | async-start | bytes 1835008 | tf_op jit(solution)/shard_map/all_to_all | solution.py:107
  200.3 6.4 %collective-permute-done.23.refs_0_.refs_6_.refs_5_ = bf16[320,2048]{1,0:T(8,128)(2,1)} collective-permute-done((bf16[320,2048]{1,0:T(8,128)(2,1)S(1)}, bf16[320,2048]{1,0:T(8,128)(2,1)}, u32[]{:S(2)}, u32[]{:S(2)}) %collective-permute-start.23) | collective-permute-done | bytes 1310752 | tf_op jit(solution)/shard_map/ppermute | solution.py:103
  208.1 3.9 %collective-permute-start.26 = (bf16[160,2048]{1,0:T(8,128)(2,1)S(1)}, bf16[160,2048]{1,0:T(8,128)(2,1)S(1)}, u32[]{:S(2)}, u32[]{:S(2)}) collective-permute-start(bf16[160,2048]{1,0:T(8,128)(2,1)S(1)} %get-tuple-element.82), channel_id=1, source_target_pairs={{0,1},{1,2},{2,3},{3,0},{4,5},{5,6},{6,7},{7,4},{8,9},{9,10},{10,1... | collective-permute-start | bytes 1966088 | tf_op jit(solution)/shard_map/ppermute | solution.py:103
  212.7 7.4 %collective-permute-done.26.refs_4_.refs_3_ = bf16[160,2048]{1,0:T(8,128)(2,1)S(1)} collective-permute-done((bf16[160,2048]{1,0:T(8,128)(2,1)S(1)}, bf16[160,2048]{1,0:T(8,128)(2,1)S(1)}, u32[]{:S(2)}, u32[]{:S(2)}) %collective-permute-start.26) | collective-permute-done | bytes 655392 | tf_op jit(solution)/shard_map/ppermute | solution.py:103
  220.1 3.7 %collective-permute-done.27.refs_5_.refs_4_ = bf16[160,2048]{1,0:T(8,128)(2,1)S(1)} collective-permute-done((bf16[160,2048]{1,0:T(8,128)(2,1)S(1)}, bf16[160,2048]{1,0:T(8,128)(2,1)S(1)}, u32[]{:S(2)}, u32[]{:S(2)}) %collective-permute-start.27) | collective-permute-done | bytes 655392 | tf_op jit(solution)/shard_map/ppermute | solution.py:103
  225.8 5.4 %adam.3.refs_3_ = bf16[8,448,128]{2,1,0:T(8,128)(2,1)S(1)} custom-call(s32[41]{0:T(128)S(1)} %copy-done.28, bf16[8,160,448]{2,1,0:T(8,128)(2,1)S(1)} %bitcast.52, bf16[320,2048]{1,0:T(8,128)(2,1)S(1)} %both.1.refs_9_.refs_2_.refs_1_, bf16[320,2048]{1,0:T(8,128)(2,1)} %collective-permute-done.22.refs_1_.refs_3_.refs_2_, ...), custom_call_target="tpu_custom_call" | custom-call | flops 1174405120 | bytes 8000000 | tf_op jit(solution)/shard_map/adam/pallas_call | solution.py:80
  236.9 6.1 %all-to-all-start.2 = ((bf16[32,224,128]{2,1,0:T(8,128)(2,1)}), bf16[32,224,128]{2,1,0:T(8,128)(2,1)}, u32[]{:S(2)}, u32[]{:S(2)}) async-start(bf16[32,224,128]{2,1,0:T(8,128)(2,1)} %copy-done), calls=%async_computation.2 | async-start | bytes 3670016 | tf_op jit(solution)/shard_map/all_to_all | solution.py:107
  248.0 6.5 %outputs.1 = (bf16[2048,512]{1,0:T(8,128)(2,1)S(1)}, bf16[2048,512]{1,0:T(8,128)(2,1)S(1)}) custom-call(s32[41]{0:T(128)S(1)} %copy-done.29, bf16[320,2048]{1,0:T(8,128)(2,1)S(1)} %both.1.refs_9_.refs_2_.refs_1_, bf16[320,2048]{1,0:T(8,128)(2,1)} %collective-permute-done.22.refs_1_.refs_3_.refs_2_, bf16[160,2048]{1,0:T(8,128)(2,1)S(1)} %copy-done.9, ...), custom_call_target="tpu_custom_call" | custom-call | flops 1174405120 | bytes 5000000 | tf_op jit(solution)/shard_map/outputs/pallas_call | solution.py:80
  254.8 3.9 %collective-permute-done.28.refs_1_ = bf16[2048,512]{1,0:T(8,128)(2,1)S(1)} collective-permute-done((bf16[2048,512]{1,0:T(8,128)(2,1)S(1)}, bf16[2048,512]{1,0:T(8,128)(2,1)S(1)}, u32[]{:S(2)}, u32[]{:S(2)}) %collective-permute-start.28) | collective-permute-done | bytes 2097184 | tf_op jit(solution)/shard_map/ppermute | solution.py:103
  262.5 19.1 %collective-permute-done.29.refs_1_.refs_4_ = bf16[512,512]{1,0:T(8,128)(2,1)S(1)} collective-permute-done((bf16[512,512]{1,0:T(8,128)(2,1)S(1)}, bf16[512,512]{1,0:T(8,128)(2,1)S(1)}, u32[]{:S(2)}, u32[]{:S(2)}) %collective-permute-start.29) | collective-permute-done | bytes 524320 | tf_op jit(solution)/shard_map/ppermute | solution.py:103
  286.3 5.4 %collective-permute-done.31.refs_1_ = bf16[256,512]{1,0:T(8,128)(2,1)S(1)} collective-permute-done((bf16[256,512]{1,0:T(8,128)(2,1)S(1)}, bf16[256,512]{1,0:T(8,128)(2,1)S(1)}, u32[]{:S(2)}, u32[]{:S(2)}) %collective-permute-start.31) | collective-permute-done | bytes 262176 | tf_op jit(solution)/shard_map/ppermute | solution.py:103
  295.4 9.4 %all-to-all-start.3 = ((bf16[32,112,128]{2,1,0:T(8,128)(2,1)}), bf16[32,112,128]{2,1,0:T(8,128)(2,1)S(1)}, u32[]{:S(2)}, u32[]{:S(2)}) async-start(bf16[32,112,128]{2,1,0:T(8,128)(2,1)} %reorder.1.refs_1_), calls=%async_computation.3 | async-start | bytes 1835008 | tf_op jit(solution)/shard_map/all_to_all | solution.py:107
  307.6 3.6 %collective-permute-start.34 = (bf16[128,512]{1,0:T(8,128)(2,1)S(1)}, bf16[128,512]{1,0:T(8,128)(2,1)S(1)}, u32[]{:S(2)}, u32[]{:S(2)}) collective-permute-start(bf16[128,512]{1,0:T(8,128)(2,1)S(1)} %get-tuple-element.96), channel_id=1, source_target_pairs={{0,32},{16,48},{32,0},{48,16},{1,33},{17,49},{33,1},{49,17},{2,34}... | collective-permute-start | bytes 393224 | tf_op jit(solution)/shard_map/ppermute | solution.py:103
  311.2 3.6 %collective-permute-start.35 = (bf16[128,512]{1,0:T(8,128)(2,1)S(1)}, bf16[128,512]{1,0:T(8,128)(2,1)S(1)}, u32[]{:S(2)}, u32[]{:S(2)}) collective-permute-start(bf16[128,512]{1,0:T(8,128)(2,1)S(1)} %get-tuple-element.97.refs_4_), channel_id=1, source_target_pairs={{0,48},{16,0},{32,16},{48,32},{1,49},{17,1},{33,17},{49,33},{2,50}... | collective-permute-start | bytes 393224 | tf_op jit(solution)/shard_map/ppermute | solution.py:103
  314.7 13.4 %collective-permute-done.33.refs_1_ = bf16[128,512]{1,0:T(8,128)(2,1)S(1)} collective-permute-done((bf16[128,512]{1,0:T(8,128)(2,1)S(1)}, bf16[128,512]{1,0:T(8,128)(2,1)S(1)}, u32[]{:S(2)}, u32[]{:S(2)}) %collective-permute-start.33) | collective-permute-done | bytes 131104 | tf_op jit(solution)/shard_map/ppermute | solution.py:103
  328.2 14.4 %collective-permute-done.34.refs_2_ = bf16[128,512]{1,0:T(8,128)(2,1)S(1)} collective-permute-done((bf16[128,512]{1,0:T(8,128)(2,1)S(1)}, bf16[128,512]{1,0:T(8,128)(2,1)S(1)}, u32[]{:S(2)}, u32[]{:S(2)}) %collective-permute-start.34) | collective-permute-done | bytes 131104 | tf_op jit(solution)/shard_map/ppermute | solution.py:103
  343.4 3.8 %place.1 = bf16[448,2048]{1,0:T(8,128)(2,1)} custom-call(bf16[32,224,128]{2,1,0:T(8,128)(2,1)} %all-to-all-done.2.refs_1_.refs_0_, bf16[32,112,128]{2,1,0:T(8,128)(2,1)S(1)} %all-to-all-done.3.refs_1_, bf16[128,448]{1,0:T(8,128)(2,1)S(1)} %sum.1.refs_2_), custom_call_target="tpu_custom_call" | custom-call | bytes 1000000 | tf_op jit(solution)/shard_map/place/pallas_call | solution.py:80
  (166 shorter events, 92.9 us)
Async XLA Ops:
  7.2 85.7 %all-gather.2.cloned.1.call-start = ((), (), s32[]{:S(2)}) async-start(), calls=%async_computation.4 | async-start | bytes 4325376 | tf_op jit(solution)/shard_map/all_gather | solution.py:513
  15.4 51.1 %all-to-all-start = ((bf16[32,40,448]{2,1,0:T(8,128)(2,1)}), bf16[32,40,448]{2,1,0:T(8,128)(2,1)S(1)}, u32[]{:S(2)}, u32[]{:S(2)}) async-start(bf16[32,40,448]{2,1,0:T(8,128)(2,1)} %bitcast.19), calls=%async_computation | async-start | bytes 2621440 | tf_op jit(solution)/shard_map/all_to_all | solution.py:107
  69.7 17.8 %collective-permute-start = (bf16[320,1024]{1,0:T(8,128)(2,1)S(1)}, bf16[320,1024]{1,0:T(8,128)(2,1)S(1)}, u32[]{:S(2)}, u32[]{:S(2)}) collective-permute-start(bf16[320,1024]{1,0:T(8,128)(2,1)S(1)} %get-tuple-element.52), channel_id=1, source_target_pairs={{0,1},{1,2},{2,3},{3,0},{4,5},{5,6},{6,7},{7,4},{8,9},{9,10},{10,1... | collective-permute-start | bytes 1966088 | tf_op jit(solution)/shard_map/ppermute | solution.py:103
  70.0 18.9 %collective-permute-start.1 = (bf16[320,1024]{1,0:T(8,128)(2,1)S(1)}, bf16[320,1024]{1,0:T(8,128)(2,1)S(1)}, u32[]{:S(2)}, u32[]{:S(2)}) collective-permute-start(bf16[320,1024]{1,0:T(8,128)(2,1)S(1)} %get-tuple-element.54), channel_id=1, source_target_pairs={{0,3},{1,0},{2,1},{3,2},{4,7},{5,4},{6,5},{7,6},{8,11},{9,8},{10,9... | collective-permute-start | bytes 1966088 | tf_op jit(solution)/shard_map/ppermute | solution.py:103
  75.3 25.5 %collective-permute-start.4 = (bf16[320,1024]{1,0:T(8,128)(2,1)}, bf16[320,1024]{1,0:T(8,128)(2,1)S(1)}, u32[]{:S(2)}, u32[]{:S(2)}) collective-permute-start(bf16[320,1024]{1,0:T(8,128)(2,1)} %get-tuple-element.59), channel_id=1, source_target_pairs={{0,1},{1,2},{2,3},{3,0},{4,5},{5,6},{6,7},{7,4},{8,9},{9,10},{10,1... | collective-permute-start | bytes 1966088 | tf_op jit(solution)/shard_map/ppermute | solution.py:103
  76.9 25.2 %collective-permute-start.5 = (bf16[320,1024]{1,0:T(8,128)(2,1)}, bf16[320,1024]{1,0:T(8,128)(2,1)S(1)}, u32[]{:S(2)}, u32[]{:S(2)}) collective-permute-start(bf16[320,1024]{1,0:T(8,128)(2,1)} %get-tuple-element.60), channel_id=1, source_target_pairs={{0,3},{1,0},{2,1},{3,2},{4,7},{5,4},{6,5},{7,6},{8,11},{9,8},{10,9... | collective-permute-start | bytes 1966088 | tf_op jit(solution)/shard_map/ppermute | solution.py:103
  90.7 13.7 %collective-permute-start.2 = (bf16[160,1024]{1,0:T(8,128)(2,1)}, bf16[160,1024]{1,0:T(8,128)(2,1)}, u32[]{:S(2)}, u32[]{:S(2)}) collective-permute-start(bf16[160,1024]{1,0:T(8,128)(2,1)} %get-tuple-element.56), channel_id=1, source_target_pairs={{0,1},{1,2},{2,3},{3,0},{4,5},{5,6},{6,7},{7,4},{8,9},{9,10},{10,1... | collective-permute-start | bytes 983048 | tf_op jit(solution)/shard_map/ppermute | solution.py:103
  90.9 14.8 %collective-permute-start.3 = (bf16[160,1024]{1,0:T(8,128)(2,1)}, bf16[160,1024]{1,0:T(8,128)(2,1)}, u32[]{:S(2)}, u32[]{:S(2)}) collective-permute-start(bf16[160,1024]{1,0:T(8,128)(2,1)} %get-tuple-element.57.refs_2_), channel_id=1, source_target_pairs={{0,3},{1,0},{2,1},{3,2},{4,7},{5,4},{6,5},{7,6},{8,11},{9,8},{10,9... | collective-permute-start | bytes 983048 | tf_op jit(solution)/shard_map/ppermute | solution.py:103
  108.0 27.9 %collective-permute-start.6 = (bf16[320,1024]{1,0:T(8,128)(2,1)S(1)}, bf16[320,1024]{1,0:T(8,128)(2,1)S(1)}, u32[]{:S(2)}, u32[]{:S(2)}) collective-permute-start(bf16[320,1024]{1,0:T(8,128)(2,1)S(1)} %third.5.refs_4_.refs_0_), channel_id=1, source_target_pairs={{0,4},{4,0},{1,5},{5,1},{2,6},{6,2},{3,7},{7,3},{8,12},{12,8},{9,1... | collective-permute-start | bytes 1966088 | tf_op jit(solution)/shard_map/ppermute | solution.py:103
  111.9 11.8 %collective-permute-start.10 = (bf16[320,512]{1,0:T(8,128)(2,1)S(1)}, bf16[320,512]{1,0:T(8,128)(2,1)S(1)}, u32[]{:S(2)}, u32[]{:S(2)}) collective-permute-start(bf16[320,512]{1,0:T(8,128)(2,1)S(1)} %get-tuple-element.70), channel_id=1, source_target_pairs={{0,3},{1,0},{2,1},{3,2},{4,7},{5,4},{6,5},{7,6},{8,11},{9,8},{10,9... | collective-permute-start | bytes 983048 | tf_op jit(solution)/shard_map/ppermute | solution.py:103
  111.9 11.8 %collective-permute-start.9 = (bf16[320,512]{1,0:T(8,128)(2,1)S(1)}, bf16[320,512]{1,0:T(8,128)(2,1)S(1)}, u32[]{:S(2)}, u32[]{:S(2)}) collective-permute-start(bf16[320,512]{1,0:T(8,128)(2,1)S(1)} %get-tuple-element.68), channel_id=1, source_target_pairs={{0,1},{1,2},{2,3},{3,0},{4,5},{5,6},{6,7},{7,4},{8,9},{9,10},{10,1... | collective-permute-start | bytes 983048 | tf_op jit(solution)/shard_map/ppermute | solution.py:103
  115.6 14.7 %collective-permute-start.7 = (bf16[160,1024]{1,0:T(8,128)(2,1)S(1)}, bf16[160,1024]{1,0:T(8,128)(2,1)S(1)}, u32[]{:S(2)}, u32[]{:S(2)}) collective-permute-start(bf16[160,1024]{1,0:T(8,128)(2,1)S(1)} %get-tuple-element.65), channel_id=1, source_target_pairs={{0,1},{1,2},{2,3},{3,0},{4,5},{5,6},{6,7},{7,4},{8,9},{9,10},{10,1... | collective-permute-start | bytes 983048 | tf_op jit(solution)/shard_map/ppermute | solution.py:103
  115.7 15.0 %collective-permute-start.8 = (bf16[160,1024]{1,0:T(8,128)(2,1)S(1)}, bf16[160,1024]{1,0:T(8,128)(2,1)S(1)}, u32[]{:S(2)}, u32[]{:S(2)}) collective-permute-start(bf16[160,1024]{1,0:T(8,128)(2,1)S(1)} %get-tuple-element.66.refs_4_), channel_id=1, source_target_pairs={{0,3},{1,0},{2,1},{3,2},{4,7},{5,4},{6,5},{7,6},{8,11},{9,8},{10,9... | collective-permute-start | bytes 983048 | tf_op jit(solution)/shard_map/ppermute | solution.py:103
  124.0 11.9 %collective-permute-start.11 = (bf16[160,512]{1,0:T(8,128)(2,1)S(1)}, bf16[160,512]{1,0:T(8,128)(2,1)S(1)}, u32[]{:S(2)}, u32[]{:S(2)}) collective-permute-start(bf16[160,512]{1,0:T(8,128)(2,1)S(1)} %get-tuple-element.71), channel_id=1, source_target_pairs={{0,1},{1,2},{2,3},{3,0},{4,5},{5,6},{6,7},{7,4},{8,9},{9,10},{10,1... | collective-permute-start | bytes 491528 | tf_op jit(solution)/shard_map/ppermute | solution.py:103
  137.0 31.2 %collective-permute-start.13 = (bf16[320,1024]{1,0:T(8,128)(2,1)S(1)}, bf16[320,1024]{1,0:T(8,128)(2,1)S(1)}, u32[]{:S(2)}, u32[]{:S(2)}) collective-permute-start(bf16[320,1024]{1,0:T(8,128)(2,1)S(1)} %third.7.refs_4_.refs_2_), channel_id=1, source_target_pairs={{0,4},{4,0},{1,5},{5,1},{2,6},{6,2},{3,7},{7,3},{8,12},{12,8},{9,1... | collective-permute-start | bytes 1966088 | tf_op jit(solution)/shard_map/ppermute | solution.py:103
  147.5 21.1 %collective-permute-start.20 = (bf16[320,1024]{1,0:T(8,128)(2,1)S(1)}, bf16[320,1024]{1,0:T(8,128)(2,1)S(1)}, u32[]{:S(2)}, u32[]{:S(2)}) collective-permute-start(bf16[320,1024]{1,0:T(8,128)(2,1)S(1)} %slope.1.refs_6_.refs_2_), channel_id=1, source_target_pairs={{0,1},{1,2},{2,3},{3,0},{4,5},{5,6},{6,7},{7,4},{8,9},{9,10},{10,1... | collective-permute-start | bytes 1966088 | tf_op jit(solution)/shard_map/ppermute | solution.py:103
  150.8 17.8 %collective-permute-start.21 = (bf16[320,1024]{1,0:T(8,128)(2,1)S(1)}, bf16[320,1024]{1,0:T(8,128)(2,1)S(1)}, u32[]{:S(2)}, u32[]{:S(2)}) collective-permute-start(bf16[320,1024]{1,0:T(8,128)(2,1)S(1)} %slope.1.refs_6_.refs_2_), channel_id=1, source_target_pairs={{0,3},{1,0},{2,1},{3,2},{4,7},{5,4},{6,5},{7,6},{8,11},{9,8},{10,9... | collective-permute-start | bytes 1966088 | tf_op jit(solution)/shard_map/ppermute | solution.py:103
  150.8 13.4 %collective-permute-start.16 = (bf16[160,512]{1,0:T(8,128)(2,1)S(1)}, bf16[160,512]{1,0:T(8,128)(2,1)S(1)}, u32[]{:S(2)}, u32[]{:S(2)}) collective-permute-start(bf16[160,512]{1,0:T(8,128)(2,1)S(1)} %get-tuple-element.78), channel_id=1, source_target_pairs={{0,1},{1,2},{2,3},{3,0},{4,5},{5,6},{6,7},{7,4},{8,9},{9,10},{10,1... | collective-permute-start | bytes 491528 | tf_op jit(solution)/shard_map/ppermute | solution.py:103
  154.0 14.2 %collective-permute-start.17 = (bf16[160,512]{1,0:T(8,128)(2,1)S(1)}, bf16[160,512]{1,0:T(8,128)(2,1)S(1)}, u32[]{:S(2)}, u32[]{:S(2)}) collective-permute-start(bf16[160,512]{1,0:T(8,128)(2,1)S(1)} %get-tuple-element.79.refs_4_), channel_id=1, source_target_pairs={{0,3},{1,0},{2,1},{3,2},{4,7},{5,4},{6,5},{7,6},{8,11},{9,8},{10,9... | collective-permute-start | bytes 491528 | tf_op jit(solution)/shard_map/ppermute | solution.py:103
  168.7 20.8 %collective-permute-start.24 = (bf16[160,1024]{1,0:T(8,128)(2,1)S(1)}, bf16[160,1024]{1,0:T(8,128)(2,1)S(1)}, u32[]{:S(2)}, u32[]{:S(2)}) collective-permute-start(bf16[160,1024]{1,0:T(8,128)(2,1)S(1)} %get-tuple-element.81), channel_id=1, source_target_pairs={{0,1},{1,2},{2,3},{3,0},{4,5},{5,6},{6,7},{7,4},{8,9},{9,10},{10,1... | collective-permute-start | bytes 983048 | tf_op jit(solution)/shard_map/ppermute | solution.py:103
  168.9 20.6 %collective-permute-start.25 = (bf16[160,1024]{1,0:T(8,128)(2,1)S(1)}, bf16[160,1024]{1,0:T(8,128)(2,1)S(1)}, u32[]{:S(2)}, u32[]{:S(2)}) collective-permute-start(bf16[160,1024]{1,0:T(8,128)(2,1)S(1)} %get-tuple-element.80.refs_6_), channel_id=1, source_target_pairs={{0,3},{1,0},{2,1},{3,2},{4,7},{5,4},{6,5},{7,6},{8,11},{9,8},{10,9... | collective-permute-start | bytes 983048 | tf_op jit(solution)/shard_map/ppermute | solution.py:103
  176.6 23.7 %collective-permute-start.22 = (bf16[320,2048]{1,0:T(8,128)(2,1)S(1)}, bf16[320,2048]{1,0:T(8,128)(2,1)}, u32[]{:S(2)}, u32[]{:S(2)}) collective-permute-start(bf16[320,2048]{1,0:T(8,128)(2,1)S(1)} %both.1.refs_9_.refs_2_.refs_1_), channel_id=1, source_target_pairs={{0,3},{1,0},{2,1},{3,2},{4,7},{5,4},{6,5},{7,6},{8,11},{9,8},{10,9... | collective-permute-start | bytes 3932168 | tf_op jit(solution)/shard_map/ppermute | solution.py:103
  176.7 30.0 %collective-permute-start.23 = (bf16[320,2048]{1,0:T(8,128)(2,1)S(1)}, bf16[320,2048]{1,0:T(8,128)(2,1)}, u32[]{:S(2)}, u32[]{:S(2)}) collective-permute-start(bf16[320,2048]{1,0:T(8,128)(2,1)S(1)} %both.1.refs_9_.refs_2_.refs_1_), channel_id=1, source_target_pairs={{0,1},{1,2},{2,3},{3,0},{4,5},{5,6},{6,7},{7,4},{8,9},{9,10},{10,1... | collective-permute-start | bytes 3932168 | tf_op jit(solution)/shard_map/ppermute | solution.py:103
  194.6 38.4 %all-to-all-start.1 = ((bf16[32,112,128]{2,1,0:T(8,128)(2,1)}), bf16[32,112,128]{2,1,0:T(8,128)(2,1)}, u32[]{:S(2)}, u32[]{:S(2)}) async-start(bf16[32,112,128]{2,1,0:T(8,128)(2,1)} %bitcast.28), calls=%async_computation.1 | async-start | bytes 1835008 | tf_op jit(solution)/shard_map/all_to_all | solution.py:107
  208.1 12.0 %collective-permute-start.26 = (bf16[160,2048]{1,0:T(8,128)(2,1)S(1)}, bf16[160,2048]{1,0:T(8,128)(2,1)S(1)}, u32[]{:S(2)}, u32[]{:S(2)}) collective-permute-start(bf16[160,2048]{1,0:T(8,128)(2,1)S(1)} %get-tuple-element.82), channel_id=1, source_target_pairs={{0,1},{1,2},{2,3},{3,0},{4,5},{5,6},{6,7},{7,4},{8,9},{9,10},{10,1... | collective-permute-start | bytes 1966088 | tf_op jit(solution)/shard_map/ppermute | solution.py:103
  236.9 55.3 %all-to-all-start.2 = ((bf16[32,224,128]{2,1,0:T(8,128)(2,1)}), bf16[32,224,128]{2,1,0:T(8,128)(2,1)}, u32[]{:S(2)}, u32[]{:S(2)}) async-start(bf16[32,224,128]{2,1,0:T(8,128)(2,1)} %copy-done), calls=%async_computation.2 | async-start | bytes 3670016 | tf_op jit(solution)/shard_map/all_to_all | solution.py:107
  259.2 22.4 %collective-permute-start.29 = (bf16[512,512]{1,0:T(8,128)(2,1)S(1)}, bf16[512,512]{1,0:T(8,128)(2,1)S(1)}, u32[]{:S(2)}, u32[]{:S(2)}) collective-permute-start(bf16[512,512]{1,0:T(8,128)(2,1)S(1)} %get-tuple-element.89), channel_id=1, source_target_pairs={{0,64},{64,128},{128,192},{192,0},{1,65},{65,129},{129,193},{193,1... | collective-permute-start | bytes 1572872 | tf_op jit(solution)/shard_map/ppermute | solution.py:103
  261.0 21.7 %collective-permute-start.30 = (bf16[512,512]{1,0:T(8,128)(2,1)S(1)}, bf16[512,512]{1,0:T(8,128)(2,1)S(1)}, u32[]{:S(2)}, u32[]{:S(2)}) collective-permute-start(bf16[512,512]{1,0:T(8,128)(2,1)S(1)} %get-tuple-element.91), channel_id=1, source_target_pairs={{0,192},{64,0},{128,64},{192,128},{1,193},{65,1},{129,65},{193,129... | collective-permute-start | bytes 1572872 | tf_op jit(solution)/shard_map/ppermute | solution.py:103
  295.4 48.0 %all-to-all-start.3 = ((bf16[32,112,128]{2,1,0:T(8,128)(2,1)}), bf16[32,112,128]{2,1,0:T(8,128)(2,1)S(1)}, u32[]{:S(2)}, u32[]{:S(2)}) async-start(bf16[32,112,128]{2,1,0:T(8,128)(2,1)} %reorder.1.refs_1_), calls=%async_computation.3 | async-start | bytes 1835008 | tf_op jit(solution)/shard_map/all_to_all | solution.py:107
  304.8 23.3 %collective-permute-start.33 = (bf16[128,512]{1,0:T(8,128)(2,1)S(1)}, bf16[128,512]{1,0:T(8,128)(2,1)S(1)}, u32[]{:S(2)}, u32[]{:S(2)}) collective-permute-start(bf16[128,512]{1,0:T(8,128)(2,1)S(1)} %get-tuple-element.95), channel_id=1, source_target_pairs={{0,16},{16,32},{32,48},{48,0},{1,17},{17,33},{33,49},{49,1},{2,18}... | collective-permute-start | bytes 393224 | tf_op jit(solution)/shard_map/ppermute | solution.py:103
  307.6 34.9 %collective-permute-start.34 = (bf16[128,512]{1,0:T(8,128)(2,1)S(1)}, bf16[128,512]{1,0:T(8,128)(2,1)S(1)}, u32[]{:S(2)}, u32[]{:S(2)}) collective-permute-start(bf16[128,512]{1,0:T(8,128)(2,1)S(1)} %get-tuple-element.96), channel_id=1, source_target_pairs={{0,32},{16,48},{32,0},{48,16},{1,33},{17,49},{33,1},{49,17},{2,34}... | collective-permute-start | bytes 393224 | tf_op jit(solution)/shard_map/ppermute | solution.py:103
  311.2 31.4 %collective-permute-start.35 = (bf16[128,512]{1,0:T(8,128)(2,1)S(1)}, bf16[128,512]{1,0:T(8,128)(2,1)S(1)}, u32[]{:S(2)}, u32[]{:S(2)}) collective-permute-start(bf16[128,512]{1,0:T(8,128)(2,1)S(1)} %get-tuple-element.97.refs_4_), channel_id=1, source_target_pairs={{0,48},{16,0},{32,16},{48,32},{1,49},{17,1},{33,17},{49,33},{2,50}... | collective-permute-start | bytes 393224 | tf_op jit(solution)/shard_map/ppermute | solution.py:103
  (45 other events, 413.4 us)
Sparse Core Ops, SparseCore 0:
  12.1 76.2 all-gather.1
